TPU v7x, 32 devices: a whole 2x2x4 slice. The times are simulated.
32 devices in a mesh: groups: 2 (over y), row: 4 (over x, core), col: 4 (over z).
Axes of the slice: x: 2, y: 2, z: 4, core: 2. Of those that a mesh axis runs over, the one named last changes fastest.
Arguments:
- queries: bfloat16 [2048, 384], P(('groups', 'row', 'col')), parts along dimension 0, may hold values from -90 to 90
- keys: bfloat16 [2048, 384], P(('groups', 'col', 'row')), parts along dimension 0, may hold values from -15 to 15
- values: bfloat16 [2048, 384], P(('groups', 'col', 'row')), parts along dimension 0, may hold values from -6 to 6
- block_mask: int32 [16, 8], P(('groups', 'row'), 'col'), parts along dimension 0, may hold values from 0 to 1, as said below
- out_weight: bfloat16 [384, 2560], P(None, ('row', 'col')), may hold values from -0.3125 to 0.3125
- residual: bfloat16 [2048, 2560], P(('groups', 'row', 'col')), parts along dimension 0, may hold values from -1.5 to 1.5
Outputs:
- block_out: bfloat16 [2048, 2560], P(('groups', 'row', 'col')), parts along dimension 0
There are 2 independent parts, one for each index of `groups`. A program takes and returns all parts, laid end to end along the dimension named above; an argument that names none is the same for every part. Nothing has to cross between parts.
Inputs may be any that keep to these rules, and one draw needn't show every extreme that they name: Entries are 0 or 1; block_mask[b, b] = 1 for every b. Each query block keeps between 1 and 2 key blocks in each key tile of 2 blocks, and in every pair of a query tile of 2 blocks and a key tile some query block keeps exactly 2.
All inputs are finite; a program needn't handle non-finite values.
Results may differ from a plain program's by a relative error of at most 0.0035.
Values may be sent and summed in bfloat16 or wider, within the bound.
No kernel may reach another device: no remote copies, remote signals or barrier semaphores. Data moves between devices by JAX's collectives and lax.ppermute only.
A program may use at most 64 MiB of HBM per device.

v0:
```python
import math

import jax
import jax.numpy as jnp
from jax import lax
from jax.sharding import PartitionSpec as P

HD = 128
HEADS = 3
BLK = 128


def local(queries, keys, values, block_mask, out_weight, residual):
    score_scale = 1.0 / math.sqrt(HD)
    query_tile = lax.all_gather(queries, "col", axis=0, tiled=True)
    key_tile, value_tile = (
        lax.all_gather(keys, "row", axis=0, tiled=True),
        lax.all_gather(values, "row", axis=0, tiled=True),
    )
    query_count = block_mask.shape[0]
    key_count = block_mask.shape[1]
    keep_most = max(2, 7 * key_count // 16)
    if query_count % 4 == 0:
        group_size = 4
    elif query_count % 2 == 0:
        group_size = 2
    else:
        group_size = 1
    key_blocks = key_tile.reshape(key_count, BLK, HEADS, HD)
    value_blocks = value_tile.reshape(key_count, BLK, HEADS, HD)
    within = jnp.arange(key_count, dtype=jnp.int32)
    priority = block_mask * (2 * key_count) + (key_count - within)[None, :]
    top_values, chosen = lax.top_k(priority, keep_most)
    usable = jnp.take_along_axis(block_mask, chosen, axis=1) > 0
    steps_count = query_count // group_size
    query_groups = query_tile.reshape(steps_count, group_size, BLK, HEADS, HD)
    chosen_groups = chosen.reshape(steps_count, group_size, keep_most)
    usable_groups = usable.reshape(steps_count, group_size, keep_most)

    def one_step(operands):
        query_rows, picked, allowed = operands
        near_keys = key_blocks[picked]
        near_values = value_blocks[picked]
        scores = (
            jnp.einsum(
                "gqhd,gkbhd->gqhkb", query_rows, near_keys, preferred_element_type=jnp.float32
            )
            * score_scale
        )
        scores = jnp.where(allowed[:, None, None, :, None], scores, -jnp.inf)
        tile_max = jnp.max(scores, axis=(3, 4))
        weights = jnp.exp(scores - tile_max[:, :, :, None, None])
        tile_total = jnp.sum(weights, axis=(3, 4))
        rounded = weights.astype(jnp.bfloat16)
        tile_sum = jnp.einsum(
            "gqhkb,gkbhd->gqhd", rounded, near_values, preferred_element_type=jnp.float32
        )
        return (tile_sum, tile_max, tile_total)

    tile_sum, tile_max, tile_total = lax.map(one_step, (query_groups, chosen_groups, usable_groups))
    query_rows_all = query_count * BLK
    tile_sum = tile_sum.reshape(query_rows_all, HEADS, HD)
    tile_max = tile_max.reshape(query_rows_all, HEADS)
    tile_total = tile_total.reshape(query_rows_all, HEADS)
    col_count = lax.axis_size("col")
    own_rows = query_rows_all // col_count
    moved_sum, moved_max, moved_total = (
        lax.all_to_all(
            tile_sum.reshape(col_count, own_rows, HEADS * HD),
            "col",
            split_axis=0,
            concat_axis=0,
            tiled=True,
        ),
        lax.all_to_all(
            tile_max.reshape(col_count, own_rows, HEADS),
            "col",
            split_axis=0,
            concat_axis=0,
            tiled=True,
        ),
        lax.all_to_all(
            tile_total.reshape(col_count, own_rows, HEADS),
            "col",
            split_axis=0,
            concat_axis=0,
            tiled=True,
        ),
    )
    row_max = jnp.max(moved_max, axis=0)
    factor = jnp.exp(moved_max - row_max[None, :, :])
    numer = jnp.sum(
        moved_sum.reshape(col_count, own_rows, HEADS, HD) * factor[:, :, :, None], axis=0
    )
    denom = jnp.sum(moved_total * factor, axis=0)
    attended = (numer / denom[:, :, None]).reshape(own_rows, HEADS * HD).astype(jnp.bfloat16)
    projected = jnp.dot(
        attended,
        lax.all_gather(out_weight, ("row", "col"), axis=1, tiled=True),
        preferred_element_type=jnp.float32,
    )
    return (projected + residual.astype(jnp.float32)).astype(jnp.bfloat16)


def solution(mesh):
    placed = (
        P(("groups", "row", "col"), None),
        P(("groups", "col", "row"), None),
        P(("groups", "col", "row"), None),
        P(("groups", "row"), "col"),
        P(None, ("row", "col")),
        P(("groups", "row", "col"), None),
    )
    return jax.shard_map(
        local,
        mesh=mesh,
        in_specs=placed,
        out_specs=P(("groups", "row", "col"), None),
        check_vma=False,
    )
```

profile of v0, /device:TPU:0, one launch (start us, length us, event | category | flops | bytes accessed | tf_op | source)
XLA Modules:
  0.0 82.4 jit_solution(12935174878868163091)
XLA Ops:
  6.5 0.7 all-gather.2.cloned.1.call-update
  7.3 0.8 copy.63
  8.1 0.6 top_k.10
  8.9 7.0 %all_gather.13 = bf16[256,384]{1,0:T(8,128)(2,1)S(1)} all-gather(bf16[64,384]{1,0:T(8,128)(2,1)} %param.7), channel_id=1, replica_groups=mesh['groups'=2,'row'=4,'col'=4] {'row'}, dimensions={0}, use_global_device_ids=true | all-gather | bytes 245760 | tf_op jit(solution)/shard_map/all_gather | solution.py:17
  16.2 0.6 gather_fusion.2
  17.2 14.6 %all_gather.14 = bf16[256,384]{1,0:T(8,128)(2,1)S(1)} all-gather(bf16[64,384]{1,0:T(8,128)(2,1)S(1)} %copy-done.2), channel_id=1, replica_groups=mesh['groups'=2,'row'=4,'col'=4] {'col'}, dimensions={0}, use_global_device_ids=true | all-gather | bytes 245760 | tf_op jit(solution)/shard_map/all_gather | solution.py:15
  31.9 0.6 gather_fusion.1
  32.5 0.3 fusion.13
  33.0 0.7 reshape.81
  33.7 5.4 %all-to-all-start.2 = ((f32[4,1,192]{2,1,0:T(1,128)}), f32[4,1,192]{2,1,0:T(1,128)S(1)}, u32[]{:S(2)}, u32[]{:S(2)}) async-start(f32[4,1,192]{2,1,0:T(1,128)} %reshape.81), calls=%async_computation.2 | async-start | bytes 8192 | tf_op jit(solution)/shard_map/all_to_all | solution.py:82
  39.1 6.6 %all_gather.12 = bf16[256,384]{1,0:T(8,128)(2,1)S(1)} all-gather(bf16[64,384]{1,0:T(8,128)(2,1)S(1)} %copy-done.3), channel_id=1, replica_groups=mesh['groups'=2,'row'=4,'col'=4] {'row'}, dimensions={0}, use_global_device_ids=true | all-gather | bytes 245760 | tf_op jit(solution)/shard_map/all_gather | solution.py:18
  45.8 0.7 reshape.79
  46.5 0.6 gather_fusion
  47.2 5.1 %all-to-all-start.1 = ((f32[4,1,192]{2,1,0:T(1,128)}), f32[4,1,192]{2,1,0:T(1,128)S(1)}, u32[]{:S(2)}, u32[]{:S(2)}) async-start(f32[4,1,192]{2,1,0:T(1,128)} %reshape.79), calls=%async_computation.1 | async-start | bytes 8192 | tf_op jit(solution)/shard_map/all_to_all | solution.py:75
  52.3 0.3 convolution_bitcast_fusion
  52.9 1.0 %reshape_reshape.9 = f32[4,64,384]{2,1,0:T(8,128)} reshape(f32[2,128,3,128]{3,2,1,0:T(4,128)S(1)} %copy.76) | data formatting | bytes 786432 | tf_op jit(solution)/shard_map/reshape;reshape | solution.py:69
  53.8 4.0 %all-to-all-done.1 = f32[4,1,192]{2,1,0:T(1,128)S(1)} async-done(((f32[4,1,192]{2,1,0:T(1,128)}), f32[4,1,192]{2,1,0:T(1,128)S(1)}, u32[]{:S(2)}, u32[]{:S(2)}) %all-to-all-start.1) | async-done | bytes 3104 | tf_op jit(solution)/shard_map/all_to_all | solution.py:75
  57.9 3.5 %all-to-all-start = ((f32[4,64,384]{2,1,0:T(8,128)}), f32[4,64,384]{2,1,0:T(8,128)S(1)}, u32[]{:S(2)}, u32[]{:S(2)}) async-start(f32[4,64,384]{2,1,0:T(8,128)} %reshape_reshape.9), calls=%async_computation | async-start | bytes 786432 | tf_op jit(solution)/shard_map/all_to_all | solution.py:68
  61.3 0.5 broadcast.95
  61.8 0.7 reduce.2
  62.6 0.7 reduce.1
  63.5 0.3 mul.24
  64.2 8.2 %all-to-all-done = f32[4,64,384]{2,1,0:T(8,128)S(1)} async-done(((f32[4,64,384]{2,1,0:T(8,128)}), f32[4,64,384]{2,1,0:T(8,128)S(1)}, u32[]{:S(2)}, u32[]{:S(2)}) %all-to-all-start) | async-done | bytes 393248 | tf_op jit(solution)/shard_map/all_to_all | solution.py:68
  72.5 3.0 %fusion = bf16[64,2560]{1,0:T(8,128)(2,1)} fusion(bf16[384,2560]{0,1:T(8,128)(2,1)} %all-gather.2.cloned.1.call-done, bf16[64,2560]{1,0:T(8,128)(2,1)S(1)} %copy-done.1, f32[64,384]{1,0:T(8,128)S(1)} %multiply_reduce_fusion, f32[8,8,3,128]{3,2,1,0:T(4,128)S(1)} %bitcast.38), kind=kOutput, calls=%fused_computation.4 | convolution fusion | flops 126369792 | bytes 2818048 | tf_op jit(solution)/shard_map/dot_general | solution.py:97
  (47 shorter events, 2.4 us)
Async XLA Ops:
  6.5 9.7 %copy-start = (s32[2,2]{1,0:T(2,128)S(1)}, s32[2,2]{1,0:T(2,128)}, u32[]{:S(2)}) copy-start(s32[2,2]{1,0:T(2,128)} %param.9) | copy-start | bytes 52
  6.5 10.6 %copy-start.2 = (bf16[64,384]{1,0:T(8,128)(2,1)S(1)}, bf16[64,384]{1,0:T(8,128)(2,1)}, u32[]{:S(2)}) copy-start(bf16[64,384]{1,0:T(8,128)(2,1)} %param.6) | copy-start | bytes 147460
  6.5 65.9 %all-gather.2.cloned.1.call-start = ((), (), s32[]{:S(2)}) async-start(), calls=%async_computation.3 | async-start | bytes 2088960 | tf_op jit(solution)/shard_map/all_gather | solution.py:99
  31.8 7.3 %copy-start.3 = (bf16[64,384]{1,0:T(8,128)(2,1)S(1)}, bf16[64,384]{1,0:T(8,128)(2,1)}, u32[]{:S(2)}) copy-start(bf16[64,384]{1,0:T(8,128)(2,1)} %param.8) | copy-start | bytes 147460
  33.7 13.5 %all-to-all-start.2 = ((f32[4,1,192]{2,1,0:T(1,128)}), f32[4,1,192]{2,1,0:T(1,128)S(1)}, u32[]{:S(2)}, u32[]{:S(2)}) async-start(f32[4,1,192]{2,1,0:T(1,128)} %reshape.81), calls=%async_computation.2 | async-start | bytes 8192 | tf_op jit(solution)/shard_map/all_to_all | solution.py:82
  47.2 10.7 %all-to-all-start.1 = ((f32[4,1,192]{2,1,0:T(1,128)}), f32[4,1,192]{2,1,0:T(1,128)S(1)}, u32[]{:S(2)}, u32[]{:S(2)}) async-start(f32[4,1,192]{2,1,0:T(1,128)} %reshape.79), calls=%async_computation.1 | async-start | bytes 8192 | tf_op jit(solution)/shard_map/all_to_all | solution.py:75
  53.8 18.7 %copy-start.1 = (bf16[64,2560]{1,0:T(8,128)(2,1)S(1)}, bf16[64,2560]{1,0:T(8,128)(2,1)}, u32[]{:S(2)}) copy-start(bf16[64,2560]{1,0:T(8,128)(2,1)} %param.11) | copy-start | bytes 983044
  57.9 14.5 %all-to-all-start = ((f32[4,64,384]{2,1,0:T(8,128)}), f32[4,64,384]{2,1,0:T(8,128)S(1)}, u32[]{:S(2)}, u32[]{:S(2)}) async-start(f32[4,64,384]{2,1,0:T(8,128)} %reshape_reshape.9), calls=%async_computation | async-start | bytes 786432 | tf_op jit(solution)/shard_map/all_to_all | solution.py:68
Sparse Core Ops, SparseCore 0:
  9.7 45.7 all-gather.1
where the time goes:
time: 82.8 us; the launch traced here: 82.4 us
  blocking collectives  28.3 us (34%)
  starting transfers between devices  13.9 us (17%)
  between operations  13.6 us (16%)
  waiting for transfers between devices  12.9 us (16%)
  local copies, waits for them, and re-layouts  7.88 us (10%)
  matrix products  3.62 us (4%)
  other arithmetic  2.23 us (3%)
    all_gather x1, blocking collectives, local(): query_tile = lax.all_gather(queries, 'col', axis=0, tiled=True)  14.6 us
    all_to_all x1, waiting for transfers between devices, local(): lax.all_to_all(tile_sum.reshape(col_count, own_rows, HEADS * HD), 'col',...  8.17 us
    all_gather x1, blocking collectives, local(): lax.all_gather(keys, 'row', axis=0, tiled=True)  7.03 us
    all_gather x1, blocking collectives, local(): lax.all_gather(values, 'row', axis=0, tiled=True)  6.61 us
    all_to_all x1, starting transfers between devices, local(): lax.all_to_all(tile_total.reshape(col_count, own_rows, HEADS), 'col', spl...  5.35 us
    all_to_all x1, starting transfers between devices, local(): lax.all_to_all(tile_max.reshape(col_count, own_rows, HEADS), 'col', split...  5.1 us
    all_to_all x1, waiting for transfers between devices, local(): lax.all_to_all(tile_max.reshape(col_count, own_rows, HEADS), 'col', split...  4.02 us
    all_to_all x1, starting transfers between devices, local(): lax.all_to_all(tile_sum.reshape(col_count, own_rows, HEADS * HD), 'col',...  3.46 us
  transfers between devices with their start and end apart: 4, of which 2 were waited for; matrix products, arithmetic and copies ran while one was open for 13% of the time, Pallas kernels for 0%

commit v1 on v0

v1 whole, which is shorter than its diff:
```python
import functools
import math

import jax
import jax.numpy as jnp
from jax import lax
from jax.experimental import pallas as pl
from jax.experimental.pallas import tpu as pltpu
from jax.sharding import PartitionSpec as P

HD = 128
BLK = 128
LANES = 128
PARTS = 3


def swap(x, axis, mask):
    return lax.ppermute(x, axis, [(i, i ^ mask) for i in range(lax.axis_size(axis))])


def split3(x):
    high = x.astype(jnp.bfloat16).astype(jnp.float32)
    rest = x - high
    middle = rest.astype(jnp.bfloat16).astype(jnp.float32)
    return (high, middle, rest - middle)


def attend_kernel(q_masks, k_masks, where_ref, mask_ref, *refs):
    nq, nk = len(q_masks), len(k_masks)
    q_refs, k_refs, v_refs = refs[:nq], refs[nq : nq + nk], refs[nq + nk : nq + 2 * nk]
    out_refs = refs[nq + 2 * nk : 2 * nq + 2 * nk]
    rows, width = q_refs[0].shape
    heads = width // HD
    scale = 1.0 / math.sqrt(HD)
    my_row, my_col = where_ref[0], where_ref[1]
    keys = nk * rows
    piece_of_lane = lax.broadcasted_iota(jnp.int32, (1, keys), 1) // rows
    group = min(nq, 4)
    lane = lax.broadcasted_iota(jnp.int32, (group * rows, LANES), 1)
    for first in range(0, nq, group):
        chosen = range(first, first + group)
        lines = []
        for i in chosen:
            q_block = ((my_col ^ q_masks[i]) * rows) // BLK
            line = jnp.zeros((1, keys), jnp.float32)
            for j in range(nk):
                k_block = ((my_row ^ k_masks[j]) * rows) // BLK
                hidden = jnp.where(mask_ref[q_block, k_block] == 1, 0.0, -jnp.inf)
                line = jnp.where(piece_of_lane == j, hidden, line)
            lines.append(jnp.broadcast_to(line, (rows, keys)))
        bias = jnp.concatenate(lines, axis=0)
        stats = jnp.zeros((group * rows, LANES), jnp.float32)
        for h in range(heads):
            columns = slice(h * HD, (h + 1) * HD)
            q = jnp.concatenate([q_refs[i][:, columns] for i in chosen], axis=0)
            k = jnp.concatenate([r[:, columns] for r in k_refs], axis=0)
            v = jnp.concatenate([r[:, columns] for r in v_refs], axis=0)
            scores = lax.dot_general(
                q, k, (((1,), (1,)), ((), ())), preferred_element_type=jnp.float32
            )
            scores = scores * scale + bias
            top = jnp.max(scores, axis=1, keepdims=True)
            weights = jnp.exp(scores - top)
            total = jnp.sum(weights, axis=1, keepdims=True)
            summed = jnp.dot(weights.astype(jnp.bfloat16), v, preferred_element_type=jnp.float32)
            mean = (summed / total).astype(jnp.bfloat16)
            for n, i in enumerate(chosen):
                out_refs[i][:, columns] = mean[n * rows : (n + 1) * rows]
            for n, piece in enumerate(split3(top) + split3(total)):
                stats = jnp.where(lane == h * 2 * PARTS + n, piece, stats)
        stats = stats.astype(jnp.bfloat16)
        for n, i in enumerate(chosen):
            out_refs[i][:, width:] = stats[n * rows : (n + 1) * rows]


def attend(where, mask, q_parts, k_parts, v_parts):
    q_masks, k_masks = tuple(q_parts), tuple(k_parts)
    rows, width = q_parts[0].shape
    smem = pl.BlockSpec(memory_space=pltpu.SMEM)
    vmem = pl.BlockSpec(memory_space=pltpu.VMEM)
    arrays = [*q_parts.values(), *k_parts.values(), *v_parts.values()]
    outs = pl.pallas_call(
        functools.partial(attend_kernel, q_masks, k_masks),
        out_shape=[jax.ShapeDtypeStruct((rows, width + LANES), jnp.bfloat16)] * len(q_masks),
        in_specs=[smem, smem] + [vmem] * len(arrays),
        out_specs=[vmem] * len(q_masks),
        compiler_params=pltpu.CompilerParams(vmem_limit_bytes=24 * 2**20),
    )(where, mask, *arrays)
    return dict(zip(q_masks, outs))


def project_kernel(n_parts, w_ids, n_col, where_ref, *refs):
    part_refs = refs[:n_parts]
    w_refs = refs[n_parts : n_parts + len(w_ids)]
    residual_ref, out_ref, whole_ref = refs[n_parts + len(w_ids) :]
    rows, width = out_ref.shape[0], whole_ref.shape[1]
    heads = width // HD
    my_row, my_col = where_ref[0], where_ref[1]
    for (a, b), ref in zip(w_ids, w_refs):
        depth = ref.shape[0]
        place = ((my_row ^ a) * n_col + (my_col ^ b)) * depth
        whole_ref[pl.ds(pl.multiple_of(place, 16), depth), :] = ref[...]
    stats = [ref[:, width:].astype(jnp.float32) for ref in part_refs]
    attended = []
    for h in range(heads):
        columns = slice(h * HD, (h + 1) * HD)
        first = h * 2 * PARTS
        tops = [s[:, first : first + 1] + s[:, first + 1 : first + 2] + s[:, first + 2 : first + 3] for s in stats]
        first += PARTS
        totals = [s[:, first : first + 1] + s[:, first + 1 : first + 2] + s[:, first + 2 : first + 3] for s in stats]
        top = functools.reduce(jnp.maximum, tops)
        shares = [jnp.exp(t - top) * n for t, n in zip(tops, totals)]
        denom = functools.reduce(jnp.add, shares)
        numer = functools.reduce(
            jnp.add, [ref[:, columns].astype(jnp.float32) * s for ref, s in zip(part_refs, shares)]
        )
        attended.append((numer / denom).astype(jnp.bfloat16))
    attended = jnp.concatenate(attended, axis=1)
    features = out_ref.shape[1]
    step = features // 4 if features % (4 * LANES) == 0 else features
    for at in range(0, features, step):
        here = slice(at, at + step)
        product = lax.dot_general(
            attended, whole_ref[here, :], (((1,), (1,)), ((), ())), preferred_element_type=jnp.float32
        )
        out_ref[:, here] = (product + residual_ref[:, here].astype(jnp.float32)).astype(out_ref.dtype)


def project(where, parts, w_parts, residual, n_col):
    w_ids = tuple(w_parts)
    rows, features = residual.shape
    width = w_parts[w_ids[0]].shape[1]
    smem = pl.BlockSpec(memory_space=pltpu.SMEM)
    vmem = pl.BlockSpec(memory_space=pltpu.VMEM)
    arrays = [*parts.values(), *w_parts.values(), residual]
    return pl.pallas_call(
        functools.partial(project_kernel, len(parts), w_ids, n_col),
        out_shape=jax.ShapeDtypeStruct((rows, features), residual.dtype),
        in_specs=[smem] + [vmem] * len(arrays),
        out_specs=vmem,
        scratch_shapes=[pltpu.VMEM((features, width), jnp.bfloat16)],
        compiler_params=pltpu.CompilerParams(vmem_limit_bytes=24 * 2**20),
    )(where, *arrays)


def local(queries, keys, values, block_mask, out_weight, residual):
    n_row, n_col = lax.axis_size("row"), lax.axis_size("col")
    far = range(n_col - 1, 0, -1)
    chips = range(2, n_row, 2)
    where = jnp.stack([lax.axis_index("row"), lax.axis_index("col")]).astype(jnp.int32)

    q_parts = {0: queries}
    for m in far:
        q_parts[m] = swap(queries, "col", m)
    k_parts, v_parts = {0: keys}, {0: values}
    for m in chips:
        k_parts[m] = swap(keys, "row", m)
        v_parts[m] = swap(values, "row", m)
    for m in (0, *chips):
        k_parts[m | 1] = swap(k_parts[m], "row", 1)
        v_parts[m | 1] = swap(v_parts[m], "row", 1)

    depth = out_weight.shape[1]
    if depth % 16 == 0:
        w_parts = {(0, 0): out_weight.T}
        for m in far:
            w_parts[0, m] = swap(w_parts[0, 0], "col", m)
        for b in (0, *far):
            for a in chips:
                w_parts[a, b] = swap(w_parts[0, b], "row", a)
        for a, b in list(w_parts):
            w_parts[a | 1, b] = swap(w_parts[a, b], "row", 1)
    else:
        gathered = lax.all_gather(out_weight, ("row", "col"), axis=1, tiled=True)
        w_parts = None

    partial = attend(where, block_mask, q_parts, k_parts, v_parts)
    parts = {0: partial[0]}
    for m in far:
        parts[m] = swap(partial[m], "col", m)
    if w_parts is None:
        zero = jnp.zeros((2,), jnp.int32)
        return project(zero, parts, {(0, 0): gathered.T}, residual, 1)
    return project(where, parts, w_parts, residual, n_col)


def solution(mesh):
    placed = (
        P(("groups", "row", "col"), None),
        P(("groups", "col", "row"), None),
        P(("groups", "col", "row"), None),
        P(("groups", "row"), "col"),
        P(None, ("row", "col")),
        P(("groups", "row", "col"), None),
    )
    return jax.shard_map(
        local,
        mesh=mesh,
        in_specs=placed,
        out_specs=P(("groups", "row", "col"), None),
        check_vma=False,
    )
```

time: 82.8 us -> 45.2 us (0.55)
  the two profiles are of different devices: /device:TPU:0 before, /device:TPU:17 now
where the time goes in v1:
time: 45.2 us; the launch traced here: 44.9 us
  starting transfers between devices  33.8 us (75%)
  waiting for transfers between devices  4.12 us (9%)
  Pallas kernels  3.81 us (8%)
  local copies, waits for them, and re-layouts  3.08 us (7%)
    ppermute x27, starting transfers between devices, swap(): lax.ppermute(x, axis, [(i, i ^ mask) for i in range(lax.axis_size(axis))])  33.8 us
    ppermute x27, waiting for transfers between devices, swap(): lax.ppermute(x, axis, [(i, i ^ mask) for i in range(lax.axis_size(axis))])  4.12 us
    unnamed x12, local copies, waits for them, and re-layouts  3.08 us
    pallas_call x1, Pallas kernels, project(): pl.pallas_call(functools.partial(project_kernel, len(parts), w_ids, n_col...  2.41 us
    pallas_call x1, Pallas kernels, attend(): pl.pallas_call(functools.partial(attend_kernel, q_masks, k_masks), out_sh...  1.4 us
  transfers between devices with their start and end apart: 27, of which 4 were waited for; matrix products, arithmetic and copies ran while one was open for 0% of the time, Pallas kernels for 3%

profile of v1, /device:TPU:17, one launch (start us, length us, event | category | flops | bytes accessed | tf_op | source)
XLA Modules:
  0.0 44.9 jit_solution(14688404277208544934)
XLA Ops:
  0.0 1.2 %collective-permute-start.3 = (bf16[64,384]{1,0:T(8,128)(2,1)}, bf16[64,384]{1,0:T(8,128)(2,1)S(1)}, u32[]{:S(2)}, u32[]{:S(2)}) collective-permute-start(bf16[64,384]{1,0:T(8,128)(2,1)} %refs_4_.1), channel_id=1, source_target_pairs={{0,8},{4,12},{8,0},{12,4},{1,9},{5,13},{9,1},{13,5},{2,10},{6,14},... | collective-permute-start | bytes 147464 | tf_op jit(solution)/shard_map/ppermute | solution.py:18
  1.2 1.0 %collective-permute-start.4 = (bf16[64,384]{1,0:T(8,128)(2,1)}, bf16[64,384]{1,0:T(8,128)(2,1)S(1)}, u32[]{:S(2)}, u32[]{:S(2)}) collective-permute-start(bf16[64,384]{1,0:T(8,128)(2,1)} %refs_4_.1), channel_id=1, source_target_pairs={{0,4},{4,0},{8,12},{12,8},{1,5},{5,1},{9,13},{13,9},{2,6},{6,2},{1... | collective-permute-start | bytes 147464 | tf_op jit(solution)/shard_map/ppermute | solution.py:18
  3.2 2.0 %collective-permute-start = (bf16[64,384]{1,0:T(8,128)(2,1)}, bf16[64,384]{1,0:T(8,128)(2,1)S(1)}, u32[]{:S(2)}, u32[]{:S(2)}) collective-permute-start(bf16[64,384]{1,0:T(8,128)(2,1)} %refs_0_.1), channel_id=1, source_target_pairs={{0,3},{1,2},{2,1},{3,0},{4,7},{5,6},{6,5},{7,4},{8,11},{9,10},{10,... | collective-permute-start | bytes 147464 | tf_op jit(solution)/shard_map/ppermute | solution.py:18
  5.2 1.1 %collective-permute-start.2 = (bf16[64,384]{1,0:T(8,128)(2,1)}, bf16[64,384]{1,0:T(8,128)(2,1)S(1)}, u32[]{:S(2)}, u32[]{:S(2)}) collective-permute-start(bf16[64,384]{1,0:T(8,128)(2,1)} %refs_0_.1), channel_id=1, source_target_pairs={{0,1},{1,0},{2,3},{3,2},{4,5},{5,4},{6,7},{7,6},{8,9},{9,8},{10,11... | collective-permute-start | bytes 147464 | tf_op jit(solution)/shard_map/ppermute | solution.py:18
  6.3 1.1 %collective-permute-start.5 = (bf16[64,384]{1,0:T(8,128)(2,1)S(1)}, bf16[64,384]{1,0:T(8,128)(2,1)S(1)}, u32[]{:S(2)}, u32[]{:S(2)}) collective-permute-start(bf16[64,384]{1,0:T(8,128)(2,1)S(1)} %collective-permute-done.3.refs_5_), channel_id=1, source_target_pairs={{0,4},{4,0},{8,12},{12,8},{1,5},{5,1},{9,13},{13,9},{2,6},{6,2},{1... | collective-permute-start | bytes 147464 | tf_op jit(solution)/shard_map/ppermute | solution.py:18
  8.1 1.9 %collective-permute-done.refs_1_ = bf16[64,384]{1,0:T(8,128)(2,1)S(1)} collective-permute-done((bf16[64,384]{1,0:T(8,128)(2,1)}, bf16[64,384]{1,0:T(8,128)(2,1)S(1)}, u32[]{:S(2)}, u32[]{:S(2)}) %collective-permute-start) | collective-permute-done | bytes 49184 | tf_op jit(solution)/shard_map/ppermute | solution.py:18
  10.0 1.2 %collective-permute-start.15 = (bf16[160,384]{1,0:T(8,128)(2,1)}, bf16[160,384]{1,0:T(8,128)(2,1)S(1)}, u32[]{:S(2)}, u32[]{:S(2)}) collective-permute-start(bf16[160,384]{1,0:T(8,128)(2,1)} %bitcast.4), channel_id=1, source_target_pairs={{0,8},{4,12},{8,0},{12,4},{1,9},{5,13},{9,1},{13,5},{2,10},{6,14},... | collective-permute-start | bytes 368648 | tf_op jit(solution)/shard_map/ppermute | solution.py:18
  11.3 0.9 %collective-permute-start.14 = (bf16[160,384]{1,0:T(8,128)(2,1)}, bf16[160,384]{1,0:T(8,128)(2,1)S(1)}, u32[]{:S(2)}, u32[]{:S(2)}) collective-permute-start(bf16[160,384]{1,0:T(8,128)(2,1)} %bitcast.5), channel_id=1, source_target_pairs={{0,1},{1,0},{2,3},{3,2},{4,5},{5,4},{6,7},{7,6},{8,9},{9,8},{10,11... | collective-permute-start | bytes 368648 | tf_op jit(solution)/shard_map/ppermute | solution.py:18
  12.6 1.3 %collective-permute-start.12 = (bf16[160,384]{1,0:T(8,128)(2,1)}, bf16[160,384]{1,0:T(8,128)(2,1)S(1)}, u32[]{:S(2)}, u32[]{:S(2)}) collective-permute-start(bf16[160,384]{1,0:T(8,128)(2,1)} %bitcast.7), channel_id=1, source_target_pairs={{0,3},{1,2},{2,1},{3,0},{4,7},{5,6},{6,5},{7,4},{8,11},{9,10},{10,... | collective-permute-start | bytes 368648 | tf_op jit(solution)/shard_map/ppermute | solution.py:18
  14.0 0.8 %copy-done.2 = bf16[64,384]{1,0:T(8,128)(2,1)S(1)} copy-done((bf16[64,384]{1,0:T(8,128)(2,1)S(1)}, bf16[64,384]{1,0:T(8,128)(2,1)}, u32[]{:S(2)}) %copy-start.2) | copy-done | bytes 49176
  14.8 0.8 %copy-done.3 = bf16[64,384]{1,0:T(8,128)(2,1)S(1)} copy-done((bf16[64,384]{1,0:T(8,128)(2,1)S(1)}, bf16[64,384]{1,0:T(8,128)(2,1)}, u32[]{:S(2)}) %copy-start.3) | copy-done | bytes 49176
  15.6 0.8 %copy-done.4 = bf16[64,384]{1,0:T(8,128)(2,1)S(1)} copy-done((bf16[64,384]{1,0:T(8,128)(2,1)S(1)}, bf16[64,384]{1,0:T(8,128)(2,1)}, u32[]{:S(2)}) %copy-start.4) | copy-done | bytes 49176
  17.1 1.4 %shard_map.64 = (bf16[64,512]{1,0:T(8,128)(2,1)S(1)}, bf16[64,512]{1,0:T(8,128)(2,1)S(1)}, bf16[64,512]{1,0:T(8,128)(2,1)S(1)}, bf16[64,512]{1,0:T(8,128)(2,1)S(1)}) custom-call(s32[2]{0:T(128)S(1)} %pad_add_fusion.where_ref, s32[2,2]{1,0:T(2,128)S(1)} %copy-done.5, bf16[64,384]{1,0:T(8,128)(2,1)S(1)} %copy-done.2, ...), custom_call_target="tpu_custom_call" | custom-call | tf_op jit(solution)/shard_map/pallas_call | solution.py:82
  18.7 3.7 %collective-permute-start.10 = (bf16[64,512]{1,0:T(8,128)(2,1)S(1)}, bf16[64,512]{1,0:T(8,128)(2,1)S(1)}, u32[]{:S(2)}, u32[]{:S(2)}) collective-permute-start(bf16[64,512]{1,0:T(8,128)(2,1)S(1)} %get-tuple-element.11), channel_id=1, source_target_pairs={{0,2},{1,3},{2,0},{3,1},{4,6},{5,7},{6,4},{7,5},{8,10},{9,11},{10,... | collective-permute-start | bytes 196616 | tf_op jit(solution)/shard_map/ppermute | solution.py:18
  22.4 3.7 %collective-permute-start.23 = (bf16[160,384]{1,0:T(8,128)(2,1)S(1)}, bf16[160,384]{1,0:T(8,128)(2,1)S(1)}, u32[]{:S(2)}, u32[]{:S(2)}) collective-permute-start(bf16[160,384]{1,0:T(8,128)(2,1)S(1)} %collective-permute-done.15.refs_8_), channel_id=1, source_target_pairs={{0,4},{4,0},{8,12},{12,8},{1,5},{5,1},{9,13},{13,9},{2,6},{6,2},{1... | collective-permute-start | bytes 368648 | tf_op jit(solution)/shard_map/ppermute | solution.py:18
  26.1 4.4 %collective-permute-start.22 = (bf16[160,384]{1,0:T(8,128)(2,1)S(1)}, bf16[160,384]{1,0:T(8,128)(2,1)S(1)}, u32[]{:S(2)}, u32[]{:S(2)}) collective-permute-start(bf16[160,384]{1,0:T(8,128)(2,1)S(1)} %collective-permute-done.14.refs_7_), channel_id=1, source_target_pairs={{0,4},{4,0},{8,12},{12,8},{1,5},{5,1},{9,13},{13,9},{2,6},{6,2},{1... | collective-permute-start | bytes 368648 | tf_op jit(solution)/shard_map/ppermute | solution.py:18
  30.5 1.5 %collective-permute-start.17 = (bf16[160,384]{1,0:T(8,128)(2,1)S(1)}, bf16[160,384]{1,0:T(8,128)(2,1)S(1)}, u32[]{:S(2)}, u32[]{:S(2)}) collective-permute-start(bf16[160,384]{1,0:T(8,128)(2,1)S(1)} %collective-permute-done.13.refs_6_), channel_id=1, source_target_pairs={{0,8},{4,12},{8,0},{12,4},{1,9},{5,13},{9,1},{13,5},{2,10},{6,14},... | collective-permute-start | bytes 368648 | tf_op jit(solution)/shard_map/ppermute | solution.py:18
  32.1 1.7 %collective-permute-start.21 = (bf16[160,384]{1,0:T(8,128)(2,1)S(1)}, bf16[160,384]{1,0:T(8,128)(2,1)S(1)}, u32[]{:S(2)}, u32[]{:S(2)}) collective-permute-start(bf16[160,384]{1,0:T(8,128)(2,1)S(1)} %collective-permute-done.13.refs_6_), channel_id=1, source_target_pairs={{0,4},{4,0},{8,12},{12,8},{1,5},{5,1},{9,13},{13,9},{2,6},{6,2},{1... | collective-permute-start | bytes 368648 | tf_op jit(solution)/shard_map/ppermute | solution.py:18
  33.9 0.8 %collective-permute-done.18.refs_11_ = bf16[160,384]{1,0:T(8,128)(2,1)S(1)} collective-permute-done((bf16[160,384]{1,0:T(8,128)(2,1)S(1)}, bf16[160,384]{1,0:T(8,128)(2,1)S(1)}, u32[]{:S(2)}, u32[]{:S(2)}) %collective-permute-start.18) | collective-permute-done | bytes 122912 | tf_op jit(solution)/shard_map/ppermute | solution.py:18
  34.6 2.9 %collective-permute-start.26 = (bf16[160,384]{1,0:T(8,128)(2,1)S(1)}, bf16[160,384]{1,0:T(8,128)(2,1)S(1)}, u32[]{:S(2)}, u32[]{:S(2)}) collective-permute-start(bf16[160,384]{1,0:T(8,128)(2,1)S(1)} %collective-permute-done.18.refs_11_), channel_id=1, source_target_pairs={{0,4},{4,0},{8,12},{12,8},{1,5},{5,1},{9,13},{13,9},{2,6},{6,2},{1... | collective-permute-start | bytes 368648 | tf_op jit(solution)/shard_map/ppermute | solution.py:18
  37.5 2.6 %collective-permute-start.25 = (bf16[160,384]{1,0:T(8,128)(2,1)S(1)}, bf16[160,384]{1,0:T(8,128)(2,1)S(1)}, u32[]{:S(2)}, u32[]{:S(2)}) collective-permute-start(bf16[160,384]{1,0:T(8,128)(2,1)S(1)} %collective-permute-done.17.refs_10_), channel_id=1, source_target_pairs={{0,4},{4,0},{8,12},{12,8},{1,5},{5,1},{9,13},{13,9},{2,6},{6,2},{1... | collective-permute-start | bytes 368648 | tf_op jit(solution)/shard_map/ppermute | solution.py:18
  40.1 1.4 %collective-permute-start.24 = (bf16[160,384]{1,0:T(8,128)(2,1)S(1)}, bf16[160,384]{1,0:T(8,128)(2,1)S(1)}, u32[]{:S(2)}, u32[]{:S(2)}) collective-permute-start(bf16[160,384]{1,0:T(8,128)(2,1)S(1)} %collective-permute-done.16.refs_9_), channel_id=1, source_target_pairs={{0,4},{4,0},{8,12},{12,8},{1,5},{5,1},{9,13},{13,9},{2,6},{6,2},{1... | collective-permute-start | bytes 368648 | tf_op jit(solution)/shard_map/ppermute | solution.py:18
  41.5 1.0 %collective-permute-done.24.refs_17_ = bf16[160,384]{1,0:T(8,128)(2,1)S(1)} collective-permute-done((bf16[160,384]{1,0:T(8,128)(2,1)S(1)}, bf16[160,384]{1,0:T(8,128)(2,1)S(1)}, u32[]{:S(2)}, u32[]{:S(2)}) %collective-permute-start.24) | collective-permute-done | bytes 122912 | tf_op jit(solution)/shard_map/ppermute | solution.py:18
  42.5 2.4 %shard_map.65 = bf16[64,2560]{1,0:T(8,128)(2,1)} custom-call(s32[2]{0:T(128)S(1)} %pad_add_fusion.where_ref, bf16[64,512]{1,0:T(8,128)(2,1)S(1)} %get-tuple-element.9.refs_0_, bf16[64,512]{1,0:T(8,128)(2,1)S(1)} %collective-permute-done.9.refs_1_, bf16[64,512]{1,0:T(8,128)(2,1)S(1)} %collective-permute-done.10.refs_2_, ...), custom_call_target="tpu_custom_call" | custom-call | tf_op jit(solution)/shard_map/pallas_call | solution.py:136
  (45 shorter events, 3.4 us)
Async XLA Ops:
  2.2 4.1 %collective-permute-start.6 = (bf16[64,384]{1,0:T(8,128)(2,1)}, bf16[64,384]{1,0:T(8,128)(2,1)S(1)}, u32[]{:S(2)}, u32[]{:S(2)}) collective-permute-start(bf16[64,384]{1,0:T(8,128)(2,1)} %refs_8_.1), channel_id=1, source_target_pairs={{0,8},{4,12},{8,0},{12,4},{1,9},{5,13},{9,1},{13,5},{2,10},{6,14},... | collective-permute-start | bytes 147464 | tf_op jit(solution)/shard_map/ppermute | solution.py:18
  2.4 4.9 %collective-permute-start.7 = (bf16[64,384]{1,0:T(8,128)(2,1)}, bf16[64,384]{1,0:T(8,128)(2,1)S(1)}, u32[]{:S(2)}, u32[]{:S(2)}) collective-permute-start(bf16[64,384]{1,0:T(8,128)(2,1)} %refs_8_.1), channel_id=1, source_target_pairs={{0,4},{4,0},{8,12},{12,8},{1,5},{5,1},{9,13},{13,9},{2,6},{6,2},{1... | collective-permute-start | bytes 147464 | tf_op jit(solution)/shard_map/ppermute | solution.py:18
  2.7 4.7 %collective-permute-start.1 = (bf16[64,384]{1,0:T(8,128)(2,1)}, bf16[64,384]{1,0:T(8,128)(2,1)S(1)}, u32[]{:S(2)}, u32[]{:S(2)}) collective-permute-start(bf16[64,384]{1,0:T(8,128)(2,1)} %refs_0_.1), channel_id=1, source_target_pairs={{0,2},{1,3},{2,0},{3,1},{4,6},{5,7},{6,4},{7,5},{8,10},{9,11},{10,... | collective-permute-start | bytes 147464 | tf_op jit(solution)/shard_map/ppermute | solution.py:18
  3.2 6.9 %collective-permute-start = (bf16[64,384]{1,0:T(8,128)(2,1)}, bf16[64,384]{1,0:T(8,128)(2,1)S(1)}, u32[]{:S(2)}, u32[]{:S(2)}) collective-permute-start(bf16[64,384]{1,0:T(8,128)(2,1)} %refs_0_.1), channel_id=1, source_target_pairs={{0,3},{1,2},{2,1},{3,0},{4,7},{5,6},{6,5},{7,4},{8,11},{9,10},{10,... | collective-permute-start | bytes 147464 | tf_op jit(solution)/shard_map/ppermute | solution.py:18
  5.2 6.1 %collective-permute-start.2 = (bf16[64,384]{1,0:T(8,128)(2,1)}, bf16[64,384]{1,0:T(8,128)(2,1)S(1)}, u32[]{:S(2)}, u32[]{:S(2)}) collective-permute-start(bf16[64,384]{1,0:T(8,128)(2,1)} %refs_0_.1), channel_id=1, source_target_pairs={{0,1},{1,0},{2,3},{3,2},{4,5},{5,4},{6,7},{7,6},{8,9},{9,8},{10,11... | collective-permute-start | bytes 147464 | tf_op jit(solution)/shard_map/ppermute | solution.py:18
  6.3 5.9 %collective-permute-start.5 = (bf16[64,384]{1,0:T(8,128)(2,1)S(1)}, bf16[64,384]{1,0:T(8,128)(2,1)S(1)}, u32[]{:S(2)}, u32[]{:S(2)}) collective-permute-start(bf16[64,384]{1,0:T(8,128)(2,1)S(1)} %collective-permute-done.3.refs_5_), channel_id=1, source_target_pairs={{0,4},{4,0},{8,12},{12,8},{1,5},{5,1},{9,13},{13,9},{2,6},{6,2},{1... | collective-permute-start | bytes 147464 | tf_op jit(solution)/shard_map/ppermute | solution.py:18
  7.3 5.2 %collective-permute-start.8 = (bf16[64,384]{1,0:T(8,128)(2,1)S(1)}, bf16[64,384]{1,0:T(8,128)(2,1)S(1)}, u32[]{:S(2)}, u32[]{:S(2)}) collective-permute-start(bf16[64,384]{1,0:T(8,128)(2,1)S(1)} %collective-permute-done.6.refs_9_), channel_id=1, source_target_pairs={{0,4},{4,0},{8,12},{12,8},{1,5},{5,1},{9,13},{13,9},{2,6},{6,2},{1... | collective-permute-start | bytes 147464 | tf_op jit(solution)/shard_map/ppermute | solution.py:18
  7.4 11.1 %collective-permute-start.19 = (bf16[160,384]{1,0:T(8,128)(2,1)}, bf16[160,384]{1,0:T(8,128)(2,1)S(1)}, u32[]{:S(2)}, u32[]{:S(2)}) collective-permute-start(bf16[160,384]{1,0:T(8,128)(2,1)} %bitcast.3), channel_id=1, source_target_pairs={{0,4},{4,0},{8,12},{12,8},{1,5},{5,1},{9,13},{13,9},{2,6},{6,2},{1... | collective-permute-start | bytes 368648 | tf_op jit(solution)/shard_map/ppermute | solution.py:18
  10.0 8.6 %collective-permute-start.15 = (bf16[160,384]{1,0:T(8,128)(2,1)}, bf16[160,384]{1,0:T(8,128)(2,1)S(1)}, u32[]{:S(2)}, u32[]{:S(2)}) collective-permute-start(bf16[160,384]{1,0:T(8,128)(2,1)} %bitcast.4), channel_id=1, source_target_pairs={{0,8},{4,12},{8,0},{12,4},{1,9},{5,13},{9,1},{13,5},{2,10},{6,14},... | collective-permute-start | bytes 368648 | tf_op jit(solution)/shard_map/ppermute | solution.py:18
  11.3 11.1 %collective-permute-start.14 = (bf16[160,384]{1,0:T(8,128)(2,1)}, bf16[160,384]{1,0:T(8,128)(2,1)S(1)}, u32[]{:S(2)}, u32[]{:S(2)}) collective-permute-start(bf16[160,384]{1,0:T(8,128)(2,1)} %bitcast.5), channel_id=1, source_target_pairs={{0,1},{1,0},{2,3},{3,2},{4,5},{5,4},{6,7},{7,6},{8,9},{9,8},{10,11... | collective-permute-start | bytes 368648 | tf_op jit(solution)/shard_map/ppermute | solution.py:18
  12.1 10.3 %collective-permute-start.13 = (bf16[160,384]{1,0:T(8,128)(2,1)}, bf16[160,384]{1,0:T(8,128)(2,1)S(1)}, u32[]{:S(2)}, u32[]{:S(2)}) collective-permute-start(bf16[160,384]{1,0:T(8,128)(2,1)} %bitcast.6), channel_id=1, source_target_pairs={{0,2},{1,3},{2,0},{3,1},{4,6},{5,7},{6,4},{7,5},{8,10},{9,11},{10,... | collective-permute-start | bytes 368648 | tf_op jit(solution)/shard_map/ppermute | solution.py:18
  12.6 13.5 %collective-permute-start.12 = (bf16[160,384]{1,0:T(8,128)(2,1)}, bf16[160,384]{1,0:T(8,128)(2,1)S(1)}, u32[]{:S(2)}, u32[]{:S(2)}) collective-permute-start(bf16[160,384]{1,0:T(8,128)(2,1)} %bitcast.7), channel_id=1, source_target_pairs={{0,3},{1,2},{2,1},{3,0},{4,7},{5,6},{6,5},{7,4},{8,11},{9,10},{10,... | collective-permute-start | bytes 368648 | tf_op jit(solution)/shard_map/ppermute | solution.py:18
  18.5 12.0 %collective-permute-start.9 = (bf16[64,512]{1,0:T(8,128)(2,1)S(1)}, bf16[64,512]{1,0:T(8,128)(2,1)S(1)}, u32[]{:S(2)}, u32[]{:S(2)}) collective-permute-start(bf16[64,512]{1,0:T(8,128)(2,1)S(1)} %get-tuple-element.10), channel_id=1, source_target_pairs={{0,3},{1,2},{2,1},{3,0},{4,7},{5,6},{6,5},{7,4},{8,11},{9,10},{10,... | collective-permute-start | bytes 196616 | tf_op jit(solution)/shard_map/ppermute | solution.py:18
  18.7 11.8 %collective-permute-start.10 = (bf16[64,512]{1,0:T(8,128)(2,1)S(1)}, bf16[64,512]{1,0:T(8,128)(2,1)S(1)}, u32[]{:S(2)}, u32[]{:S(2)}) collective-permute-start(bf16[64,512]{1,0:T(8,128)(2,1)S(1)} %get-tuple-element.11), channel_id=1, source_target_pairs={{0,2},{1,3},{2,0},{3,1},{4,6},{5,7},{6,4},{7,5},{8,10},{9,11},{10,... | collective-permute-start | bytes 196616 | tf_op jit(solution)/shard_map/ppermute | solution.py:18
  22.4 9.6 %collective-permute-start.11 = (bf16[64,512]{1,0:T(8,128)(2,1)S(1)}, bf16[64,512]{1,0:T(8,128)(2,1)S(1)}, u32[]{:S(2)}, u32[]{:S(2)}) collective-permute-start(bf16[64,512]{1,0:T(8,128)(2,1)S(1)} %get-tuple-element.12), channel_id=1, source_target_pairs={{0,1},{1,0},{2,3},{3,2},{4,5},{5,4},{6,7},{7,6},{8,9},{9,8},{10,11... | collective-permute-start | bytes 196616 | tf_op jit(solution)/shard_map/ppermute | solution.py:18
  22.4 9.7 %collective-permute-start.23 = (bf16[160,384]{1,0:T(8,128)(2,1)S(1)}, bf16[160,384]{1,0:T(8,128)(2,1)S(1)}, u32[]{:S(2)}, u32[]{:S(2)}) collective-permute-start(bf16[160,384]{1,0:T(8,128)(2,1)S(1)} %collective-permute-done.15.refs_8_), channel_id=1, source_target_pairs={{0,4},{4,0},{8,12},{12,8},{1,5},{5,1},{9,13},{13,9},{2,6},{6,2},{1... | collective-permute-start | bytes 368648 | tf_op jit(solution)/shard_map/ppermute | solution.py:18
  26.1 7.7 %collective-permute-start.22 = (bf16[160,384]{1,0:T(8,128)(2,1)S(1)}, bf16[160,384]{1,0:T(8,128)(2,1)S(1)}, u32[]{:S(2)}, u32[]{:S(2)}) collective-permute-start(bf16[160,384]{1,0:T(8,128)(2,1)S(1)} %collective-permute-done.14.refs_7_), channel_id=1, source_target_pairs={{0,4},{4,0},{8,12},{12,8},{1,5},{5,1},{9,13},{13,9},{2,6},{6,2},{1... | collective-permute-start | bytes 368648 | tf_op jit(solution)/shard_map/ppermute | solution.py:18
  30.5 4.1 %collective-permute-start.18 = (bf16[160,384]{1,0:T(8,128)(2,1)S(1)}, bf16[160,384]{1,0:T(8,128)(2,1)S(1)}, u32[]{:S(2)}, u32[]{:S(2)}) collective-permute-start(bf16[160,384]{1,0:T(8,128)(2,1)S(1)} %collective-permute-done.14.refs_7_), channel_id=1, source_target_pairs={{0,8},{4,12},{8,0},{12,4},{1,9},{5,13},{9,1},{13,5},{2,10},{6,14},... | collective-permute-start | bytes 368648 | tf_op jit(solution)/shard_map/ppermute | solution.py:18
  30.5 7.0 %collective-permute-start.17 = (bf16[160,384]{1,0:T(8,128)(2,1)S(1)}, bf16[160,384]{1,0:T(8,128)(2,1)S(1)}, u32[]{:S(2)}, u32[]{:S(2)}) collective-permute-start(bf16[160,384]{1,0:T(8,128)(2,1)S(1)} %collective-permute-done.13.refs_6_), channel_id=1, source_target_pairs={{0,8},{4,12},{8,0},{12,4},{1,9},{5,13},{9,1},{13,5},{2,10},{6,14},... | collective-permute-start | bytes 368648 | tf_op jit(solution)/shard_map/ppermute | solution.py:18
  32.0 8.1 %collective-permute-start.16 = (bf16[160,384]{1,0:T(8,128)(2,1)S(1)}, bf16[160,384]{1,0:T(8,128)(2,1)S(1)}, u32[]{:S(2)}, u32[]{:S(2)}) collective-permute-start(bf16[160,384]{1,0:T(8,128)(2,1)S(1)} %collective-permute-done.12.refs_5_), channel_id=1, source_target_pairs={{0,8},{4,12},{8,0},{12,4},{1,9},{5,13},{9,1},{13,5},{2,10},{6,14},... | collective-permute-start | bytes 368648 | tf_op jit(solution)/shard_map/ppermute | solution.py:18
  32.1 9.5 %collective-permute-start.21 = (bf16[160,384]{1,0:T(8,128)(2,1)S(1)}, bf16[160,384]{1,0:T(8,128)(2,1)S(1)}, u32[]{:S(2)}, u32[]{:S(2)}) collective-permute-start(bf16[160,384]{1,0:T(8,128)(2,1)S(1)} %collective-permute-done.13.refs_6_), channel_id=1, source_target_pairs={{0,4},{4,0},{8,12},{12,8},{1,5},{5,1},{9,13},{13,9},{2,6},{6,2},{1... | collective-permute-start | bytes 368648 | tf_op jit(solution)/shard_map/ppermute | solution.py:18
  33.8 7.7 %collective-permute-start.20 = (bf16[160,384]{1,0:T(8,128)(2,1)S(1)}, bf16[160,384]{1,0:T(8,128)(2,1)S(1)}, u32[]{:S(2)}, u32[]{:S(2)}) collective-permute-start(bf16[160,384]{1,0:T(8,128)(2,1)S(1)} %collective-permute-done.12.refs_5_), channel_id=1, source_target_pairs={{0,4},{4,0},{8,12},{12,8},{1,5},{5,1},{9,13},{13,9},{2,6},{6,2},{1... | collective-permute-start | bytes 368648 | tf_op jit(solution)/shard_map/ppermute | solution.py:18
  34.6 6.9 %collective-permute-start.26 = (bf16[160,384]{1,0:T(8,128)(2,1)S(1)}, bf16[160,384]{1,0:T(8,128)(2,1)S(1)}, u32[]{:S(2)}, u32[]{:S(2)}) collective-permute-start(bf16[160,384]{1,0:T(8,128)(2,1)S(1)} %collective-permute-done.18.refs_11_), channel_id=1, source_target_pairs={{0,4},{4,0},{8,12},{12,8},{1,5},{5,1},{9,13},{13,9},{2,6},{6,2},{1... | collective-permute-start | bytes 368648 | tf_op jit(solution)/shard_map/ppermute | solution.py:18
  37.5 4.0 %collective-permute-start.25 = (bf16[160,384]{1,0:T(8,128)(2,1)S(1)}, bf16[160,384]{1,0:T(8,128)(2,1)S(1)}, u32[]{:S(2)}, u32[]{:S(2)}) collective-permute-start(bf16[160,384]{1,0:T(8,128)(2,1)S(1)} %collective-permute-done.17.refs_10_), channel_id=1, source_target_pairs={{0,4},{4,0},{8,12},{12,8},{1,5},{5,1},{9,13},{13,9},{2,6},{6,2},{1... | collective-permute-start | bytes 368648 | tf_op jit(solution)/shard_map/ppermute | solution.py:18
  (9 other events, 80.5 us)

commit v2 on v1

v2 whole, which is shorter than its diff:
```python
import functools
import math

import jax
import jax.numpy as jnp
from jax import lax
from jax.experimental import pallas as pl
from jax.experimental.pallas import tpu as pltpu
from jax.sharding import PartitionSpec as P

HD = 128
BLK = 128
LANES = 128
PARTS = 3
SPAN = 8192.0


def swap(x, axis, mask):
    return lax.ppermute(x, axis, [(i, i ^ mask) for i in range(lax.axis_size(axis))])


def after(x, *others):
    return lax.optimization_barrier((x, *others))[0]


def split3(x):
    high = x.astype(jnp.bfloat16).astype(jnp.float32)
    rest = x - high
    middle = rest.astype(jnp.bfloat16).astype(jnp.float32)
    return (high, middle, rest - middle)


def attend_kernel(q_masks, k_masks, top, mask_shape, place_ref, *refs):
    nq, nk = len(q_masks), len(k_masks)
    q_refs, kv_refs, out_refs = refs[:nq], refs[nq : nq + nk], refs[nq + nk :]
    rows, width = q_refs[0].shape
    heads = width // HD
    scale = 1.0 / math.sqrt(HD)
    my_row, my_col = place_ref[0], place_ref[1]
    keys = nk * rows
    piece_of_lane = lax.broadcasted_iota(jnp.int32, (1, keys), 1) // rows
    group = min(nq, 4)
    lane = lax.broadcasted_iota(jnp.int32, (group * rows, LANES), 1)
    for first in range(0, nq, group):
        chosen = range(first, first + group)
        lines = []
        for i in chosen:
            q_block = ((my_col ^ q_masks[i]) * rows) // BLK
            line = jnp.zeros((1, keys), jnp.float32)
            for j, (a, b) in enumerate(k_masks):
                k_block = ((my_row ^ a) * rows) // BLK
                at = 2 + q_block * mask_shape[1] + k_block
                if b:
                    at += mask_shape[0] * mask_shape[1]
                hidden = jnp.where(place_ref[at] == 1, 0.0, -jnp.inf)
                line = jnp.where(piece_of_lane == j, hidden, line)
            lines.append(jnp.broadcast_to(line, (rows, keys)))
        bias = jnp.concatenate(lines, axis=0)
        stats = jnp.zeros((group * rows, LANES), jnp.float32)
        for h in range(heads):
            columns = slice(h * HD, (h + 1) * HD)
            q = jnp.concatenate([q_refs[i][:, columns] for i in chosen], axis=0)
            k = jnp.concatenate([r[:rows, columns] for r in kv_refs], axis=0)
            v = jnp.concatenate([r[rows : 2 * rows, columns] for r in kv_refs], axis=0)
            scores = lax.dot_general(
                q, k, (((1,), (1,)), ((), ())), preferred_element_type=jnp.float32
            )
            scores = scores * scale + bias
            top_score = jnp.max(scores, axis=1, keepdims=True)
            weights = jnp.exp(scores - top_score)
            total = jnp.sum(weights, axis=1, keepdims=True)
            summed = jnp.dot(weights.astype(jnp.bfloat16), v, preferred_element_type=jnp.float32)
            mean = summed * (SPAN / total)
            for n, i in enumerate(chosen):
                out_refs[i][:, columns] = mean[n * rows : (n + 1) * rows]
            for n, piece in enumerate(split3(top_score) + split3(total)):
                stats = jnp.where(lane == h * 2 * PARTS + n, piece, stats)
        for n, i in enumerate(chosen):
            out_refs[i][:, width:] = stats[n * rows : (n + 1) * rows]


def attend(place, mask_shape, top, q_parts, kv_parts):
    q_masks, k_masks = tuple(q_parts), tuple(kv_parts)
    rows, width = q_parts[0].shape
    smem = pl.BlockSpec(memory_space=pltpu.SMEM)
    vmem = pl.BlockSpec(memory_space=pltpu.VMEM)
    arrays = [*q_parts.values(), *kv_parts.values()]
    outs = pl.pallas_call(
        functools.partial(attend_kernel, q_masks, k_masks, top, mask_shape),
        out_shape=[jax.ShapeDtypeStruct((rows, width + LANES), jnp.float32)] * len(q_masks),
        in_specs=[smem] + [vmem] * len(arrays),
        out_specs=[vmem] * len(q_masks),
        compiler_params=pltpu.CompilerParams(vmem_limit_bytes=24 * 2**20),
    )(place, *arrays)
    return dict(zip(q_masks, outs))


def project_kernel(n_parts, w_ids, n_col, depth, where_ref, *refs):
    part_refs = refs[:n_parts]
    w_refs = refs[n_parts : n_parts + len(w_ids)]
    residual_ref, out_ref, whole_ref = refs[n_parts + len(w_ids) :]
    rows, width = out_ref.shape[0], whole_ref.shape[1]
    my_row, my_col = where_ref[0], where_ref[1]
    for ids, ref in zip(w_ids, w_refs):
        first = ref.shape[0] - len(ids) * depth
        for n, (a, b) in enumerate(ids):
            place = ((my_row ^ a) * n_col + (my_col ^ b)) * depth
            piece = ref[first + n * depth : first + (n + 1) * depth, :]
            whole_ref[pl.ds(pl.multiple_of(place, 16), depth), :] = piece
    source = lax.broadcasted_iota(jnp.int32, (LANES, 2 * width), 0) // PARTS
    target = lax.broadcasted_iota(jnp.int32, (LANES, 2 * width), 1)
    target = target % width // HD * 2 + target // width
    spread = (source == target).astype(jnp.bfloat16)
    tops, totals = [], []
    for ref in part_refs:
        stats = jnp.dot(ref[:, width:].astype(jnp.bfloat16), spread, preferred_element_type=jnp.float32)
        tops.append(stats[:, :width])
        totals.append(stats[:, width:])
    top = functools.reduce(jnp.maximum, tops)
    shares = [jnp.exp(t - top) * n for t, n in zip(tops, totals)]
    denom = functools.reduce(jnp.add, shares)
    numer = functools.reduce(jnp.add, [ref[:, :width] * s for ref, s in zip(part_refs, shares)])
    attended = (numer / (denom * SPAN)).astype(jnp.bfloat16)
    features = out_ref.shape[1]
    step = features // 4 if features % (4 * LANES) == 0 else features
    for at in range(0, features, step):
        here = slice(at, at + step)
        product = lax.dot_general(
            attended, whole_ref[here, :], (((1,), (1,)), ((), ())), preferred_element_type=jnp.float32
        )
        out_ref[:, here] = (product + residual_ref[:, here].astype(jnp.float32)).astype(out_ref.dtype)


def project(where, parts, w_parts, residual, n_col, depth):
    w_ids = [ids for _, ids in w_parts]
    rows, features = residual.shape
    width = w_parts[0][0].shape[1]
    smem = pl.BlockSpec(memory_space=pltpu.SMEM)
    vmem = pl.BlockSpec(memory_space=pltpu.VMEM)
    arrays = [*parts.values(), *(x for x, _ in w_parts), residual]
    return pl.pallas_call(
        functools.partial(project_kernel, len(parts), w_ids, n_col, depth),
        out_shape=jax.ShapeDtypeStruct((rows, features), residual.dtype),
        in_specs=[smem] + [vmem] * len(arrays),
        out_specs=vmem,
        scratch_shapes=[pltpu.VMEM((features, width), jnp.bfloat16)],
        compiler_params=pltpu.CompilerParams(vmem_limit_bytes=24 * 2**20),
    )(where, *arrays)


def local(queries, keys, values, block_mask, out_weight, residual):
    n_row, n_col = lax.axis_size("row"), lax.axis_size("col")
    top = n_col // 2
    near = range(1, max(top, 1))
    chips = range(2, n_row, 2)
    rows, depth = queries.shape[0], out_weight.shape[1]
    ride = depth % 16 == 0
    where = jnp.stack([lax.axis_index("row"), lax.axis_index("col")]).astype(jnp.int32)
    weight = out_weight.T

    pack = jnp.concatenate([keys, values, weight] if ride else [keys, values])
    kv_parts = {(0, 0): pack}
    if top:
        far_k, far_v = swap(keys, "col", top), swap(values, "col", top)
        far_mask = swap(block_mask, "col", top)
    q_parts = {0: queries}
    for m in near:
        q_parts[m] = swap(queries, "col", m)
    for a in chips:
        kv_parts[a, 0] = swap(pack, "row", a)
    for a in (0, *chips):
        kv_parts[a | 1, 0] = swap(kv_parts[a, 0], "row", 1)
    gate = tuple(q_parts[m] for m in near) + ((far_mask,) if top else ())
    masks = [where, block_mask.reshape(-1)]
    if top:
        kv_parts[0, top] = jnp.concatenate([after(far_k, *gate), far_v])
        for a in chips:
            kv_parts[a, top] = swap(kv_parts[0, top], "row", a)
        for a in (0, *chips):
            kv_parts[a | 1, top] = swap(kv_parts[a, top], "row", 1)
        masks.append(far_mask.reshape(-1))
    place = jnp.concatenate(masks)
    partial = attend(place, block_mask.shape, top, q_parts, kv_parts)
    parts = {0: partial[0]}
    for m in near:
        parts[m] = swap(partial[m].astype(jnp.float16), "col", m).astype(jnp.float32)

    if not ride:
        gathered = lax.all_gather(weight, ("row", "col"), axis=0, tiled=True)
        return project(jnp.zeros_like(where), parts, [(gathered, [(0, 0)])], residual, 1, gathered.shape[0])
    w_parts = [(kv_parts[a, 0], [(a, 0)]) for a in range(n_row)]
    received = tuple(parts[m] for m in near)
    mine = [(weight, 0)]
    bit = top
    while bit:
        mine += [(swap(after(x, kv_parts[1, top]) if m else x, "col", bit), m | bit) for x, m in mine]
        bit //= 2
    for n, batch in enumerate((mine[1:-1], mine[-1:])):
        if not batch:
            continue
        batch = [(after(x, kv_parts[1, top]), m) for x, m in batch]
        block = jnp.concatenate([x for x, _ in batch]) if len(batch) > 1 else batch[0][0]
        cols = [m for _, m in batch]
        if n:
            block = after(block, partial[0])
        held = {0: block}
        for a in chips:
            held[a] = swap(block, "row", a)
        for a in (0, *chips):
            held[a | 1] = swap(after(held[a], *received), "row", 1)
        w_parts += [(x, [(a, m) for m in cols]) for a, x in held.items()]
    return project(where, parts, w_parts, residual, n_col, depth)


def solution(mesh):
    placed = (
        P(("groups", "row", "col"), None),
        P(("groups", "col", "row"), None),
        P(("groups", "col", "row"), None),
        P(("groups", "row"), "col"),
        P(None, ("row", "col")),
        P(("groups", "row", "col"), None),
    )
    return jax.shard_map(
        local,
        mesh=mesh,
        in_specs=placed,
        out_specs=P(("groups", "row", "col"), None),
        check_vma=False,
    )
```

time: 45.2 us -> 34 us (0.75)
  the two profiles are of different devices: /device:TPU:17 before, /device:TPU:0 now
where the time goes in v2:
time: 34 us; the launch traced here: 33.8 us
  starting transfers between devices  18.2 us (54%)
  waiting for transfers between devices  10.3 us (30%)
  Pallas kernels  3.83 us (11%)
  other arithmetic  1.13 us (3%)
    ppermute x20, starting transfers between devices, swap(): lax.ppermute(x, axis, [(i, i ^ mask) for i in range(lax.axis_size(axis))])  18.2 us
    ppermute x20, waiting for transfers between devices, swap(): lax.ppermute(x, axis, [(i, i ^ mask) for i in range(lax.axis_size(axis))])  10.3 us
    pallas_call x1, Pallas kernels, project(): pl.pallas_call(functools.partial(project_kernel, len(parts), w_ids, n_col...  2.32 us
    pallas_call x1, Pallas kernels, attend(): pl.pallas_call(functools.partial(attend_kernel, q_masks, k_masks, top, ma...  1.51 us
    concatenate x1, other arithmetic, local(): pack = jnp.concatenate([keys, values, weight] if ride else [keys, values])  0.96 us
  transfers between devices with their start and end apart: 20, of which 9 were waited for; matrix products, arithmetic and copies ran while one was open for 4% of the time, Pallas kernels for 4%

profile of v2, /device:TPU:0, one launch (start us, length us, event | category | flops | bytes accessed | tf_op | source)
XLA Modules:
  0.0 33.8 jit_solution(16428951460196470608)
XLA Ops:
  0.0 4.0 %collective-permute-start = (s32[2,2]{1,0:T(2,128)}, s32[2,2]{1,0:T(2,128)S(1)}, u32[]{:S(2)}, u32[]{:S(2)}) collective-permute-start(s32[2,2]{1,0:T(2,128)} %param.9), channel_id=1, source_target_pairs={{0,2},{1,3},{2,0},{3,1},{4,6},{5,7},{6,4},{7,5},{8,10},{9,11},{10,... | collective-permute-start | bytes 56 | tf_op jit(solution)/shard_map/ppermute | solution.py:19
  4.0 1.6 %collective-permute-start.1 = (bf16[64,384]{1,0:T(8,128)(2,1)}, bf16[64,384]{1,0:T(8,128)(2,1)S(1)}, u32[]{:S(2)}, u32[]{:S(2)}) collective-permute-start(bf16[64,384]{1,0:T(8,128)(2,1)} %refs_0_.1), channel_id=1, source_target_pairs={{0,1},{1,0},{2,3},{3,2},{4,5},{5,4},{6,7},{7,6},{8,9},{9,8},{10,11... | collective-permute-start | bytes 147464 | tf_op jit(solution)/shard_map/ppermute | solution.py:19
  5.6 0.3 collective-permute-start.5
  6.0 2.6 %collective-permute-start.6 = (bf16[64,384]{1,0:T(8,128)(2,1)}, bf16[64,384]{1,0:T(8,128)(2,1)S(1)}, u32[]{:S(2)}, u32[]{:S(2)}) collective-permute-start(bf16[64,384]{1,0:T(8,128)(2,1)} %param.8), channel_id=1, source_target_pairs={{0,2},{1,3},{2,0},{3,1},{4,6},{5,7},{6,4},{7,5},{8,10},{9,11},{10,... | collective-permute-start | bytes 147464 | tf_op jit(solution)/shard_map/ppermute | solution.py:19
  8.5 0.4 %collective-permute-start.12 = (bf16[160,384]{1,0:T(8,128)(2,1)}, bf16[160,384]{1,0:T(8,128)(2,1)S(1)}, u32[]{:S(2)}, u32[]{:S(2)}) collective-permute-start(bf16[160,384]{1,0:T(8,128)(2,1)} %bitcast.3), channel_id=1, source_target_pairs={{0,1},{1,0},{2,3},{3,2},{4,5},{5,4},{6,7},{7,6},{8,9},{9,8},{10,11... | collective-permute-start | bytes 368648 | tf_op jit(solution)/shard_map/ppermute | solution.py:19
  9.0 1.0 %pad_maximum_fusion.refs_2_ = bf16[288,384]{1,0:T(8,128)(2,1)S(1)} fusion(bf16[160,384]{1,0:T(8,128)(2,1)} %bitcast.4, bf16[64,384]{1,0:T(8,128)(2,1)} %param.8, bf16[64,384]{1,0:T(8,128)(2,1)} %param.7), kind=kLoop, calls=%fused_computation | loop fusion | flops 663552 | bytes 442368 | tf_op jit(solution)/shard_map/concatenate | solution.py:161
  10.1 1.8 %collective-permute-start.2 = (bf16[288,384]{1,0:T(8,128)(2,1)S(1)}, bf16[288,384]{1,0:T(8,128)(2,1)S(1)}, u32[]{:S(2)}, u32[]{:S(2)}) collective-permute-start(bf16[288,384]{1,0:T(8,128)(2,1)S(1)} %pad_maximum_fusion.refs_2_), channel_id=1, source_target_pairs={{0,8},{4,12},{8,0},{12,4},{1,9},{5,13},{9,1},{13,5},{2,10},{6,14},... | collective-permute-start | bytes 663560 | tf_op jit(solution)/shard_map/ppermute | solution.py:19
  12.1 1.3 %collective-permute-done.6 = bf16[64,384]{1,0:T(8,128)(2,1)S(1)} collective-permute-done((bf16[64,384]{1,0:T(8,128)(2,1)}, bf16[64,384]{1,0:T(8,128)(2,1)S(1)}, u32[]{:S(2)}, u32[]{:S(2)}) %collective-permute-start.6) | collective-permute-done | bytes 49184 | tf_op jit(solution)/shard_map/ppermute | solution.py:19
  13.4 0.5 %collective-permute-start.3 = (bf16[288,384]{1,0:T(8,128)(2,1)S(1)}, bf16[288,384]{1,0:T(8,128)(2,1)S(1)}, u32[]{:S(2)}, u32[]{:S(2)}) collective-permute-start(bf16[288,384]{1,0:T(8,128)(2,1)S(1)} %pad_maximum_fusion.refs_2_), channel_id=1, source_target_pairs={{0,4},{4,0},{8,12},{12,8},{1,5},{5,1},{9,13},{13,9},{2,6},{6,2},{1... | collective-permute-start | bytes 663560 | tf_op jit(solution)/shard_map/ppermute | solution.py:19
  13.9 2.0 %collective-permute-done.12 = bf16[160,384]{1,0:T(8,128)(2,1)S(1)} collective-permute-done((bf16[160,384]{1,0:T(8,128)(2,1)}, bf16[160,384]{1,0:T(8,128)(2,1)S(1)}, u32[]{:S(2)}, u32[]{:S(2)}) %collective-permute-start.12) | collective-permute-done | bytes 122912 | tf_op jit(solution)/shard_map/ppermute | solution.py:19
  15.9 1.5 %collective-permute-start.7 = (bf16[128,384]{1,0:T(8,128)(2,1)S(1)}, bf16[128,384]{1,0:T(8,128)(2,1)S(1)}, u32[]{:S(2)}, u32[]{:S(2)}) collective-permute-start(bf16[128,384]{1,0:T(8,128)(2,1)S(1)} %constant_dynamic-update-slice_fusion.refs_6_), channel_id=1, source_target_pairs={{0,8},{4,12},{8,0},{12,4},{1,9},{5,13},{9,1},{13,5},{2,10},{6,14},... | collective-permute-start | bytes 294920 | tf_op jit(solution)/shard_map/ppermute | solution.py:19
  17.4 0.6 %collective-permute-done.11 = bf16[160,384]{1,0:T(8,128)(2,1)S(1)} collective-permute-done((bf16[160,384]{1,0:T(8,128)(2,1)S(1)}, bf16[160,384]{1,0:T(8,128)(2,1)S(1)}, u32[]{:S(2)}, u32[]{:S(2)}) %collective-permute-start.11) | collective-permute-done | bytes 122912 | tf_op jit(solution)/shard_map/ppermute | solution.py:19
  18.1 1.6 %collective-permute-start.13 = (bf16[320,384]{1,0:T(8,128)(2,1)S(1)}, bf16[320,384]{1,0:T(8,128)(2,1)S(1)}, u32[]{:S(2)}, u32[]{:S(2)}) collective-permute-start(bf16[320,384]{1,0:T(8,128)(2,1)S(1)} %constant_dynamic-update-slice_fusion.2.refs_6_), channel_id=1, source_target_pairs={{0,8},{4,12},{8,0},{12,4},{1,9},{5,13},{9,1},{13,5},{2,10},{6,14},... | collective-permute-start | bytes 737288 | tf_op jit(solution)/shard_map/ppermute | solution.py:19
  19.8 0.9 %collective-permute-start.16 = (bf16[160,384]{1,0:T(8,128)(2,1)S(1)}, bf16[160,384]{1,0:T(8,128)(2,1)S(1)}, u32[]{:S(2)}, u32[]{:S(2)}) collective-permute-start(bf16[160,384]{1,0:T(8,128)(2,1)S(1)} %collective-permute-done.11), channel_id=1, source_target_pairs={{0,1},{1,0},{2,3},{3,2},{4,5},{5,4},{6,7},{7,6},{8,9},{9,8},{10,11... | collective-permute-start | bytes 368648 | tf_op jit(solution)/shard_map/ppermute | solution.py:19
  20.8 1.2 %collective-permute-done.9.refs_9_ = bf16[128,384]{1,0:T(8,128)(2,1)S(1)} collective-permute-done((bf16[128,384]{1,0:T(8,128)(2,1)S(1)}, bf16[128,384]{1,0:T(8,128)(2,1)S(1)}, u32[]{:S(2)}, u32[]{:S(2)}) %collective-permute-start.9) | collective-permute-done | bytes 98336 | tf_op jit(solution)/shard_map/ppermute | solution.py:19
  22.0 1.5 %shard_map.64 = (f32[64,512]{1,0:T(8,128)S(1)}, f32[64,512]{1,0:T(8,128)S(1)}) custom-call(s32[10]{0:T(128)S(1)} %pad_add_fusion.1.place_ref, bf16[64,384]{1,0:T(8,128)(2,1)S(1)} %copy-done.1, bf16[64,384]{1,0:T(8,128)(2,1)S(1)} %collective-permute-done.1.refs_1_, bf16[288,384]{1,0:T(8,128)(2,1)S(1)} %pad_maximum_fusion.refs_2_, ...), custom_call_target="tpu_custom_call" | custom-call | tf_op jit(solution)/shard_map/pallas_call | solution.py:88
  23.6 1.2 %collective-permute-start.10 = (f16[64,512]{1,0:T(8,128)(2,1)S(1)}, f16[64,512]{1,0:T(8,128)(2,1)S(1)}, u32[]{:S(2)}, u32[]{:S(2)}) collective-permute-start(f16[64,512]{1,0:T(8,128)(2,1)S(1)} %convert_element_type.6), channel_id=1, source_target_pairs={{0,1},{1,0},{2,3},{3,2},{4,5},{5,4},{6,7},{7,6},{8,9},{9,8},{10,11... | collective-permute-start | bytes 196616 | tf_op jit(solution)/shard_map/ppermute | solution.py:19
  24.8 0.5 %collective-permute-done.16.refs_10_ = bf16[160,384]{1,0:T(8,128)(2,1)S(1)} collective-permute-done((bf16[160,384]{1,0:T(8,128)(2,1)S(1)}, bf16[160,384]{1,0:T(8,128)(2,1)S(1)}, u32[]{:S(2)}, u32[]{:S(2)}) %collective-permute-start.16) | collective-permute-done | bytes 122912 | tf_op jit(solution)/shard_map/ppermute | solution.py:19
  25.3 0.9 %collective-permute-start.17 = (bf16[160,384]{1,0:T(8,128)(2,1)S(1)}, bf16[160,384]{1,0:T(8,128)(2,1)S(1)}, u32[]{:S(2)}, u32[]{:S(2)}) collective-permute-start(bf16[160,384]{1,0:T(8,128)(2,1)S(1)} %collective-permute-done.16.refs_10_), channel_id=1, source_target_pairs={{0,8},{4,12},{8,0},{12,4},{1,9},{5,13},{9,1},{13,5},{2,10},{6,14},... | collective-permute-start | bytes 368648 | tf_op jit(solution)/shard_map/ppermute | solution.py:19
  26.2 1.7 %collective-permute-done.10 = f16[64,512]{1,0:T(8,128)(2,1)S(1)} collective-permute-done((f16[64,512]{1,0:T(8,128)(2,1)S(1)}, f16[64,512]{1,0:T(8,128)(2,1)S(1)}, u32[]{:S(2)}, u32[]{:S(2)}) %collective-permute-start.10) | collective-permute-done | bytes 65568 | tf_op jit(solution)/shard_map/ppermute | solution.py:19
  28.0 0.5 %collective-permute-start.15 = (bf16[320,384]{1,0:T(8,128)(2,1)S(1)}, bf16[320,384]{1,0:T(8,128)(2,1)S(1)}, u32[]{:S(2)}, u32[]{:S(2)}) collective-permute-start(bf16[320,384]{1,0:T(8,128)(2,1)S(1)} %collective-permute-done.13.refs_7_), channel_id=1, source_target_pairs={{0,4},{4,0},{8,12},{12,8},{1,5},{5,1},{9,13},{13,9},{2,6},{6,2},{1... | collective-permute-start | bytes 737288 | tf_op jit(solution)/shard_map/ppermute | solution.py:19
  28.6 1.6 %collective-permute-done.17.refs_11_ = bf16[160,384]{1,0:T(8,128)(2,1)S(1)} collective-permute-done((bf16[160,384]{1,0:T(8,128)(2,1)S(1)}, bf16[160,384]{1,0:T(8,128)(2,1)S(1)}, u32[]{:S(2)}, u32[]{:S(2)}) %collective-permute-start.17) | collective-permute-done | bytes 122912 | tf_op jit(solution)/shard_map/ppermute | solution.py:19
  30.2 1.3 %collective-permute-done.19.refs_13_ = bf16[160,384]{1,0:T(8,128)(2,1)S(1)} collective-permute-done((bf16[160,384]{1,0:T(8,128)(2,1)S(1)}, bf16[160,384]{1,0:T(8,128)(2,1)S(1)}, u32[]{:S(2)}, u32[]{:S(2)}) %collective-permute-start.19) | collective-permute-done | bytes 122912 | tf_op jit(solution)/shard_map/ppermute | solution.py:19
  31.5 2.3 %shard_map.65 = bf16[64,2560]{1,0:T(8,128)(2,1)} custom-call(s32[2]{0:T(128)S(1)} %pad_add_fusion.where_ref, f32[64,512]{1,0:T(8,128)S(1)} %get-tuple-element.17.refs_0_, f32[64,512]{1,0:T(8,128)S(1)} %convert_element_type.7.refs_1_, bf16[288,384]{1,0:T(8,128)(2,1)S(1)} %pad_maximum_fusion.refs_2_, ...), custom_call_target="tpu_custom_call" | custom-call | tf_op jit(solution)/shard_map/pallas_call | solution.py:141
  (37 shorter events, 1.0 us)
Async XLA Ops:
  0.0 10.0 %collective-permute-start = (s32[2,2]{1,0:T(2,128)}, s32[2,2]{1,0:T(2,128)S(1)}, u32[]{:S(2)}, u32[]{:S(2)}) collective-permute-start(s32[2,2]{1,0:T(2,128)} %param.9), channel_id=1, source_target_pairs={{0,2},{1,3},{2,0},{3,1},{4,6},{5,7},{6,4},{7,5},{8,10},{9,11},{10,... | collective-permute-start | bytes 56 | tf_op jit(solution)/shard_map/ppermute | solution.py:19
  4.0 6.0 %collective-permute-start.1 = (bf16[64,384]{1,0:T(8,128)(2,1)}, bf16[64,384]{1,0:T(8,128)(2,1)S(1)}, u32[]{:S(2)}, u32[]{:S(2)}) collective-permute-start(bf16[64,384]{1,0:T(8,128)(2,1)} %refs_0_.1), channel_id=1, source_target_pairs={{0,1},{1,0},{2,3},{3,2},{4,5},{5,4},{6,7},{7,6},{8,9},{9,8},{10,11... | collective-permute-start | bytes 147464 | tf_op jit(solution)/shard_map/ppermute | solution.py:19
  5.6 6.4 %collective-permute-start.5 = (bf16[64,384]{1,0:T(8,128)(2,1)}, bf16[64,384]{1,0:T(8,128)(2,1)S(1)}, u32[]{:S(2)}, u32[]{:S(2)}) collective-permute-start(bf16[64,384]{1,0:T(8,128)(2,1)} %param.7), channel_id=1, source_target_pairs={{0,2},{1,3},{2,0},{3,1},{4,6},{5,7},{6,4},{7,5},{8,10},{9,11},{10,... | collective-permute-start | bytes 147464 | tf_op jit(solution)/shard_map/ppermute | solution.py:19
  6.0 7.4 %collective-permute-start.6 = (bf16[64,384]{1,0:T(8,128)(2,1)}, bf16[64,384]{1,0:T(8,128)(2,1)S(1)}, u32[]{:S(2)}, u32[]{:S(2)}) collective-permute-start(bf16[64,384]{1,0:T(8,128)(2,1)} %param.8), channel_id=1, source_target_pairs={{0,2},{1,3},{2,0},{3,1},{4,6},{5,7},{6,4},{7,5},{8,10},{9,11},{10,... | collective-permute-start | bytes 147464 | tf_op jit(solution)/shard_map/ppermute | solution.py:19
  8.5 1.4 %copy-start.2 = (bf16[384,160]{0,1:T(8,128)(2,1)S(1)}, bf16[384,160]{0,1:T(8,128)(2,1)}, u32[]{:S(2)}) copy-start(bf16[384,160]{0,1:T(8,128)(2,1)} %param.10) | copy-start | bytes 368644
  8.5 7.3 %collective-permute-start.12 = (bf16[160,384]{1,0:T(8,128)(2,1)}, bf16[160,384]{1,0:T(8,128)(2,1)S(1)}, u32[]{:S(2)}, u32[]{:S(2)}) collective-permute-start(bf16[160,384]{1,0:T(8,128)(2,1)} %bitcast.3), channel_id=1, source_target_pairs={{0,1},{1,0},{2,3},{3,2},{4,5},{5,4},{6,7},{7,6},{8,9},{9,8},{10,11... | collective-permute-start | bytes 368648 | tf_op jit(solution)/shard_map/ppermute | solution.py:19
  10.0 8.0 %collective-permute-start.11 = (bf16[160,384]{1,0:T(8,128)(2,1)S(1)}, bf16[160,384]{1,0:T(8,128)(2,1)S(1)}, u32[]{:S(2)}, u32[]{:S(2)}) collective-permute-start(bf16[160,384]{1,0:T(8,128)(2,1)S(1)} %bitcast.5), channel_id=1, source_target_pairs={{0,2},{1,3},{2,0},{3,1},{4,6},{5,7},{6,4},{7,5},{8,10},{9,11},{10,... | collective-permute-start | bytes 368648 | tf_op jit(solution)/shard_map/ppermute | solution.py:19
  10.1 7.9 %collective-permute-start.2 = (bf16[288,384]{1,0:T(8,128)(2,1)S(1)}, bf16[288,384]{1,0:T(8,128)(2,1)S(1)}, u32[]{:S(2)}, u32[]{:S(2)}) collective-permute-start(bf16[288,384]{1,0:T(8,128)(2,1)S(1)} %pad_maximum_fusion.refs_2_), channel_id=1, source_target_pairs={{0,8},{4,12},{8,0},{12,4},{1,9},{5,13},{9,1},{13,5},{2,10},{6,14},... | collective-permute-start | bytes 663560 | tf_op jit(solution)/shard_map/ppermute | solution.py:19
  13.3 4.0 %collective-permute-start.8 = (bf16[128,384]{1,0:T(8,128)(2,1)S(1)}, bf16[128,384]{1,0:T(8,128)(2,1)S(1)}, u32[]{:S(2)}, u32[]{:S(2)}) collective-permute-start(bf16[128,384]{1,0:T(8,128)(2,1)S(1)} %constant_dynamic-update-slice_fusion.refs_6_), channel_id=1, source_target_pairs={{0,4},{4,0},{8,12},{12,8},{1,5},{5,1},{9,13},{13,9},{2,6},{6,2},{1... | collective-permute-start | bytes 294920 | tf_op jit(solution)/shard_map/ppermute | solution.py:19
  13.4 7.4 %collective-permute-start.3 = (bf16[288,384]{1,0:T(8,128)(2,1)S(1)}, bf16[288,384]{1,0:T(8,128)(2,1)S(1)}, u32[]{:S(2)}, u32[]{:S(2)}) collective-permute-start(bf16[288,384]{1,0:T(8,128)(2,1)S(1)} %pad_maximum_fusion.refs_2_), channel_id=1, source_target_pairs={{0,4},{4,0},{8,12},{12,8},{1,5},{5,1},{9,13},{13,9},{2,6},{6,2},{1... | collective-permute-start | bytes 663560 | tf_op jit(solution)/shard_map/ppermute | solution.py:19
  15.9 4.8 %collective-permute-start.7 = (bf16[128,384]{1,0:T(8,128)(2,1)S(1)}, bf16[128,384]{1,0:T(8,128)(2,1)S(1)}, u32[]{:S(2)}, u32[]{:S(2)}) collective-permute-start(bf16[128,384]{1,0:T(8,128)(2,1)S(1)} %constant_dynamic-update-slice_fusion.refs_6_), channel_id=1, source_target_pairs={{0,8},{4,12},{8,0},{12,4},{1,9},{5,13},{9,1},{13,5},{2,10},{6,14},... | collective-permute-start | bytes 294920 | tf_op jit(solution)/shard_map/ppermute | solution.py:19
  18.0 4.0 %collective-permute-start.4 = (bf16[288,384]{1,0:T(8,128)(2,1)S(1)}, bf16[288,384]{1,0:T(8,128)(2,1)S(1)}, u32[]{:S(2)}, u32[]{:S(2)}) collective-permute-start(bf16[288,384]{1,0:T(8,128)(2,1)S(1)} %collective-permute-done.2.refs_3_.refs_4_), channel_id=1, source_target_pairs={{0,4},{4,0},{8,12},{12,8},{1,5},{5,1},{9,13},{13,9},{2,6},{6,2},{1... | collective-permute-start | bytes 663560 | tf_op jit(solution)/shard_map/ppermute | solution.py:19
  18.1 4.0 %copy-start.1 = (bf16[64,384]{1,0:T(8,128)(2,1)S(1)}, bf16[64,384]{1,0:T(8,128)(2,1)}, u32[]{:S(2)}) copy-start(bf16[64,384]{1,0:T(8,128)(2,1)} %refs_0_.1) | copy-start | bytes 147460
  18.1 1.6 %copy-start.3 = (s32[2,2]{1,0:T(2,128)S(1)}, s32[2,2]{1,0:T(2,128)}, u32[]{:S(2)}) copy-start(s32[2,2]{1,0:T(2,128)} %param.9) | copy-start | bytes 52
  18.1 9.9 %collective-permute-start.13 = (bf16[320,384]{1,0:T(8,128)(2,1)S(1)}, bf16[320,384]{1,0:T(8,128)(2,1)S(1)}, u32[]{:S(2)}, u32[]{:S(2)}) collective-permute-start(bf16[320,384]{1,0:T(8,128)(2,1)S(1)} %constant_dynamic-update-slice_fusion.2.refs_6_), channel_id=1, source_target_pairs={{0,8},{4,12},{8,0},{12,4},{1,9},{5,13},{9,1},{13,5},{2,10},{6,14},... | collective-permute-start | bytes 737288 | tf_op jit(solution)/shard_map/ppermute | solution.py:19
  19.8 5.4 %collective-permute-start.16 = (bf16[160,384]{1,0:T(8,128)(2,1)S(1)}, bf16[160,384]{1,0:T(8,128)(2,1)S(1)}, u32[]{:S(2)}, u32[]{:S(2)}) collective-permute-start(bf16[160,384]{1,0:T(8,128)(2,1)S(1)} %collective-permute-done.11), channel_id=1, source_target_pairs={{0,1},{1,0},{2,3},{3,2},{4,5},{5,4},{6,7},{7,6},{8,9},{9,8},{10,11... | collective-permute-start | bytes 368648 | tf_op jit(solution)/shard_map/ppermute | solution.py:19
  20.7 1.3 %collective-permute-start.9 = (bf16[128,384]{1,0:T(8,128)(2,1)S(1)}, bf16[128,384]{1,0:T(8,128)(2,1)S(1)}, u32[]{:S(2)}, u32[]{:S(2)}) collective-permute-start(bf16[128,384]{1,0:T(8,128)(2,1)S(1)} %collective-permute-done.7.refs_7_), channel_id=1, source_target_pairs={{0,4},{4,0},{8,12},{12,8},{1,5},{5,1},{9,13},{13,9},{2,6},{6,2},{1... | collective-permute-start | bytes 294920 | tf_op jit(solution)/shard_map/ppermute | solution.py:19
  23.5 8.0 %copy-start = (bf16[64,2560]{1,0:T(8,128)(2,1)S(1)}, bf16[64,2560]{1,0:T(8,128)(2,1)}, u32[]{:S(2)}) copy-start(bf16[64,2560]{1,0:T(8,128)(2,1)} %refs_14_.1) | copy-start | bytes 983044
  23.6 4.3 %collective-permute-start.10 = (f16[64,512]{1,0:T(8,128)(2,1)S(1)}, f16[64,512]{1,0:T(8,128)(2,1)S(1)}, u32[]{:S(2)}, u32[]{:S(2)}) collective-permute-start(f16[64,512]{1,0:T(8,128)(2,1)S(1)} %convert_element_type.6), channel_id=1, source_target_pairs={{0,1},{1,0},{2,3},{3,2},{4,5},{5,4},{6,7},{7,6},{8,9},{9,8},{10,11... | collective-permute-start | bytes 196616 | tf_op jit(solution)/shard_map/ppermute | solution.py:19
  25.3 4.9 %collective-permute-start.17 = (bf16[160,384]{1,0:T(8,128)(2,1)S(1)}, bf16[160,384]{1,0:T(8,128)(2,1)S(1)}, u32[]{:S(2)}, u32[]{:S(2)}) collective-permute-start(bf16[160,384]{1,0:T(8,128)(2,1)S(1)} %collective-permute-done.16.refs_10_), channel_id=1, source_target_pairs={{0,8},{4,12},{8,0},{12,4},{1,9},{5,13},{9,1},{13,5},{2,10},{6,14},... | collective-permute-start | bytes 368648 | tf_op jit(solution)/shard_map/ppermute | solution.py:19
  27.9 3.6 %collective-permute-start.14 = (bf16[320,384]{1,0:T(8,128)(2,1)S(1)}, bf16[320,384]{1,0:T(8,128)(2,1)S(1)}, u32[]{:S(2)}, u32[]{:S(2)}) collective-permute-start(bf16[320,384]{1,0:T(8,128)(2,1)S(1)} %constant_dynamic-update-slice_fusion.2.refs_6_), channel_id=1, source_target_pairs={{0,4},{4,0},{8,12},{12,8},{1,5},{5,1},{9,13},{13,9},{2,6},{6,2},{1... | collective-permute-start | bytes 737288 | tf_op jit(solution)/shard_map/ppermute | solution.py:19
  28.0 3.5 %collective-permute-start.15 = (bf16[320,384]{1,0:T(8,128)(2,1)S(1)}, bf16[320,384]{1,0:T(8,128)(2,1)S(1)}, u32[]{:S(2)}, u32[]{:S(2)}) collective-permute-start(bf16[320,384]{1,0:T(8,128)(2,1)S(1)} %collective-permute-done.13.refs_7_), channel_id=1, source_target_pairs={{0,4},{4,0},{8,12},{12,8},{1,5},{5,1},{9,13},{13,9},{2,6},{6,2},{1... | collective-permute-start | bytes 737288 | tf_op jit(solution)/shard_map/ppermute | solution.py:19
  28.5 1.7 %collective-permute-start.18 = (bf16[160,384]{1,0:T(8,128)(2,1)S(1)}, bf16[160,384]{1,0:T(8,128)(2,1)S(1)}, u32[]{:S(2)}, u32[]{:S(2)}) collective-permute-start(bf16[160,384]{1,0:T(8,128)(2,1)S(1)} %collective-permute-done.16.refs_10_), channel_id=1, source_target_pairs={{0,4},{4,0},{8,12},{12,8},{1,5},{5,1},{9,13},{13,9},{2,6},{6,2},{1... | collective-permute-start | bytes 368648 | tf_op jit(solution)/shard_map/ppermute | solution.py:19
  30.1 1.3 %collective-permute-start.19 = (bf16[160,384]{1,0:T(8,128)(2,1)S(1)}, bf16[160,384]{1,0:T(8,128)(2,1)S(1)}, u32[]{:S(2)}, u32[]{:S(2)}) collective-permute-start(bf16[160,384]{1,0:T(8,128)(2,1)S(1)} %collective-permute-done.17.refs_11_), channel_id=1, source_target_pairs={{0,4},{4,0},{8,12},{12,8},{1,5},{5,1},{9,13},{13,9},{2,6},{6,2},{1... | collective-permute-start | bytes 368648 | tf_op jit(solution)/shard_map/ppermute | solution.py:19

commit v3 on v2

v3 whole, which is shorter than its diff:
```python
import functools
import math

import jax
import jax.numpy as jnp
from jax import lax
from jax.experimental import pallas as pl
from jax.experimental.pallas import tpu as pltpu
from jax.sharding import PartitionSpec as P

HD = 128
BLK = 128
LANES = 128
PARTS = 3
SPAN = 8192.0


def swap(x, axis, mask):
    return lax.ppermute(x, axis, [(i, i ^ mask) for i in range(lax.axis_size(axis))])


def after(x, *others):
    return lax.optimization_barrier((x, *others))[0]


def split3(x):
    high = x.astype(jnp.bfloat16).astype(jnp.float32)
    rest = x - high
    middle = rest.astype(jnp.bfloat16).astype(jnp.float32)
    return (high, middle, rest - middle)


def attend_kernel(q_masks, k_masks, per_tile, mask_shape, place_ref, *refs):
    nq, nk = len(q_masks), len(k_masks)
    q_refs, kv_refs, out_ref = refs[:nq], refs[nq : nq + nk], refs[-1]
    rows, width = q_refs[0].shape
    heads = width // HD
    scale = 1.0 / math.sqrt(HD)
    my_row, my_col = place_ref[0], place_ref[1]
    keys = nk * rows
    piece_of_lane = lax.broadcasted_iota(jnp.int32, (1, keys), 1) // rows
    group = min(nq, 4)
    lane = lax.broadcasted_iota(jnp.int32, (group * rows, LANES), 1)
    for first in range(0, nq, group):
        chosen = range(first, first + group)
        lines = []
        for i in chosen:
            q_block = ((my_col ^ q_masks[i]) * rows) // BLK
            line = jnp.zeros((1, keys), jnp.float32)
            for j, (a, b) in enumerate(k_masks):
                k_block = ((my_row ^ a) * rows) // BLK
                at = 2 + q_block * mask_shape[1] + k_block
                if b:
                    at += mask_shape[0] * mask_shape[1]
                hidden = jnp.where(place_ref[at] == 1, 0.0, -jnp.inf)
                line = jnp.where(piece_of_lane == j, hidden, line)
            lines.append(jnp.broadcast_to(line, (rows, keys)))
        bias = jnp.concatenate(lines, axis=0)
        stats = jnp.zeros((group * rows, LANES), jnp.float32)
        here = slice(first * rows, (first + group) * rows)
        for h in range(heads):
            columns = slice(h * HD, (h + 1) * HD)
            q = jnp.concatenate([q_refs[i][:rows, columns] for i in chosen], axis=0)
            tops, totals, sums = [], [], []
            for tile in range(0, nk, per_tile):
                refs_here = kv_refs[tile : tile + per_tile]
                k = jnp.concatenate([r[:rows, columns] for r in refs_here], axis=0)
                v = jnp.concatenate([r[rows : 2 * rows, columns] for r in refs_here], axis=0)
                scores = lax.dot_general(
                    q, k, (((1,), (1,)), ((), ())), preferred_element_type=jnp.float32
                )
                scores = scores * scale + bias[:, tile * rows : (tile + per_tile) * rows]
                tops.append(jnp.max(scores, axis=1, keepdims=True))
                weights = jnp.exp(scores - tops[-1])
                totals.append(jnp.sum(weights, axis=1, keepdims=True))
                sums.append(jnp.dot(weights.astype(jnp.bfloat16), v, preferred_element_type=jnp.float32))
            top_score = functools.reduce(jnp.maximum, tops)
            factors = [jnp.exp(t - top_score) for t in tops]
            total = functools.reduce(jnp.add, [f * t for f, t in zip(factors, totals)])
            summed = functools.reduce(jnp.add, [f * t for f, t in zip(factors, sums)])
            out_ref[here, columns] = summed * (SPAN / total)
            for n, piece in enumerate(split3(top_score) + split3(total)):
                stats = jnp.where(lane == h * 2 * PARTS + n, piece, stats)
        out_ref[here, width:] = stats


def attend(place, mask_shape, per_tile, q_parts, kv_parts):
    q_masks, k_masks = tuple(q_parts), tuple(kv_parts)
    rows, width = q_parts[0].shape
    smem = pl.BlockSpec(memory_space=pltpu.SMEM)
    vmem = pl.BlockSpec(memory_space=pltpu.VMEM)
    arrays = [*q_parts.values(), *kv_parts.values()]
    return pl.pallas_call(
        functools.partial(attend_kernel, q_masks, k_masks, per_tile, mask_shape),
        out_shape=jax.ShapeDtypeStruct((len(q_masks) * rows, width + LANES), jnp.float32),
        in_specs=[smem] + [vmem] * len(arrays),
        out_specs=vmem,
        compiler_params=pltpu.CompilerParams(vmem_limit_bytes=24 * 2**20),
    )(place, *arrays)


def merge(parts):
    width = parts[0].shape[1] - LANES
    source = lax.broadcasted_iota(jnp.int32, (LANES, 2 * width), 0) // PARTS
    target = lax.broadcasted_iota(jnp.int32, (LANES, 2 * width), 1)
    target = target % width // HD * 2 + target // width
    spread = (source == target).astype(jnp.bfloat16)
    tops, totals = [], []
    for part in parts:
        stats = jnp.dot(part[:, width:].astype(jnp.bfloat16), spread, preferred_element_type=jnp.float32)
        tops.append(stats[:, :width])
        totals.append(stats[:, width:])
    top = functools.reduce(jnp.maximum, tops)
    shares = [jnp.exp(t - top) * n for t, n in zip(tops, totals)]
    denom = functools.reduce(jnp.add, shares)
    numer = functools.reduce(jnp.add, [part[:, :width] * s for part, s in zip(parts, shares)])
    return (numer / (denom * SPAN)).astype(jnp.bfloat16)


def times(attended, weight):
    return lax.dot_general(attended, weight, (((1,), (1,)), ((), ())), preferred_element_type=jnp.float32)


def project_kernel(n_parts, w_ids, n_col, depth, where_ref, *refs):
    part_refs = refs[:n_parts]
    w_refs = refs[n_parts : n_parts + len(w_ids)]
    residual_ref, out_ref, whole_ref = refs[n_parts + len(w_ids) :]
    rows, features = out_ref.shape
    my_row, my_col = where_ref[0], where_ref[1]
    for ids, ref in zip(w_ids, w_refs):
        first = ref.shape[0] - len(ids) * depth
        for n, (a, b) in enumerate(ids):
            place = ((my_row ^ a) * n_col + (my_col ^ b)) * depth
            whole_ref[pl.ds(pl.multiple_of(place, 16), depth), :] = ref[first + n * depth : first + (n + 1) * depth, :]
    attended = merge([ref[:rows, :] for ref in part_refs])
    step = features // 4 if features % (4 * LANES) == 0 else features
    for at in range(0, features, step):
        here = slice(at, at + step)
        product = times(attended, whole_ref[here, :])
        out_ref[:, here] = (product + residual_ref[:, here].astype(jnp.float32)).astype(out_ref.dtype)


def call(kernel, shapes, where, arrays, scratch=()):
    smem = pl.BlockSpec(memory_space=pltpu.SMEM)
    vmem = pl.BlockSpec(memory_space=pltpu.VMEM)
    return pl.pallas_call(
        kernel,
        out_shape=shapes,
        in_specs=[smem] + [vmem] * len(arrays),
        out_specs=jax.tree.map(lambda _: vmem, shapes),
        scratch_shapes=list(scratch),
        compiler_params=pltpu.CompilerParams(vmem_limit_bytes=24 * 2**20),
    )(where, *arrays)


def local(queries, keys, values, block_mask, out_weight, residual):
    n_row, n_col = lax.axis_size("row"), lax.axis_size("col")
    top = n_col // 2
    near = range(1, max(top, 1))
    chips = range(2, n_row, 2)
    rows, depth = queries.shape[0], out_weight.shape[1]
    ride = depth % 16 == 0
    where = jnp.stack([lax.axis_index("row"), lax.axis_index("col")]).astype(jnp.int32)
    weight = out_weight.T

    pack = jnp.concatenate([keys, values, weight] if ride else [keys, values])
    gate = ()
    if top:
        far_k, far_v = swap(keys, "col", top), swap(values, "col", top)
        far_mask = swap(block_mask, "col", top)
        gate = (far_mask,)
    q_parts = {0: queries}
    for m in near:
        q_parts[m] = swap(queries, "col", m)
        gate += (q_parts[m],)
    kv_parts = {(0, 0): pack}
    for a in chips:
        kv_parts[a, 0] = swap(pack, "row", a)
    for a in (0, *chips):
        kv_parts[a | 1, 0] = swap(kv_parts[a, 0], "row", 1)
    masks = [where, block_mask.reshape(-1)]
    if top:
        kv_parts[0, top] = jnp.concatenate([after(far_k, *gate), far_v])
        for a in chips:
            kv_parts[a, top] = swap(kv_parts[0, top], "row", a)
        for a in (0, *chips):
            kv_parts[a | 1, top] = swap(kv_parts[a, top], "row", 1)
        masks.append(far_mask.reshape(-1))
    partial = attend(jnp.concatenate(masks), block_mask.shape, n_row, q_parts, kv_parts)

    parts = [partial]
    for n, m in enumerate(near, 1):
        sent = partial[n * rows : (n + 1) * rows].astype(jnp.float16)
        parts.append(swap(sent, "col", m).astype(jnp.float32))

    if ride:
        w_parts = [(kv_parts[a, 0], [(a, 0)]) for a in range(n_row)]
        ready = kv_parts[1, top]
        mine = [(weight, 0)]
        bit = top
        while bit:
            mine += [(swap(after(x, ready) if m else x, "col", bit), m | bit) for x, m in mine]
            bit //= 2
        for batch, gates in ((mine[1:-1], (ready,)), (mine[-1:], (ready, partial))):
            if not batch or not batch[0][1]:
                continue
            batch = [(after(x, *gates), m) for x, m in batch]
            block = jnp.concatenate([x for x, _ in batch]) if len(batch) > 1 else batch[0][0]
            held = {0: block}
            for a in chips:
                held[a] = swap(block, "row", a)
            for a in (0, *chips):
                held[a | 1] = swap(after(held[a], *parts[1:]), "row", 1)
            w_parts += [(x, [(a, m) for _, m in batch]) for a, x in held.items()]
    else:
        weight = lax.all_gather(weight, ("row", "col"), axis=0, tiled=True)
        w_parts, depth, n_col, where = [(weight, [(0, 0)])], weight.shape[0], 1, jnp.zeros_like(where)
    w_ids = [ids for _, ids in w_parts]
    arrays = [*parts, *(x for x, _ in w_parts), residual]
    scratch = [pltpu.VMEM((residual.shape[1], queries.shape[1]), jnp.bfloat16)]
    shape = jax.ShapeDtypeStruct(residual.shape, residual.dtype)
    return call(functools.partial(project_kernel, len(parts), w_ids, n_col, depth), shape, where, arrays, scratch)


def solution(mesh):
    placed = (
        P(("groups", "row", "col"), None),
        P(("groups", "col", "row"), None),
        P(("groups", "col", "row"), None),
        P(("groups", "row"), "col"),
        P(None, ("row", "col")),
        P(("groups", "row", "col"), None),
    )
    return jax.shard_map(
        local,
        mesh=mesh,
        in_specs=placed,
        out_specs=P(("groups", "row", "col"), None),
        check_vma=False,
    )
```

time: 34 us -> 33.9 us (level)
  local copies, waits for them, and re-layouts: 0.24 us -> 0.9 us
  waiting for transfers between devices: 10.3 us -> 9.69 us
    unnamed x10, local copies, waits for them, and re-layouts: 0.04 us -> 0.71 us
    ppermute x20, waiting for transfers between devices: 10.3 us -> 9.69 us  [swap(): lax.ppermute(x, axis, [(i, i ^ mask) for i in range(lax.axis_size(axis))])]
  transfers between devices with their start and end apart: 20 -> 20, of which waited for: 9 -> 8; matrix products, arithmetic and copies ran while one was open for 4% -> 4% of each run, Pallas kernels for 4% -> 4%
where the time goes in v3:
time: 33.9 us; the launch traced here: 33.8 us
  starting transfers between devices  18.2 us (54%)
  waiting for transfers between devices  9.69 us (29%)
  Pallas kernels  3.71 us (11%)
  other arithmetic  1.13 us (3%)
  local copies, waits for them, and re-layouts  0.9 us (3%)
    ppermute x20, starting transfers between devices, swap(): lax.ppermute(x, axis, [(i, i ^ mask) for i in range(lax.axis_size(axis))])  18.2 us
    ppermute x20, waiting for transfers between devices, swap(): lax.ppermute(x, axis, [(i, i ^ mask) for i in range(lax.axis_size(axis))])  9.69 us
    pallas_call x1, Pallas kernels, call(): pl.pallas_call(kernel, out_shape=shapes, in_specs=[smem] + [vmem] * len(a...  2.33 us
    pallas_call x1, Pallas kernels, attend(): pl.pallas_call(functools.partial(attend_kernel, q_masks, k_masks, per_til...  1.38 us
    concatenate x1, other arithmetic, local(): pack = jnp.concatenate([keys, values, weight] if ride else [keys, values])  0.96 us
    unnamed x10, local copies, waits for them, and re-layouts  0.71 us
  transfers between devices with their start and end apart: 20, of which 8 were waited for; matrix products, arithmetic and copies ran while one was open for 4% of the time, Pallas kernels for 4%

profile of v3, /device:TPU:0, one launch (start us, length us, event | category | flops | bytes accessed | tf_op | source)
XLA Modules:
  0.0 33.8 jit_solution(10263526037823179638)
XLA Ops:
  0.0 4.0 %collective-permute-start = (s32[2,2]{1,0:T(2,128)}, s32[2,2]{1,0:T(2,128)S(1)}, u32[]{:S(2)}, u32[]{:S(2)}) collective-permute-start(s32[2,2]{1,0:T(2,128)} %param.9), channel_id=1, source_target_pairs={{0,2},{1,3},{2,0},{3,1},{4,6},{5,7},{6,4},{7,5},{8,10},{9,11},{10,... | collective-permute-start | bytes 56 | tf_op jit(solution)/shard_map/ppermute | solution.py:19
  4.0 1.6 %collective-permute-start.1 = (bf16[64,384]{1,0:T(8,128)(2,1)}, bf16[64,384]{1,0:T(8,128)(2,1)S(1)}, u32[]{:S(2)}, u32[]{:S(2)}) collective-permute-start(bf16[64,384]{1,0:T(8,128)(2,1)} %refs_0_.1), channel_id=1, source_target_pairs={{0,1},{1,0},{2,3},{3,2},{4,5},{5,4},{6,7},{7,6},{8,9},{9,8},{10,11... | collective-permute-start | bytes 147464 | tf_op jit(solution)/shard_map/ppermute | solution.py:19
  5.6 0.3 collective-permute-start.5
  6.0 2.6 %collective-permute-start.6 = (bf16[64,384]{1,0:T(8,128)(2,1)}, bf16[64,384]{1,0:T(8,128)(2,1)S(1)}, u32[]{:S(2)}, u32[]{:S(2)}) collective-permute-start(bf16[64,384]{1,0:T(8,128)(2,1)} %param.8), channel_id=1, source_target_pairs={{0,2},{1,3},{2,0},{3,1},{4,6},{5,7},{6,4},{7,5},{8,10},{9,11},{10,... | collective-permute-start | bytes 147464 | tf_op jit(solution)/shard_map/ppermute | solution.py:19
  8.5 0.4 %collective-permute-start.12 = (bf16[160,384]{1,0:T(8,128)(2,1)}, bf16[160,384]{1,0:T(8,128)(2,1)S(1)}, u32[]{:S(2)}, u32[]{:S(2)}) collective-permute-start(bf16[160,384]{1,0:T(8,128)(2,1)} %bitcast.3), channel_id=1, source_target_pairs={{0,1},{1,0},{2,3},{3,2},{4,5},{5,4},{6,7},{7,6},{8,9},{9,8},{10,11... | collective-permute-start | bytes 368648 | tf_op jit(solution)/shard_map/ppermute | solution.py:19
  9.0 1.0 %pad_maximum_fusion.refs_2_ = bf16[288,384]{1,0:T(8,128)(2,1)S(1)} fusion(bf16[160,384]{1,0:T(8,128)(2,1)} %bitcast.4, bf16[64,384]{1,0:T(8,128)(2,1)} %param.8, bf16[64,384]{1,0:T(8,128)(2,1)} %param.7), kind=kLoop, calls=%fused_computation | loop fusion | flops 663552 | bytes 442368 | tf_op jit(solution)/shard_map/concatenate | solution.py:166
  10.0 0.7 %copy-done.3 = s32[2,2]{1,0:T(2,128)S(1)} copy-done((s32[2,2]{1,0:T(2,128)S(1)}, s32[2,2]{1,0:T(2,128)}, u32[]{:S(2)}) %copy-start.3) | copy-done | bytes 40
  10.9 1.8 %collective-permute-start.2 = (bf16[288,384]{1,0:T(8,128)(2,1)S(1)}, bf16[288,384]{1,0:T(8,128)(2,1)S(1)}, u32[]{:S(2)}, u32[]{:S(2)}) collective-permute-start(bf16[288,384]{1,0:T(8,128)(2,1)S(1)} %pad_maximum_fusion.refs_2_), channel_id=1, source_target_pairs={{0,8},{4,12},{8,0},{12,4},{1,9},{5,13},{9,1},{13,5},{2,10},{6,14},... | collective-permute-start | bytes 663560 | tf_op jit(solution)/shard_map/ppermute | solution.py:19
  12.8 1.6 %collective-permute-start.7 = (bf16[128,384]{1,0:T(8,128)(2,1)S(1)}, bf16[128,384]{1,0:T(8,128)(2,1)S(1)}, u32[]{:S(2)}, u32[]{:S(2)}) collective-permute-start(bf16[128,384]{1,0:T(8,128)(2,1)S(1)} %constant_dynamic-update-slice_fusion.refs_6_), channel_id=1, source_target_pairs={{0,8},{4,12},{8,0},{12,4},{1,9},{5,13},{9,1},{13,5},{2,10},{6,14},... | collective-permute-start | bytes 294920 | tf_op jit(solution)/shard_map/ppermute | solution.py:19
  14.5 2.1 %collective-permute-done.12 = bf16[160,384]{1,0:T(8,128)(2,1)S(1)} collective-permute-done((bf16[160,384]{1,0:T(8,128)(2,1)}, bf16[160,384]{1,0:T(8,128)(2,1)S(1)}, u32[]{:S(2)}, u32[]{:S(2)}) %collective-permute-start.12) | collective-permute-done | bytes 122912 | tf_op jit(solution)/shard_map/ppermute | solution.py:19
  16.5 1.5 %collective-permute-done.11 = bf16[160,384]{1,0:T(8,128)(2,1)S(1)} collective-permute-done((bf16[160,384]{1,0:T(8,128)(2,1)S(1)}, bf16[160,384]{1,0:T(8,128)(2,1)S(1)}, u32[]{:S(2)}, u32[]{:S(2)}) %collective-permute-start.11) | collective-permute-done | bytes 122912 | tf_op jit(solution)/shard_map/ppermute | solution.py:19
  18.0 0.2 collective-permute-start.16
  18.2 0.7 %collective-permute-done.7.refs_7_ = bf16[128,384]{1,0:T(8,128)(2,1)S(1)} collective-permute-done((bf16[128,384]{1,0:T(8,128)(2,1)S(1)}, bf16[128,384]{1,0:T(8,128)(2,1)S(1)}, u32[]{:S(2)}, u32[]{:S(2)}) %collective-permute-start.7) | collective-permute-done | bytes 98336 | tf_op jit(solution)/shard_map/ppermute | solution.py:19
  18.9 0.5 %collective-permute-start.4 = (bf16[288,384]{1,0:T(8,128)(2,1)S(1)}, bf16[288,384]{1,0:T(8,128)(2,1)S(1)}, u32[]{:S(2)}, u32[]{:S(2)}) collective-permute-start(bf16[288,384]{1,0:T(8,128)(2,1)S(1)} %collective-permute-done.2.refs_3_.refs_4_), channel_id=1, source_target_pairs={{0,4},{4,0},{8,12},{12,8},{1,5},{5,1},{9,13},{13,9},{2,6},{6,2},{1... | collective-permute-start | bytes 663560 | tf_op jit(solution)/shard_map/ppermute | solution.py:19
  19.5 1.9 %collective-permute-start.13 = (bf16[320,384]{1,0:T(8,128)(2,1)S(1)}, bf16[320,384]{1,0:T(8,128)(2,1)S(1)}, u32[]{:S(2)}, u32[]{:S(2)}) collective-permute-start(bf16[320,384]{1,0:T(8,128)(2,1)S(1)} %constant_dynamic-update-slice_fusion.2.refs_6_), channel_id=1, source_target_pairs={{0,8},{4,12},{8,0},{12,4},{1,9},{5,13},{9,1},{13,5},{2,10},{6,14},... | collective-permute-start | bytes 737288 | tf_op jit(solution)/shard_map/ppermute | solution.py:19
  21.4 1.4 %shard_map.64.refs_0_ = f32[128,512]{1,0:T(8,128)S(1)} custom-call(s32[10]{0:T(128)S(1)} %pad_add_fusion.1.place_ref, bf16[64,384]{1,0:T(8,128)(2,1)S(1)} %copy-done.1, bf16[64,384]{1,0:T(8,128)(2,1)S(1)} %collective-permute-done.1.refs_1_, bf16[288,384]{1,0:T(8,128)(2,1)S(1)} %pad_maximum_fusion.refs_2_, ...), custom_call_target="tpu_custom_call" | custom-call | tf_op jit(solution)/shard_map/pallas_call | solution.py:93
  22.8 1.6 %collective-permute-start.10 = (f16[64,512]{1,0:T(8,128)(2,1)S(1)}, f16[64,512]{1,0:T(8,128)(2,1)S(1)}, u32[]{:S(2)}, u32[]{:S(2)}) collective-permute-start(f16[64,512]{1,0:T(8,128)(2,1)S(1)} %slice_convert_fusion), channel_id=1, source_target_pairs={{0,1},{1,0},{2,3},{3,2},{4,5},{5,4},{6,7},{7,6},{8,9},{9,8},{10,11... | collective-permute-start | bytes 196616 | tf_op jit(solution)/shard_map/ppermute | solution.py:19
  24.4 1.0 %collective-permute-start.17 = (bf16[160,384]{1,0:T(8,128)(2,1)S(1)}, bf16[160,384]{1,0:T(8,128)(2,1)S(1)}, u32[]{:S(2)}, u32[]{:S(2)}) collective-permute-start(bf16[160,384]{1,0:T(8,128)(2,1)S(1)} %collective-permute-done.16.refs_10_), channel_id=1, source_target_pairs={{0,8},{4,12},{8,0},{12,4},{1,9},{5,13},{9,1},{13,5},{2,10},{6,14},... | collective-permute-start | bytes 368648 | tf_op jit(solution)/shard_map/ppermute | solution.py:19
  25.4 1.7 %collective-permute-done.10 = f16[64,512]{1,0:T(8,128)(2,1)S(1)} collective-permute-done((f16[64,512]{1,0:T(8,128)(2,1)S(1)}, f16[64,512]{1,0:T(8,128)(2,1)S(1)}, u32[]{:S(2)}, u32[]{:S(2)}) %collective-permute-start.10) | collective-permute-done | bytes 65568 | tf_op jit(solution)/shard_map/ppermute | solution.py:19
  27.2 1.1 %collective-permute-done.13.refs_7_ = bf16[320,384]{1,0:T(8,128)(2,1)S(1)} collective-permute-done((bf16[320,384]{1,0:T(8,128)(2,1)S(1)}, bf16[320,384]{1,0:T(8,128)(2,1)S(1)}, u32[]{:S(2)}, u32[]{:S(2)}) %collective-permute-start.13) | collective-permute-done | bytes 245792 | tf_op jit(solution)/shard_map/ppermute | solution.py:19
  28.3 0.5 %collective-permute-start.18 = (bf16[160,384]{1,0:T(8,128)(2,1)S(1)}, bf16[160,384]{1,0:T(8,128)(2,1)S(1)}, u32[]{:S(2)}, u32[]{:S(2)}) collective-permute-start(bf16[160,384]{1,0:T(8,128)(2,1)S(1)} %collective-permute-done.16.refs_10_), channel_id=1, source_target_pairs={{0,4},{4,0},{8,12},{12,8},{1,5},{5,1},{9,13},{13,9},{2,6},{6,2},{1... | collective-permute-start | bytes 368648 | tf_op jit(solution)/shard_map/ppermute | solution.py:19
  28.8 1.3 %collective-permute-done.17.refs_11_ = bf16[160,384]{1,0:T(8,128)(2,1)S(1)} collective-permute-done((bf16[160,384]{1,0:T(8,128)(2,1)S(1)}, bf16[160,384]{1,0:T(8,128)(2,1)S(1)}, u32[]{:S(2)}, u32[]{:S(2)}) %collective-permute-start.17) | collective-permute-done | bytes 122912 | tf_op jit(solution)/shard_map/ppermute | solution.py:19
  30.2 1.3 %collective-permute-done.19.refs_13_ = bf16[160,384]{1,0:T(8,128)(2,1)S(1)} collective-permute-done((bf16[160,384]{1,0:T(8,128)(2,1)S(1)}, bf16[160,384]{1,0:T(8,128)(2,1)S(1)}, u32[]{:S(2)}, u32[]{:S(2)}) %collective-permute-start.19) | collective-permute-done | bytes 122912 | tf_op jit(solution)/shard_map/ppermute | solution.py:19
  31.4 2.3 %shard_map.65 = bf16[64,2560]{1,0:T(8,128)(2,1)} custom-call(s32[2]{0:T(128)S(1)} %pad_add_fusion.where_ref, f32[128,512]{1,0:T(8,128)S(1)} %shard_map.64.refs_0_, f32[64,512]{1,0:T(8,128)S(1)} %convert_element_type.4.refs_1_, bf16[288,384]{1,0:T(8,128)(2,1)S(1)} %pad_maximum_fusion.refs_2_, bf16[288,384]{1,0:T(8,128)(2,1)S(1)} %collective-permute-done.3.refs_4_.refs_3_, ...), custom_call_target="tpu_custom_call" | custom-call | tf_op jit(solution)/shard_map/pallas_call | solution.py:146
  (37 shorter events, 0.7 us)
Async XLA Ops:
  0.0 10.7 %collective-permute-start = (s32[2,2]{1,0:T(2,128)}, s32[2,2]{1,0:T(2,128)S(1)}, u32[]{:S(2)}, u32[]{:S(2)}) collective-permute-start(s32[2,2]{1,0:T(2,128)} %param.9), channel_id=1, source_target_pairs={{0,2},{1,3},{2,0},{3,1},{4,6},{5,7},{6,4},{7,5},{8,10},{9,11},{10,... | collective-permute-start | bytes 56 | tf_op jit(solution)/shard_map/ppermute | solution.py:19
  4.0 6.8 %collective-permute-start.1 = (bf16[64,384]{1,0:T(8,128)(2,1)}, bf16[64,384]{1,0:T(8,128)(2,1)S(1)}, u32[]{:S(2)}, u32[]{:S(2)}) collective-permute-start(bf16[64,384]{1,0:T(8,128)(2,1)} %refs_0_.1), channel_id=1, source_target_pairs={{0,1},{1,0},{2,3},{3,2},{4,5},{5,4},{6,7},{7,6},{8,9},{9,8},{10,11... | collective-permute-start | bytes 147464 | tf_op jit(solution)/shard_map/ppermute | solution.py:19
  5.6 7.0 %collective-permute-start.5 = (bf16[64,384]{1,0:T(8,128)(2,1)}, bf16[64,384]{1,0:T(8,128)(2,1)S(1)}, u32[]{:S(2)}, u32[]{:S(2)}) collective-permute-start(bf16[64,384]{1,0:T(8,128)(2,1)} %param.7), channel_id=1, source_target_pairs={{0,2},{1,3},{2,0},{3,1},{4,6},{5,7},{6,4},{7,5},{8,10},{9,11},{10,... | collective-permute-start | bytes 147464 | tf_op jit(solution)/shard_map/ppermute | solution.py:19
  6.0 6.8 %collective-permute-start.6 = (bf16[64,384]{1,0:T(8,128)(2,1)}, bf16[64,384]{1,0:T(8,128)(2,1)S(1)}, u32[]{:S(2)}, u32[]{:S(2)}) collective-permute-start(bf16[64,384]{1,0:T(8,128)(2,1)} %param.8), channel_id=1, source_target_pairs={{0,2},{1,3},{2,0},{3,1},{4,6},{5,7},{6,4},{7,5},{8,10},{9,11},{10,... | collective-permute-start | bytes 147464 | tf_op jit(solution)/shard_map/ppermute | solution.py:19
  8.5 2.2 %copy-start.2 = (bf16[384,160]{0,1:T(8,128)(2,1)S(1)}, bf16[384,160]{0,1:T(8,128)(2,1)}, u32[]{:S(2)}) copy-start(bf16[384,160]{0,1:T(8,128)(2,1)} %param.10) | copy-start | bytes 368644
  8.5 8.0 %collective-permute-start.12 = (bf16[160,384]{1,0:T(8,128)(2,1)}, bf16[160,384]{1,0:T(8,128)(2,1)S(1)}, u32[]{:S(2)}, u32[]{:S(2)}) collective-permute-start(bf16[160,384]{1,0:T(8,128)(2,1)} %bitcast.3), channel_id=1, source_target_pairs={{0,1},{1,0},{2,3},{3,2},{4,5},{5,4},{6,7},{7,6},{8,9},{9,8},{10,11... | collective-permute-start | bytes 368648 | tf_op jit(solution)/shard_map/ppermute | solution.py:19
  10.0 0.7 %copy-start.3 = (s32[2,2]{1,0:T(2,128)S(1)}, s32[2,2]{1,0:T(2,128)}, u32[]{:S(2)}) copy-start(s32[2,2]{1,0:T(2,128)} %param.9) | copy-start | bytes 52
  10.7 7.3 %collective-permute-start.11 = (bf16[160,384]{1,0:T(8,128)(2,1)S(1)}, bf16[160,384]{1,0:T(8,128)(2,1)S(1)}, u32[]{:S(2)}, u32[]{:S(2)}) collective-permute-start(bf16[160,384]{1,0:T(8,128)(2,1)S(1)} %bitcast.5), channel_id=1, source_target_pairs={{0,2},{1,3},{2,0},{3,1},{4,6},{5,7},{6,4},{7,5},{8,10},{9,11},{10,... | collective-permute-start | bytes 368648 | tf_op jit(solution)/shard_map/ppermute | solution.py:19
  10.9 8.0 %collective-permute-start.2 = (bf16[288,384]{1,0:T(8,128)(2,1)S(1)}, bf16[288,384]{1,0:T(8,128)(2,1)S(1)}, u32[]{:S(2)}, u32[]{:S(2)}) collective-permute-start(bf16[288,384]{1,0:T(8,128)(2,1)S(1)} %pad_maximum_fusion.refs_2_), channel_id=1, source_target_pairs={{0,8},{4,12},{8,0},{12,4},{1,9},{5,13},{9,1},{13,5},{2,10},{6,14},... | collective-permute-start | bytes 663560 | tf_op jit(solution)/shard_map/ppermute | solution.py:19
  12.7 3.8 %collective-permute-start.8 = (bf16[128,384]{1,0:T(8,128)(2,1)S(1)}, bf16[128,384]{1,0:T(8,128)(2,1)S(1)}, u32[]{:S(2)}, u32[]{:S(2)}) collective-permute-start(bf16[128,384]{1,0:T(8,128)(2,1)S(1)} %constant_dynamic-update-slice_fusion.refs_6_), channel_id=1, source_target_pairs={{0,4},{4,0},{8,12},{12,8},{1,5},{5,1},{9,13},{13,9},{2,6},{6,2},{1... | collective-permute-start | bytes 294920 | tf_op jit(solution)/shard_map/ppermute | solution.py:19
  12.8 6.1 %collective-permute-start.7 = (bf16[128,384]{1,0:T(8,128)(2,1)S(1)}, bf16[128,384]{1,0:T(8,128)(2,1)S(1)}, u32[]{:S(2)}, u32[]{:S(2)}) collective-permute-start(bf16[128,384]{1,0:T(8,128)(2,1)S(1)} %constant_dynamic-update-slice_fusion.refs_6_), channel_id=1, source_target_pairs={{0,8},{4,12},{8,0},{12,4},{1,9},{5,13},{9,1},{13,5},{2,10},{6,14},... | collective-permute-start | bytes 294920 | tf_op jit(solution)/shard_map/ppermute | solution.py:19
  16.5 4.8 %collective-permute-start.3 = (bf16[288,384]{1,0:T(8,128)(2,1)S(1)}, bf16[288,384]{1,0:T(8,128)(2,1)S(1)}, u32[]{:S(2)}, u32[]{:S(2)}) collective-permute-start(bf16[288,384]{1,0:T(8,128)(2,1)S(1)} %pad_maximum_fusion.refs_2_), channel_id=1, source_target_pairs={{0,4},{4,0},{8,12},{12,8},{1,5},{5,1},{9,13},{13,9},{2,6},{6,2},{1... | collective-permute-start | bytes 663560 | tf_op jit(solution)/shard_map/ppermute | solution.py:19
  18.0 6.4 %collective-permute-start.16 = (bf16[160,384]{1,0:T(8,128)(2,1)S(1)}, bf16[160,384]{1,0:T(8,128)(2,1)S(1)}, u32[]{:S(2)}, u32[]{:S(2)}) collective-permute-start(bf16[160,384]{1,0:T(8,128)(2,1)S(1)} %collective-permute-done.11), channel_id=1, source_target_pairs={{0,1},{1,0},{2,3},{3,2},{4,5},{5,4},{6,7},{7,6},{8,9},{9,8},{10,11... | collective-permute-start | bytes 368648 | tf_op jit(solution)/shard_map/ppermute | solution.py:19
  18.9 2.4 %collective-permute-start.9 = (bf16[128,384]{1,0:T(8,128)(2,1)S(1)}, bf16[128,384]{1,0:T(8,128)(2,1)S(1)}, u32[]{:S(2)}, u32[]{:S(2)}) collective-permute-start(bf16[128,384]{1,0:T(8,128)(2,1)S(1)} %collective-permute-done.7.refs_7_), channel_id=1, source_target_pairs={{0,4},{4,0},{8,12},{12,8},{1,5},{5,1},{9,13},{13,9},{2,6},{6,2},{1... | collective-permute-start | bytes 294920 | tf_op jit(solution)/shard_map/ppermute | solution.py:19
  18.9 2.4 %collective-permute-start.4 = (bf16[288,384]{1,0:T(8,128)(2,1)S(1)}, bf16[288,384]{1,0:T(8,128)(2,1)S(1)}, u32[]{:S(2)}, u32[]{:S(2)}) collective-permute-start(bf16[288,384]{1,0:T(8,128)(2,1)S(1)} %collective-permute-done.2.refs_3_.refs_4_), channel_id=1, source_target_pairs={{0,4},{4,0},{8,12},{12,8},{1,5},{5,1},{9,13},{13,9},{2,6},{6,2},{1... | collective-permute-start | bytes 663560 | tf_op jit(solution)/shard_map/ppermute | solution.py:19
  19.4 1.9 %copy-start.1 = (bf16[64,384]{1,0:T(8,128)(2,1)S(1)}, bf16[64,384]{1,0:T(8,128)(2,1)}, u32[]{:S(2)}) copy-start(bf16[64,384]{1,0:T(8,128)(2,1)} %refs_0_.1) | copy-start | bytes 147460
  19.5 8.8 %collective-permute-start.13 = (bf16[320,384]{1,0:T(8,128)(2,1)S(1)}, bf16[320,384]{1,0:T(8,128)(2,1)S(1)}, u32[]{:S(2)}, u32[]{:S(2)}) collective-permute-start(bf16[320,384]{1,0:T(8,128)(2,1)S(1)} %constant_dynamic-update-slice_fusion.2.refs_6_), channel_id=1, source_target_pairs={{0,8},{4,12},{8,0},{12,4},{1,9},{5,13},{9,1},{13,5},{2,10},{6,14},... | collective-permute-start | bytes 737288 | tf_op jit(solution)/shard_map/ppermute | solution.py:19
  22.7 8.7 %copy-start = (bf16[64,2560]{1,0:T(8,128)(2,1)S(1)}, bf16[64,2560]{1,0:T(8,128)(2,1)}, u32[]{:S(2)}) copy-start(bf16[64,2560]{1,0:T(8,128)(2,1)} %refs_14_.1) | copy-start | bytes 983044
  22.8 4.3 %collective-permute-start.10 = (f16[64,512]{1,0:T(8,128)(2,1)S(1)}, f16[64,512]{1,0:T(8,128)(2,1)S(1)}, u32[]{:S(2)}, u32[]{:S(2)}) collective-permute-start(f16[64,512]{1,0:T(8,128)(2,1)S(1)} %slice_convert_fusion), channel_id=1, source_target_pairs={{0,1},{1,0},{2,3},{3,2},{4,5},{5,4},{6,7},{7,6},{8,9},{9,8},{10,11... | collective-permute-start | bytes 196616 | tf_op jit(solution)/shard_map/ppermute | solution.py:19
  24.4 5.7 %collective-permute-start.17 = (bf16[160,384]{1,0:T(8,128)(2,1)S(1)}, bf16[160,384]{1,0:T(8,128)(2,1)S(1)}, u32[]{:S(2)}, u32[]{:S(2)}) collective-permute-start(bf16[160,384]{1,0:T(8,128)(2,1)S(1)} %collective-permute-done.16.refs_10_), channel_id=1, source_target_pairs={{0,8},{4,12},{8,0},{12,4},{1,9},{5,13},{9,1},{13,5},{2,10},{6,14},... | collective-permute-start | bytes 368648 | tf_op jit(solution)/shard_map/ppermute | solution.py:19
  27.1 4.3 %collective-permute-start.14 = (bf16[320,384]{1,0:T(8,128)(2,1)S(1)}, bf16[320,384]{1,0:T(8,128)(2,1)S(1)}, u32[]{:S(2)}, u32[]{:S(2)}) collective-permute-start(bf16[320,384]{1,0:T(8,128)(2,1)S(1)} %constant_dynamic-update-slice_fusion.2.refs_6_), channel_id=1, source_target_pairs={{0,4},{4,0},{8,12},{12,8},{1,5},{5,1},{9,13},{13,9},{2,6},{6,2},{1... | collective-permute-start | bytes 737288 | tf_op jit(solution)/shard_map/ppermute | solution.py:19
  28.3 3.2 %collective-permute-start.15 = (bf16[320,384]{1,0:T(8,128)(2,1)S(1)}, bf16[320,384]{1,0:T(8,128)(2,1)S(1)}, u32[]{:S(2)}, u32[]{:S(2)}) collective-permute-start(bf16[320,384]{1,0:T(8,128)(2,1)S(1)} %collective-permute-done.13.refs_7_), channel_id=1, source_target_pairs={{0,4},{4,0},{8,12},{12,8},{1,5},{5,1},{9,13},{13,9},{2,6},{6,2},{1... | collective-permute-start | bytes 737288 | tf_op jit(solution)/shard_map/ppermute | solution.py:19
  28.3 1.9 %collective-permute-start.18 = (bf16[160,384]{1,0:T(8,128)(2,1)S(1)}, bf16[160,384]{1,0:T(8,128)(2,1)S(1)}, u32[]{:S(2)}, u32[]{:S(2)}) collective-permute-start(bf16[160,384]{1,0:T(8,128)(2,1)S(1)} %collective-permute-done.16.refs_10_), channel_id=1, source_target_pairs={{0,4},{4,0},{8,12},{12,8},{1,5},{5,1},{9,13},{13,9},{2,6},{6,2},{1... | collective-permute-start | bytes 368648 | tf_op jit(solution)/shard_map/ppermute | solution.py:19
  30.1 1.3 %collective-permute-start.19 = (bf16[160,384]{1,0:T(8,128)(2,1)S(1)}, bf16[160,384]{1,0:T(8,128)(2,1)S(1)}, u32[]{:S(2)}, u32[]{:S(2)}) collective-permute-start(bf16[160,384]{1,0:T(8,128)(2,1)S(1)} %collective-permute-done.17.refs_11_), channel_id=1, source_target_pairs={{0,4},{4,0},{8,12},{12,8},{1,5},{5,1},{9,13},{13,9},{2,6},{6,2},{1... | collective-permute-start | bytes 368648 | tf_op jit(solution)/shard_map/ppermute | solution.py:19

commit v4 on v3

--- a/solution.py
+++ b/solution.py
@@ -121,18 +121,26 @@
     return lax.dot_general(attended, weight, (((1,), (1,)), ((), ())), preferred_element_type=jnp.float32)
 
 
-def project_kernel(n_parts, w_ids, n_col, depth, where_ref, *refs):
-    part_refs = refs[:n_parts]
-    w_refs = refs[n_parts : n_parts + len(w_ids)]
-    residual_ref, out_ref, whole_ref = refs[n_parts + len(w_ids) :]
-    rows, features = out_ref.shape
-    my_row, my_col = where_ref[0], where_ref[1]
+def place_weight(w_ids, n_col, depth, w_refs, whole_ref):
+    my_row, my_col = (lax.axis_index("row"), lax.axis_index("col")) if len(w_ids) > 1 else (0, 0)
     for ids, ref in zip(w_ids, w_refs):
         first = ref.shape[0] - len(ids) * depth
         for n, (a, b) in enumerate(ids):
             place = ((my_row ^ a) * n_col + (my_col ^ b)) * depth
             whole_ref[pl.ds(pl.multiple_of(place, 16), depth), :] = ref[first + n * depth : first + (n + 1) * depth, :]
-    attended = merge([ref[:rows, :] for ref in part_refs])
+
+
+def merge_kernel(n_parts, w_ids, n_col, depth, *refs):
+    part_refs, w_refs, (attended_ref, whole_ref) = refs[:n_parts], refs[n_parts:-2], refs[-2:]
+    place_weight(w_ids, n_col, depth, w_refs, whole_ref)
+    attended_ref[...] = merge([ref[: attended_ref.shape[0], :] for ref in part_refs])
+
+
+def project_kernel(w_ids, n_col, depth, begun_ref, attended_ref, *refs):
+    w_refs, (residual_ref, out_ref, whole_ref) = refs[: len(w_ids)], refs[len(w_ids) :]
+    place_weight(w_ids, n_col, depth, w_refs, whole_ref)
+    features = out_ref.shape[1]
+    attended = attended_ref[...]
     step = features // 4 if features % (4 * LANES) == 0 else features
     for at in range(0, features, step):
         here = slice(at, at + step)
@@ -140,17 +148,16 @@
         out_ref[:, here] = (product + residual_ref[:, here].astype(jnp.float32)).astype(out_ref.dtype)
 
 
-def call(kernel, shapes, where, arrays, scratch=()):
-    smem = pl.BlockSpec(memory_space=pltpu.SMEM)
+def call(kernel, shapes, arrays, aliases=None):
     vmem = pl.BlockSpec(memory_space=pltpu.VMEM)
     return pl.pallas_call(
         kernel,
         out_shape=shapes,
-        in_specs=[smem] + [vmem] * len(arrays),
+        in_specs=[vmem] * len(arrays),
         out_specs=jax.tree.map(lambda _: vmem, shapes),
-        scratch_shapes=list(scratch),
+        input_output_aliases=aliases or {},
         compiler_params=pltpu.CompilerParams(vmem_limit_bytes=24 * 2**20),
-    )(where, *arrays)
+    )(*arrays)
 
 
 def local(queries, keys, values, block_mask, out_weight, residual):
@@ -214,12 +221,19 @@
             w_parts += [(x, [(a, m) for _, m in batch]) for a, x in held.items()]
     else:
         weight = lax.all_gather(weight, ("row", "col"), axis=0, tiled=True)
-        w_parts, depth, n_col, where = [(weight, [(0, 0)])], weight.shape[0], 1, jnp.zeros_like(where)
-    w_ids = [ids for _, ids in w_parts]
-    arrays = [*parts, *(x for x, _ in w_parts), residual]
-    scratch = [pltpu.VMEM((residual.shape[1], queries.shape[1]), jnp.bfloat16)]
-    shape = jax.ShapeDtypeStruct(residual.shape, residual.dtype)
-    return call(functools.partial(project_kernel, len(parts), w_ids, n_col, depth), shape, where, arrays, scratch)
+        w_parts, depth, n_col = [(weight, [(0, 0)])], weight.shape[0], 1
+    soon = [w for w in w_parts if not w[1][0][0] & 1 or w[1][0][1] == 0]
+    last = [w for w in w_parts if all(w is not other for other in soon)]
+    whole = jax.ShapeDtypeStruct((residual.shape[1], queries.shape[1]), jnp.bfloat16)
+    attended, begun = call(
+        functools.partial(merge_kernel, len(parts), [ids for _, ids in soon], n_col, depth),
+        [jax.ShapeDtypeStruct(queries.shape, queries.dtype), whole], [*parts, *(x for x, _ in soon)],
+    )
+    return call(
+        functools.partial(project_kernel, [ids for _, ids in last], n_col, depth),
+        [jax.ShapeDtypeStruct(residual.shape, residual.dtype), whole],
+        [begun, attended, *(x for x, _ in last), residual], {0: 1},
+    )[0]
 
 
 def solution(mesh):

time: 33.9 us -> 33.2 us (0.979)
  waiting for transfers between devices: 9.69 us -> 8.5 us
  local copies, waits for them, and re-layouts: 0.9 us -> 1.69 us
  Pallas kernels: 3.71 us -> 3.35 us
    ppermute x20, waiting for transfers between devices: 9.69 us -> 8.5 us  [swap(): lax.ppermute(x, axis, [(i, i ^ mask) for i in range(lax.axis_size(axis))])]
    reshape x1, local copies, waits for them, and re-layouts: 0.08 us -> 0.76 us  [local(): masks = [where, block_mask.reshape(-1)]]
    pallas_call x1 -> x2, Pallas kernels: 2.33 us -> 1.98 us  [call(): pl.pallas_call(kernel, out_shape=shapes, in_specs=[vmem] * len(arrays), o...]
    unnamed x10 -> x6, local copies, waits for them, and re-layouts: 0.71 us -> 0.82 us
  transfers between devices with their start and end apart: 20 -> 20, of which waited for: 8 -> 7; matrix products, arithmetic and copies ran while one was open for 4% -> 6% of each run, Pallas kernels for 4% -> 5%
where the time goes in v4:
time: 33.2 us; the launch traced here: 33 us
  starting transfers between devices  18.3 us (55%)
  waiting for transfers between devices  8.5 us (26%)
  Pallas kernels  3.35 us (10%)
  local copies, waits for them, and re-layouts  1.69 us (5%)
  other arithmetic  1.06 us (3%)
    ppermute x20, starting transfers between devices, swap(): lax.ppermute(x, axis, [(i, i ^ mask) for i in range(lax.axis_size(axis))])  18.3 us
    ppermute x20, waiting for transfers between devices, swap(): lax.ppermute(x, axis, [(i, i ^ mask) for i in range(lax.axis_size(axis))])  8.5 us
    pallas_call x2, Pallas kernels, call(): pl.pallas_call(kernel, out_shape=shapes, in_specs=[vmem] * len(arrays), o...  1.98 us
    pallas_call x1, Pallas kernels, attend(): pl.pallas_call(functools.partial(attend_kernel, q_masks, k_masks, per_til...  1.37 us
    concatenate x1, other arithmetic, local(): pack = jnp.concatenate([keys, values, weight] if ride else [keys, values])  0.96 us
    unnamed x6, local copies, waits for them, and re-layouts  0.82 us
    reshape x1, local copies, waits for them, and re-layouts, local(): masks = [where, block_mask.reshape(-1)]  0.76 us
  transfers between devices with their start and end apart: 20, of which 7 were waited for; matrix products, arithmetic and copies ran while one was open for 6% of the time, Pallas kernels for 5%

profile of v4, /device:TPU:0, one launch (start us, length us, event | category | flops | bytes accessed | tf_op | source)
XLA Modules:
  0.0 33.0 jit_solution(345292196096400950)
XLA Ops:
  0.0 4.0 %collective-permute-start = (s32[2,2]{1,0:T(2,128)}, s32[2,2]{1,0:T(2,128)S(1)}, u32[]{:S(2)}, u32[]{:S(2)}) collective-permute-start(s32[2,2]{1,0:T(2,128)} %param.9), channel_id=1, source_target_pairs={{0,2},{1,3},{2,0},{3,1},{4,6},{5,7},{6,4},{7,5},{8,10},{9,11},{10,... | collective-permute-start | bytes 56 | tf_op jit(solution)/shard_map/ppermute | solution.py:19
  4.0 1.6 %collective-permute-start.1 = (bf16[64,384]{1,0:T(8,128)(2,1)}, bf16[64,384]{1,0:T(8,128)(2,1)S(1)}, u32[]{:S(2)}, u32[]{:S(2)}) collective-permute-start(bf16[64,384]{1,0:T(8,128)(2,1)} %refs_0_.1), channel_id=1, source_target_pairs={{0,1},{1,0},{2,3},{3,2},{4,5},{5,4},{6,7},{7,6},{8,9},{9,8},{10,11... | collective-permute-start | bytes 147464 | tf_op jit(solution)/shard_map/ppermute | solution.py:19
  5.6 0.3 %collective-permute-start.5 = (bf16[64,384]{1,0:T(8,128)(2,1)}, bf16[64,384]{1,0:T(8,128)(2,1)S(1)}, u32[]{:S(2)}, u32[]{:S(2)}) collective-permute-start(bf16[64,384]{1,0:T(8,128)(2,1)} %param.7), channel_id=1, source_target_pairs={{0,2},{1,3},{2,0},{3,1},{4,6},{5,7},{6,4},{7,5},{8,10},{9,11},{10,... | collective-permute-start | bytes 147464 | tf_op jit(solution)/shard_map/ppermute | solution.py:19
  6.0 2.6 %collective-permute-start.6 = (bf16[64,384]{1,0:T(8,128)(2,1)}, bf16[64,384]{1,0:T(8,128)(2,1)S(1)}, u32[]{:S(2)}, u32[]{:S(2)}) collective-permute-start(bf16[64,384]{1,0:T(8,128)(2,1)} %param.8), channel_id=1, source_target_pairs={{0,2},{1,3},{2,0},{3,1},{4,6},{5,7},{6,4},{7,5},{8,10},{9,11},{10,... | collective-permute-start | bytes 147464 | tf_op jit(solution)/shard_map/ppermute | solution.py:19
  8.5 0.4 %collective-permute-start.12 = (bf16[160,384]{1,0:T(8,128)(2,1)}, bf16[160,384]{1,0:T(8,128)(2,1)S(1)}, u32[]{:S(2)}, u32[]{:S(2)}) collective-permute-start(bf16[160,384]{1,0:T(8,128)(2,1)} %bitcast.3), channel_id=1, source_target_pairs={{0,1},{1,0},{2,3},{3,2},{4,5},{5,4},{6,7},{7,6},{8,9},{9,8},{10,11... | collective-permute-start | bytes 368648 | tf_op jit(solution)/shard_map/ppermute | solution.py:19
  9.0 1.0 %pad_maximum_fusion.refs_2_ = bf16[288,384]{1,0:T(8,128)(2,1)S(1)} fusion(bf16[160,384]{1,0:T(8,128)(2,1)} %bitcast.4, bf16[64,384]{1,0:T(8,128)(2,1)} %param.8, bf16[64,384]{1,0:T(8,128)(2,1)} %param.7), kind=kLoop, calls=%fused_computation | loop fusion | flops 663552 | bytes 442368 | tf_op jit(solution)/shard_map/concatenate | solution.py:173
  10.0 0.8 %reshape.6 = s32[4]{0:T(128)S(1)} reshape(s32[2,2]{1,0:T(2,128)} %param.9) | data formatting | bytes 32 | tf_op jit(solution)/shard_map/reshape | solution.py:188
  10.8 1.8 %collective-permute-start.2 = (bf16[288,384]{1,0:T(8,128)(2,1)S(1)}, bf16[288,384]{1,0:T(8,128)(2,1)S(1)}, u32[]{:S(2)}, u32[]{:S(2)}) collective-permute-start(bf16[288,384]{1,0:T(8,128)(2,1)S(1)} %pad_maximum_fusion.refs_2_), channel_id=1, source_target_pairs={{0,8},{4,12},{8,0},{12,4},{1,9},{5,13},{9,1},{13,5},{2,10},{6,14},... | collective-permute-start | bytes 663560 | tf_op jit(solution)/shard_map/ppermute | solution.py:19
  12.8 1.6 %collective-permute-start.7 = (bf16[128,384]{1,0:T(8,128)(2,1)S(1)}, bf16[128,384]{1,0:T(8,128)(2,1)S(1)}, u32[]{:S(2)}, u32[]{:S(2)}) collective-permute-start(bf16[128,384]{1,0:T(8,128)(2,1)S(1)} %constant_dynamic-update-slice_fusion.refs_6_), channel_id=1, source_target_pairs={{0,8},{4,12},{8,0},{12,4},{1,9},{5,13},{9,1},{13,5},{2,10},{6,14},... | collective-permute-start | bytes 294920 | tf_op jit(solution)/shard_map/ppermute | solution.py:19
  14.5 0.9 %collective-permute-done.12 = bf16[160,384]{1,0:T(8,128)(2,1)S(1)} collective-permute-done((bf16[160,384]{1,0:T(8,128)(2,1)}, bf16[160,384]{1,0:T(8,128)(2,1)S(1)}, u32[]{:S(2)}, u32[]{:S(2)}) %collective-permute-start.12) | collective-permute-done | bytes 122912 | tf_op jit(solution)/shard_map/ppermute | solution.py:19
  15.4 2.8 %collective-permute-done.11 = bf16[160,384]{1,0:T(8,128)(2,1)S(1)} collective-permute-done((bf16[160,384]{1,0:T(8,128)(2,1)}, bf16[160,384]{1,0:T(8,128)(2,1)S(1)}, u32[]{:S(2)}, u32[]{:S(2)}) %collective-permute-start.11) | collective-permute-done | bytes 122912 | tf_op jit(solution)/shard_map/ppermute | solution.py:19
  18.4 0.5 %collective-permute-done.7.refs_7_ = bf16[128,384]{1,0:T(8,128)(2,1)S(1)} collective-permute-done((bf16[128,384]{1,0:T(8,128)(2,1)S(1)}, bf16[128,384]{1,0:T(8,128)(2,1)S(1)}, u32[]{:S(2)}, u32[]{:S(2)}) %collective-permute-start.7) | collective-permute-done | bytes 98336 | tf_op jit(solution)/shard_map/ppermute | solution.py:19
  18.9 0.5 %collective-permute-start.4 = (bf16[288,384]{1,0:T(8,128)(2,1)S(1)}, bf16[288,384]{1,0:T(8,128)(2,1)S(1)}, u32[]{:S(2)}, u32[]{:S(2)}) collective-permute-start(bf16[288,384]{1,0:T(8,128)(2,1)S(1)} %collective-permute-done.2.refs_3_.refs_4_), channel_id=1, source_target_pairs={{0,4},{4,0},{8,12},{12,8},{1,5},{5,1},{9,13},{13,9},{2,6},{6,2},{1... | collective-permute-start | bytes 663560 | tf_op jit(solution)/shard_map/ppermute | solution.py:19
  19.5 1.9 %collective-permute-start.13 = (bf16[320,384]{1,0:T(8,128)(2,1)S(1)}, bf16[320,384]{1,0:T(8,128)(2,1)S(1)}, u32[]{:S(2)}, u32[]{:S(2)}) collective-permute-start(bf16[320,384]{1,0:T(8,128)(2,1)S(1)} %constant_dynamic-update-slice_fusion.2.refs_6_), channel_id=1, source_target_pairs={{0,8},{4,12},{8,0},{12,4},{1,9},{5,13},{9,1},{13,5},{2,10},{6,14},... | collective-permute-start | bytes 737288 | tf_op jit(solution)/shard_map/ppermute | solution.py:19
  21.3 0.8 %copy-done.1 = bf16[64,384]{1,0:T(8,128)(2,1)S(1)} copy-done((bf16[64,384]{1,0:T(8,128)(2,1)S(1)}, bf16[64,384]{1,0:T(8,128)(2,1)}, u32[]{:S(2)}) %copy-start.1) | copy-done | bytes 49176
  22.1 1.4 %shard_map.64.refs_0_ = f32[128,512]{1,0:T(8,128)S(1)} custom-call(s32[10]{0:T(128)S(1)} %pad_add_fusion.place_ref, bf16[64,384]{1,0:T(8,128)(2,1)S(1)} %copy-done.1, bf16[64,384]{1,0:T(8,128)(2,1)S(1)} %collective-permute-done.1.refs_1_, bf16[288,384]{1,0:T(8,128)(2,1)S(1)} %pad_maximum_fusion.refs_2_, ...), custom_call_target="tpu_custom_call" | custom-call | tf_op jit(solution)/shard_map/pallas_call | solution.py:93
  23.5 1.6 %collective-permute-start.10 = (f16[64,512]{1,0:T(8,128)(2,1)S(1)}, f16[64,512]{1,0:T(8,128)(2,1)S(1)}, u32[]{:S(2)}, u32[]{:S(2)}) collective-permute-start(f16[64,512]{1,0:T(8,128)(2,1)S(1)} %slice_convert_fusion), channel_id=1, source_target_pairs={{0,1},{1,0},{2,3},{3,2},{4,5},{5,4},{6,7},{7,6},{8,9},{9,8},{10,11... | collective-permute-start | bytes 196616 | tf_op jit(solution)/shard_map/ppermute | solution.py:19
  25.2 1.0 %collective-permute-start.15 = (bf16[160,384]{1,0:T(8,128)(2,1)S(1)}, bf16[160,384]{1,0:T(8,128)(2,1)S(1)}, u32[]{:S(2)}, u32[]{:S(2)}) collective-permute-start(bf16[160,384]{1,0:T(8,128)(2,1)S(1)} %collective-permute-done.14.refs_8_), channel_id=1, source_target_pairs={{0,8},{4,12},{8,0},{12,4},{1,9},{5,13},{9,1},{13,5},{2,10},{6,14},... | collective-permute-start | bytes 368648 | tf_op jit(solution)/shard_map/ppermute | solution.py:19
  26.2 1.7 %collective-permute-done.10 = f16[64,512]{1,0:T(8,128)(2,1)S(1)} collective-permute-done((f16[64,512]{1,0:T(8,128)(2,1)S(1)}, f16[64,512]{1,0:T(8,128)(2,1)S(1)}, u32[]{:S(2)}, u32[]{:S(2)}) %collective-permute-start.10) | collective-permute-done | bytes 65568 | tf_op jit(solution)/shard_map/ppermute | solution.py:19
  28.0 0.5 %collective-permute-start.17 = (bf16[320,384]{1,0:T(8,128)(2,1)S(1)}, bf16[320,384]{1,0:T(8,128)(2,1)S(1)}, u32[]{:S(2)}, u32[]{:S(2)}) collective-permute-start(bf16[320,384]{1,0:T(8,128)(2,1)S(1)} %collective-permute-done.13.refs_7_), channel_id=1, source_target_pairs={{0,4},{4,0},{8,12},{12,8},{1,5},{5,1},{9,13},{13,9},{2,6},{6,2},{1... | collective-permute-start | bytes 737288 | tf_op jit(solution)/shard_map/ppermute | solution.py:19
  28.5 1.5 %collective-permute-done.15.refs_9_ = bf16[160,384]{1,0:T(8,128)(2,1)S(1)} collective-permute-done((bf16[160,384]{1,0:T(8,128)(2,1)S(1)}, bf16[160,384]{1,0:T(8,128)(2,1)S(1)}, u32[]{:S(2)}, u32[]{:S(2)}) %collective-permute-start.15) | collective-permute-done | bytes 122912 | tf_op jit(solution)/shard_map/ppermute | solution.py:19
  30.1 0.4 %shard_map.65 = (bf16[64,384]{1,0:T(8,128)(2,1)S(1)}, bf16[2560,384]{1,0:T(8,128)(2,1)S(1)}) custom-call(f32[128,512]{1,0:T(8,128)S(1)} %shard_map.64.refs_0_, f32[64,512]{1,0:T(8,128)S(1)} %convert_element_type.4.refs_1_, bf16[288,384]{1,0:T(8,128)(2,1)S(1)} %pad_maximum_fusion.refs_2_, bf16[288,384]{1,0:T(8,128)(2,1)S(1)} %collective-permute-done.3.refs_4_.refs_3_, ...), custom_call_target="tpu_custom_call" | custom-call | tf_op jit(solution)/shard_map/pallas_call | solution.py:153
  30.5 1.0 %collective-permute-done.19.refs_3_ = bf16[160,384]{1,0:T(8,128)(2,1)S(1)} collective-permute-done((bf16[160,384]{1,0:T(8,128)(2,1)S(1)}, bf16[160,384]{1,0:T(8,128)(2,1)S(1)}, u32[]{:S(2)}, u32[]{:S(2)}) %collective-permute-start.19) | collective-permute-done | bytes 122912 | tf_op jit(solution)/shard_map/ppermute | solution.py:19
  31.4 1.6 %shard_map.66 = (bf16[64,2560]{1,0:T(8,128)(2,1)}, bf16[2560,384]{1,0:T(8,128)(2,1)S(1)}) custom-call(bf16[2560,384]{1,0:T(8,128)(2,1)S(1)} %get-tuple-element.20.begun_ref, bf16[64,384]{1,0:T(8,128)(2,1)S(1)} %get-tuple-element.21.attended_ref, bf16[320,384]{1,0:T(8,128)(2,1)S(1)} %collective-permute-done.16.refs_0_, ...), custom_call_target="tpu_custom_call", output_to_operand_aliasing={{1}: (0, {})} | custom-call | tf_op jit(solution)/shard_map/pallas_call | solution.py:153
  (33 shorter events, 0.9 us)
Async XLA Ops:
  0.0 10.7 %collective-permute-start = (s32[2,2]{1,0:T(2,128)}, s32[2,2]{1,0:T(2,128)S(1)}, u32[]{:S(2)}, u32[]{:S(2)}) collective-permute-start(s32[2,2]{1,0:T(2,128)} %param.9), channel_id=1, source_target_pairs={{0,2},{1,3},{2,0},{3,1},{4,6},{5,7},{6,4},{7,5},{8,10},{9,11},{10,... | collective-permute-start | bytes 56 | tf_op jit(solution)/shard_map/ppermute | solution.py:19
  4.0 6.8 %collective-permute-start.1 = (bf16[64,384]{1,0:T(8,128)(2,1)}, bf16[64,384]{1,0:T(8,128)(2,1)S(1)}, u32[]{:S(2)}, u32[]{:S(2)}) collective-permute-start(bf16[64,384]{1,0:T(8,128)(2,1)} %refs_0_.1), channel_id=1, source_target_pairs={{0,1},{1,0},{2,3},{3,2},{4,5},{5,4},{6,7},{7,6},{8,9},{9,8},{10,11... | collective-permute-start | bytes 147464 | tf_op jit(solution)/shard_map/ppermute | solution.py:19
  5.6 7.0 %collective-permute-start.5 = (bf16[64,384]{1,0:T(8,128)(2,1)}, bf16[64,384]{1,0:T(8,128)(2,1)S(1)}, u32[]{:S(2)}, u32[]{:S(2)}) collective-permute-start(bf16[64,384]{1,0:T(8,128)(2,1)} %param.7), channel_id=1, source_target_pairs={{0,2},{1,3},{2,0},{3,1},{4,6},{5,7},{6,4},{7,5},{8,10},{9,11},{10,... | collective-permute-start | bytes 147464 | tf_op jit(solution)/shard_map/ppermute | solution.py:19
  6.0 6.8 %collective-permute-start.6 = (bf16[64,384]{1,0:T(8,128)(2,1)}, bf16[64,384]{1,0:T(8,128)(2,1)S(1)}, u32[]{:S(2)}, u32[]{:S(2)}) collective-permute-start(bf16[64,384]{1,0:T(8,128)(2,1)} %param.8), channel_id=1, source_target_pairs={{0,2},{1,3},{2,0},{3,1},{4,6},{5,7},{6,4},{7,5},{8,10},{9,11},{10,... | collective-permute-start | bytes 147464 | tf_op jit(solution)/shard_map/ppermute | solution.py:19
  8.5 6.9 %collective-permute-start.12 = (bf16[160,384]{1,0:T(8,128)(2,1)}, bf16[160,384]{1,0:T(8,128)(2,1)S(1)}, u32[]{:S(2)}, u32[]{:S(2)}) collective-permute-start(bf16[160,384]{1,0:T(8,128)(2,1)} %bitcast.3), channel_id=1, source_target_pairs={{0,1},{1,0},{2,3},{3,2},{4,5},{5,4},{6,7},{7,6},{8,9},{9,8},{10,11... | collective-permute-start | bytes 368648 | tf_op jit(solution)/shard_map/ppermute | solution.py:19
  10.7 7.4 %collective-permute-start.11 = (bf16[160,384]{1,0:T(8,128)(2,1)}, bf16[160,384]{1,0:T(8,128)(2,1)S(1)}, u32[]{:S(2)}, u32[]{:S(2)}) collective-permute-start(bf16[160,384]{1,0:T(8,128)(2,1)} %bitcast.5), channel_id=1, source_target_pairs={{0,2},{1,3},{2,0},{3,1},{4,6},{5,7},{6,4},{7,5},{8,10},{9,11},{10,... | collective-permute-start | bytes 368648 | tf_op jit(solution)/shard_map/ppermute | solution.py:19
  10.8 8.0 %collective-permute-start.2 = (bf16[288,384]{1,0:T(8,128)(2,1)S(1)}, bf16[288,384]{1,0:T(8,128)(2,1)S(1)}, u32[]{:S(2)}, u32[]{:S(2)}) collective-permute-start(bf16[288,384]{1,0:T(8,128)(2,1)S(1)} %pad_maximum_fusion.refs_2_), channel_id=1, source_target_pairs={{0,8},{4,12},{8,0},{12,4},{1,9},{5,13},{9,1},{13,5},{2,10},{6,14},... | collective-permute-start | bytes 663560 | tf_op jit(solution)/shard_map/ppermute | solution.py:19
  12.7 2.7 %collective-permute-start.8 = (bf16[128,384]{1,0:T(8,128)(2,1)S(1)}, bf16[128,384]{1,0:T(8,128)(2,1)S(1)}, u32[]{:S(2)}, u32[]{:S(2)}) collective-permute-start(bf16[128,384]{1,0:T(8,128)(2,1)S(1)} %constant_dynamic-update-slice_fusion.refs_6_), channel_id=1, source_target_pairs={{0,4},{4,0},{8,12},{12,8},{1,5},{5,1},{9,13},{13,9},{2,6},{6,2},{1... | collective-permute-start | bytes 294920 | tf_op jit(solution)/shard_map/ppermute | solution.py:19
  12.8 6.1 %collective-permute-start.7 = (bf16[128,384]{1,0:T(8,128)(2,1)S(1)}, bf16[128,384]{1,0:T(8,128)(2,1)S(1)}, u32[]{:S(2)}, u32[]{:S(2)}) collective-permute-start(bf16[128,384]{1,0:T(8,128)(2,1)S(1)} %constant_dynamic-update-slice_fusion.refs_6_), channel_id=1, source_target_pairs={{0,8},{4,12},{8,0},{12,4},{1,9},{5,13},{9,1},{13,5},{2,10},{6,14},... | collective-permute-start | bytes 294920 | tf_op jit(solution)/shard_map/ppermute | solution.py:19
  15.4 5.9 %collective-permute-start.3 = (bf16[288,384]{1,0:T(8,128)(2,1)S(1)}, bf16[288,384]{1,0:T(8,128)(2,1)S(1)}, u32[]{:S(2)}, u32[]{:S(2)}) collective-permute-start(bf16[288,384]{1,0:T(8,128)(2,1)S(1)} %pad_maximum_fusion.refs_2_), channel_id=1, source_target_pairs={{0,4},{4,0},{8,12},{12,8},{1,5},{5,1},{9,13},{13,9},{2,6},{6,2},{1... | collective-permute-start | bytes 663560 | tf_op jit(solution)/shard_map/ppermute | solution.py:19
  18.2 7.0 %collective-permute-start.14 = (bf16[160,384]{1,0:T(8,128)(2,1)S(1)}, bf16[160,384]{1,0:T(8,128)(2,1)S(1)}, u32[]{:S(2)}, u32[]{:S(2)}) collective-permute-start(bf16[160,384]{1,0:T(8,128)(2,1)S(1)} %collective-permute-done.11), channel_id=1, source_target_pairs={{0,1},{1,0},{2,3},{3,2},{4,5},{5,4},{6,7},{7,6},{8,9},{9,8},{10,11... | collective-permute-start | bytes 368648 | tf_op jit(solution)/shard_map/ppermute | solution.py:19
  18.9 2.4 %collective-permute-start.9 = (bf16[128,384]{1,0:T(8,128)(2,1)S(1)}, bf16[128,384]{1,0:T(8,128)(2,1)S(1)}, u32[]{:S(2)}, u32[]{:S(2)}) collective-permute-start(bf16[128,384]{1,0:T(8,128)(2,1)S(1)} %collective-permute-done.7.refs_7_), channel_id=1, source_target_pairs={{0,4},{4,0},{8,12},{12,8},{1,5},{5,1},{9,13},{13,9},{2,6},{6,2},{1... | collective-permute-start | bytes 294920 | tf_op jit(solution)/shard_map/ppermute | solution.py:19
  18.9 2.4 %collective-permute-start.4 = (bf16[288,384]{1,0:T(8,128)(2,1)S(1)}, bf16[288,384]{1,0:T(8,128)(2,1)S(1)}, u32[]{:S(2)}, u32[]{:S(2)}) collective-permute-start(bf16[288,384]{1,0:T(8,128)(2,1)S(1)} %collective-permute-done.2.refs_3_.refs_4_), channel_id=1, source_target_pairs={{0,4},{4,0},{8,12},{12,8},{1,5},{5,1},{9,13},{13,9},{2,6},{6,2},{1... | collective-permute-start | bytes 663560 | tf_op jit(solution)/shard_map/ppermute | solution.py:19
  19.4 12.0 %copy-start = (bf16[64,2560]{1,0:T(8,128)(2,1)S(1)}, bf16[64,2560]{1,0:T(8,128)(2,1)}, u32[]{:S(2)}) copy-start(bf16[64,2560]{1,0:T(8,128)(2,1)} %refs_4_.1) | copy-start | bytes 983044
  19.5 8.5 %collective-permute-start.13 = (bf16[320,384]{1,0:T(8,128)(2,1)S(1)}, bf16[320,384]{1,0:T(8,128)(2,1)S(1)}, u32[]{:S(2)}, u32[]{:S(2)}) collective-permute-start(bf16[320,384]{1,0:T(8,128)(2,1)S(1)} %constant_dynamic-update-slice_fusion.2.refs_6_), channel_id=1, source_target_pairs={{0,8},{4,12},{8,0},{12,4},{1,9},{5,13},{9,1},{13,5},{2,10},{6,14},... | collective-permute-start | bytes 737288 | tf_op jit(solution)/shard_map/ppermute | solution.py:19
  21.3 0.8 %copy-start.1 = (bf16[64,384]{1,0:T(8,128)(2,1)S(1)}, bf16[64,384]{1,0:T(8,128)(2,1)}, u32[]{:S(2)}) copy-start(bf16[64,384]{1,0:T(8,128)(2,1)} %refs_0_.1) | copy-start | bytes 147460
  23.5 4.3 %collective-permute-start.10 = (f16[64,512]{1,0:T(8,128)(2,1)S(1)}, f16[64,512]{1,0:T(8,128)(2,1)S(1)}, u32[]{:S(2)}, u32[]{:S(2)}) collective-permute-start(f16[64,512]{1,0:T(8,128)(2,1)S(1)} %slice_convert_fusion), channel_id=1, source_target_pairs={{0,1},{1,0},{2,3},{3,2},{4,5},{5,4},{6,7},{7,6},{8,9},{9,8},{10,11... | collective-permute-start | bytes 196616 | tf_op jit(solution)/shard_map/ppermute | solution.py:19
  25.2 4.9 %collective-permute-start.15 = (bf16[160,384]{1,0:T(8,128)(2,1)S(1)}, bf16[160,384]{1,0:T(8,128)(2,1)S(1)}, u32[]{:S(2)}, u32[]{:S(2)}) collective-permute-start(bf16[160,384]{1,0:T(8,128)(2,1)S(1)} %collective-permute-done.14.refs_8_), channel_id=1, source_target_pairs={{0,8},{4,12},{8,0},{12,4},{1,9},{5,13},{9,1},{13,5},{2,10},{6,14},... | collective-permute-start | bytes 368648 | tf_op jit(solution)/shard_map/ppermute | solution.py:19
  27.9 3.5 %collective-permute-start.16 = (bf16[320,384]{1,0:T(8,128)(2,1)S(1)}, bf16[320,384]{1,0:T(8,128)(2,1)S(1)}, u32[]{:S(2)}, u32[]{:S(2)}) collective-permute-start(bf16[320,384]{1,0:T(8,128)(2,1)S(1)} %constant_dynamic-update-slice_fusion.2.refs_6_), channel_id=1, source_target_pairs={{0,4},{4,0},{8,12},{12,8},{1,5},{5,1},{9,13},{13,9},{2,6},{6,2},{1... | collective-permute-start | bytes 737288 | tf_op jit(solution)/shard_map/ppermute | solution.py:19
  28.0 3.5 %collective-permute-start.17 = (bf16[320,384]{1,0:T(8,128)(2,1)S(1)}, bf16[320,384]{1,0:T(8,128)(2,1)S(1)}, u32[]{:S(2)}, u32[]{:S(2)}) collective-permute-start(bf16[320,384]{1,0:T(8,128)(2,1)S(1)} %collective-permute-done.13.refs_7_), channel_id=1, source_target_pairs={{0,4},{4,0},{8,12},{12,8},{1,5},{5,1},{9,13},{13,9},{2,6},{6,2},{1... | collective-permute-start | bytes 737288 | tf_op jit(solution)/shard_map/ppermute | solution.py:19
  28.5 2.0 %collective-permute-start.18 = (bf16[160,384]{1,0:T(8,128)(2,1)S(1)}, bf16[160,384]{1,0:T(8,128)(2,1)S(1)}, u32[]{:S(2)}, u32[]{:S(2)}) collective-permute-start(bf16[160,384]{1,0:T(8,128)(2,1)S(1)} %collective-permute-done.14.refs_8_), channel_id=1, source_target_pairs={{0,4},{4,0},{8,12},{12,8},{1,5},{5,1},{9,13},{13,9},{2,6},{6,2},{1... | collective-permute-start | bytes 368648 | tf_op jit(solution)/shard_map/ppermute | solution.py:19
  30.1 1.3 %collective-permute-start.19 = (bf16[160,384]{1,0:T(8,128)(2,1)S(1)}, bf16[160,384]{1,0:T(8,128)(2,1)S(1)}, u32[]{:S(2)}, u32[]{:S(2)}) collective-permute-start(bf16[160,384]{1,0:T(8,128)(2,1)S(1)} %collective-permute-done.15.refs_9_), channel_id=1, source_target_pairs={{0,4},{4,0},{8,12},{12,8},{1,5},{5,1},{9,13},{13,9},{2,6},{6,2},{1... | collective-permute-start | bytes 368648 | tf_op jit(solution)/shard_map/ppermute | solution.py:19

commit v5 on v4

--- a/solution.py
+++ b/solution.py
@@ -30,13 +30,17 @@
     return (high, middle, rest - middle)
 
 
-def attend_kernel(q_masks, k_masks, per_tile, mask_shape, place_ref, *refs):
+def attend_kernel(q_masks, k_masks, per_tile, seen_ref, *refs):
     nq, nk = len(q_masks), len(k_masks)
     q_refs, kv_refs, out_ref = refs[:nq], refs[nq : nq + nk], refs[-1]
     rows, width = q_refs[0].shape
     heads = width // HD
     scale = 1.0 / math.sqrt(HD)
-    my_row, my_col = place_ref[0], place_ref[1]
+    my_row, my_col = lax.axis_index("row"), lax.axis_index("col")
+    visible = seen_ref[...]
+    far_rows = seen_ref.shape[0] // 2
+    q_line = lax.broadcasted_iota(jnp.int32, seen_ref.shape, 0)
+    k_line = lax.broadcasted_iota(jnp.int32, seen_ref.shape, 1)
     keys = nk * rows
     piece_of_lane = lax.broadcasted_iota(jnp.int32, (1, keys), 1) // rows
     group = min(nq, 4)
@@ -49,10 +53,9 @@
             line = jnp.zeros((1, keys), jnp.float32)
             for j, (a, b) in enumerate(k_masks):
                 k_block = ((my_row ^ a) * rows) // BLK
-                at = 2 + q_block * mask_shape[1] + k_block
-                if b:
-                    at += mask_shape[0] * mask_shape[1]
-                hidden = jnp.where(place_ref[at] == 1, 0.0, -jnp.inf)
+                here = (q_line == q_block + (far_rows if b else 0)) & (k_line == k_block)
+                seen = jnp.sum(jnp.where(here, visible, 0.0), axis=(0, 1), keepdims=True)
+                hidden = jnp.where(seen > 0.5, 0.0, -jnp.inf)
                 line = jnp.where(piece_of_lane == j, hidden, line)
             lines.append(jnp.broadcast_to(line, (rows, keys)))
         bias = jnp.concatenate(lines, axis=0)
@@ -84,19 +87,18 @@
         out_ref[here, width:] = stats
 
 
-def attend(place, mask_shape, per_tile, q_parts, kv_parts):
+def attend(masks, per_tile, q_parts, kv_parts):
     q_masks, k_masks = tuple(q_parts), tuple(kv_parts)
     rows, width = q_parts[0].shape
-    smem = pl.BlockSpec(memory_space=pltpu.SMEM)
     vmem = pl.BlockSpec(memory_space=pltpu.VMEM)
     arrays = [*q_parts.values(), *kv_parts.values()]
     return pl.pallas_call(
-        functools.partial(attend_kernel, q_masks, k_masks, per_tile, mask_shape),
+        functools.partial(attend_kernel, q_masks, k_masks, per_tile),
         out_shape=jax.ShapeDtypeStruct((len(q_masks) * rows, width + LANES), jnp.float32),
-        in_specs=[smem] + [vmem] * len(arrays),
+        in_specs=[vmem] * (1 + len(arrays)),
         out_specs=vmem,
         compiler_params=pltpu.CompilerParams(vmem_limit_bytes=24 * 2**20),
-    )(place, *arrays)
+    )(masks, *arrays)
 
 
 def merge(parts):
@@ -167,7 +169,6 @@
     chips = range(2, n_row, 2)
     rows, depth = queries.shape[0], out_weight.shape[1]
     ride = depth % 16 == 0
-    where = jnp.stack([lax.axis_index("row"), lax.axis_index("col")]).astype(jnp.int32)
     weight = out_weight.T
 
     pack = jnp.concatenate([keys, values, weight] if ride else [keys, values])
@@ -185,15 +186,14 @@
         kv_parts[a, 0] = swap(pack, "row", a)
     for a in (0, *chips):
         kv_parts[a | 1, 0] = swap(kv_parts[a, 0], "row", 1)
-    masks = [where, block_mask.reshape(-1)]
+    masks = jnp.concatenate([block_mask, far_mask if top else block_mask]).astype(jnp.float32)
     if top:
         kv_parts[0, top] = jnp.concatenate([after(far_k, *gate), far_v])
         for a in chips:
             kv_parts[a, top] = swap(kv_parts[0, top], "row", a)
         for a in (0, *chips):
             kv_parts[a | 1, top] = swap(kv_parts[a, top], "row", 1)
-        masks.append(far_mask.reshape(-1))
-    partial = attend(jnp.concatenate(masks), block_mask.shape, n_row, q_parts, kv_parts)
+    partial = attend(masks, n_row, q_parts, kv_parts)
 
     parts = [partial]
     for n, m in enumerate(near, 1):

time: 33.2 us -> 32.7 us (0.985)
  local copies, waits for them, and re-layouts: 1.69 us -> 0.85 us
  waiting for transfers between devices: 8.5 us -> 9.31 us
  other arithmetic: 1.06 us -> 1.67 us
  Pallas kernels: 3.35 us -> 2.82 us
  starting transfers between devices: 18.3 us -> 17.8 us
    reshape x2 -> x0, local copies, waits for them, and re-layouts: 0.84 us -> none  [the longest x1 0.76 us: local(): masks = [where, block_mask.reshape(-1)]]
    ppermute x20, waiting for transfers between devices: 8.5 us -> 9.31 us  [swap(): lax.ppermute(x, axis, [(i, i ^ mask) for i in range(lax.axis_size(axis))])]
    convert_element_type x0 -> x1, other arithmetic: none -> 0.69 us  [local(): jnp.concatenate([block_mask, far_mask if top else block_mask])]
    ppermute x20, starting transfers between devices: 18.3 us -> 17.8 us  [swap(): lax.ppermute(x, axis, [(i, i ^ mask) for i in range(lax.axis_size(axis))])]
    pallas_call x1, Pallas kernels: 1.37 us -> 0.84 us  [attend(): pl.pallas_call(functools.partial(attend_kernel, q_masks, k_masks, per_til...]
  transfers between devices with their start and end apart: 20 -> 20, of which waited for: 7 -> 9; matrix products, arithmetic and copies ran while one was open for 6% -> 5% of each run, Pallas kernels for 5% -> 4%
where the time goes in v5:
time: 32.7 us; the launch traced here: 32.5 us
  starting transfers between devices  17.8 us (54%)
  waiting for transfers between devices  9.31 us (28%)
  Pallas kernels  2.82 us (9%)
  other arithmetic  1.67 us (5%)
  local copies, waits for them, and re-layouts  0.85 us (3%)
    ppermute x20, starting transfers between devices, swap(): lax.ppermute(x, axis, [(i, i ^ mask) for i in range(lax.axis_size(axis))])  17.8 us
    ppermute x20, waiting for transfers between devices, swap(): lax.ppermute(x, axis, [(i, i ^ mask) for i in range(lax.axis_size(axis))])  9.31 us
    pallas_call x2, Pallas kernels, call(): pl.pallas_call(kernel, out_shape=shapes, in_specs=[vmem] * len(arrays), o...  1.97 us
    concatenate x1, other arithmetic, local(): pack = jnp.concatenate([keys, values, weight] if ride else [keys, values])  0.96 us
    pallas_call x1, Pallas kernels, attend(): pl.pallas_call(functools.partial(attend_kernel, q_masks, k_masks, per_til...  0.84 us
    unnamed x6, local copies, waits for them, and re-layouts  0.82 us
    convert_element_type x1, other arithmetic, local(): jnp.concatenate([block_mask, far_mask if top else block_mask])  0.69 us
  transfers between devices with their start and end apart: 20, of which 9 were waited for; matrix products, arithmetic and copies ran while one was open for 5% of the time, Pallas kernels for 4%

profile of v5, /device:TPU:0, one launch (start us, length us, event | category | flops | bytes accessed | tf_op | source)
XLA Modules:
  0.0 32.5 jit_solution(18265581745130026221)
XLA Ops:
  0.0 4.0 %collective-permute-start = (s32[2,2]{1,0:T(2,128)}, s32[2,2]{1,0:T(2,128)S(1)}, u32[]{:S(2)}, u32[]{:S(2)}) collective-permute-start(s32[2,2]{1,0:T(2,128)} %param.9), channel_id=1, source_target_pairs={{0,2},{1,3},{2,0},{3,1},{4,6},{5,7},{6,4},{7,5},{8,10},{9,11},{10,... | collective-permute-start | bytes 56 | tf_op jit(solution)/shard_map/ppermute | solution.py:19
  4.0 1.6 %collective-permute-start.1 = (bf16[64,384]{1,0:T(8,128)(2,1)}, bf16[64,384]{1,0:T(8,128)(2,1)S(1)}, u32[]{:S(2)}, u32[]{:S(2)}) collective-permute-start(bf16[64,384]{1,0:T(8,128)(2,1)} %refs_0_.1), channel_id=1, source_target_pairs={{0,1},{1,0},{2,3},{3,2},{4,5},{5,4},{6,7},{7,6},{8,9},{9,8},{10,11... | collective-permute-start | bytes 147464 | tf_op jit(solution)/shard_map/ppermute | solution.py:19
  6.0 2.6 %collective-permute-start.6 = (bf16[64,384]{1,0:T(8,128)(2,1)}, bf16[64,384]{1,0:T(8,128)(2,1)S(1)}, u32[]{:S(2)}, u32[]{:S(2)}) collective-permute-start(bf16[64,384]{1,0:T(8,128)(2,1)} %param.8), channel_id=1, source_target_pairs={{0,2},{1,3},{2,0},{3,1},{4,6},{5,7},{6,4},{7,5},{8,10},{9,11},{10,... | collective-permute-start | bytes 147464 | tf_op jit(solution)/shard_map/ppermute | solution.py:19
  8.5 0.4 %collective-permute-start.12 = (bf16[160,384]{1,0:T(8,128)(2,1)}, bf16[160,384]{1,0:T(8,128)(2,1)S(1)}, u32[]{:S(2)}, u32[]{:S(2)}) collective-permute-start(bf16[160,384]{1,0:T(8,128)(2,1)} %bitcast.1), channel_id=1, source_target_pairs={{0,1},{1,0},{2,3},{3,2},{4,5},{5,4},{6,7},{7,6},{8,9},{9,8},{10,11... | collective-permute-start | bytes 368648 | tf_op jit(solution)/shard_map/ppermute | solution.py:19
  9.0 1.0 %pad_maximum_fusion.refs_2_ = bf16[288,384]{1,0:T(8,128)(2,1)S(1)} fusion(bf16[160,384]{1,0:T(8,128)(2,1)} %bitcast.2, bf16[64,384]{1,0:T(8,128)(2,1)} %param.8, bf16[64,384]{1,0:T(8,128)(2,1)} %param.7), kind=kLoop, calls=%fused_computation | loop fusion | flops 663552 | bytes 442368 | tf_op jit(solution)/shard_map/concatenate | solution.py:174
  10.1 1.8 %collective-permute-start.2 = (bf16[288,384]{1,0:T(8,128)(2,1)S(1)}, bf16[288,384]{1,0:T(8,128)(2,1)S(1)}, u32[]{:S(2)}, u32[]{:S(2)}) collective-permute-start(bf16[288,384]{1,0:T(8,128)(2,1)S(1)} %pad_maximum_fusion.refs_2_), channel_id=1, source_target_pairs={{0,8},{4,12},{8,0},{12,4},{1,9},{5,13},{9,1},{13,5},{2,10},{6,14},... | collective-permute-start | bytes 663560 | tf_op jit(solution)/shard_map/ppermute | solution.py:19
  12.1 1.1 %collective-permute-done.6 = bf16[64,384]{1,0:T(8,128)(2,1)S(1)} collective-permute-done((bf16[64,384]{1,0:T(8,128)(2,1)}, bf16[64,384]{1,0:T(8,128)(2,1)S(1)}, u32[]{:S(2)}, u32[]{:S(2)}) %collective-permute-start.6) | collective-permute-done | bytes 49184 | tf_op jit(solution)/shard_map/ppermute | solution.py:19
  13.2 1.6 %collective-permute-start.7 = (bf16[128,384]{1,0:T(8,128)(2,1)S(1)}, bf16[128,384]{1,0:T(8,128)(2,1)S(1)}, u32[]{:S(2)}, u32[]{:S(2)}) collective-permute-start(bf16[128,384]{1,0:T(8,128)(2,1)S(1)} %constant_dynamic-update-slice_fusion.refs_6_), channel_id=1, source_target_pairs={{0,8},{4,12},{8,0},{12,4},{1,9},{5,13},{9,1},{13,5},{2,10},{6,14},... | collective-permute-start | bytes 294920 | tf_op jit(solution)/shard_map/ppermute | solution.py:19
  14.8 0.7 %add_convert_fusion.seen_ref = f32[4,2]{1,0:T(4,128)S(1)} fusion(s32[2,2]{1,0:T(2,128)S(1)} %collective-permute-done, s32[2,2]{1,0:T(2,128)} %param.9), kind=kLoop, calls=%fused_computation.6 | loop fusion | flops 16 | bytes 64 | tf_op jit(solution)/shard_map/convert_element_type | solution.py:189
  15.5 0.6 %collective-permute-done.12 = bf16[160,384]{1,0:T(8,128)(2,1)S(1)} collective-permute-done((bf16[160,384]{1,0:T(8,128)(2,1)}, bf16[160,384]{1,0:T(8,128)(2,1)S(1)}, u32[]{:S(2)}, u32[]{:S(2)}) %collective-permute-start.12) | collective-permute-done | bytes 122912 | tf_op jit(solution)/shard_map/ppermute | solution.py:19
  16.1 1.9 %collective-permute-done.11 = bf16[160,384]{1,0:T(8,128)(2,1)S(1)} collective-permute-done((bf16[160,384]{1,0:T(8,128)(2,1)}, bf16[160,384]{1,0:T(8,128)(2,1)S(1)}, u32[]{:S(2)}, u32[]{:S(2)}) %collective-permute-start.11) | collective-permute-done | bytes 122912 | tf_op jit(solution)/shard_map/ppermute | solution.py:19
  18.0 0.5 %collective-permute-done.7.refs_7_ = bf16[128,384]{1,0:T(8,128)(2,1)S(1)} collective-permute-done((bf16[128,384]{1,0:T(8,128)(2,1)S(1)}, bf16[128,384]{1,0:T(8,128)(2,1)S(1)}, u32[]{:S(2)}, u32[]{:S(2)}) %collective-permute-start.7) | collective-permute-done | bytes 98336 | tf_op jit(solution)/shard_map/ppermute | solution.py:19
  18.4 0.5 %collective-permute-start.4 = (bf16[288,384]{1,0:T(8,128)(2,1)S(1)}, bf16[288,384]{1,0:T(8,128)(2,1)S(1)}, u32[]{:S(2)}, u32[]{:S(2)}) collective-permute-start(bf16[288,384]{1,0:T(8,128)(2,1)S(1)} %collective-permute-done.2.refs_3_.refs_4_), channel_id=1, source_target_pairs={{0,4},{4,0},{8,12},{12,8},{1,5},{5,1},{9,13},{13,9},{2,6},{6,2},{1... | collective-permute-start | bytes 663560 | tf_op jit(solution)/shard_map/ppermute | solution.py:19
  19.0 1.6 %collective-permute-start.13 = (bf16[320,384]{1,0:T(8,128)(2,1)S(1)}, bf16[320,384]{1,0:T(8,128)(2,1)S(1)}, u32[]{:S(2)}, u32[]{:S(2)}) collective-permute-start(bf16[320,384]{1,0:T(8,128)(2,1)S(1)} %constant_dynamic-update-slice_fusion.2.refs_6_), channel_id=1, source_target_pairs={{0,8},{4,12},{8,0},{12,4},{1,9},{5,13},{9,1},{13,5},{2,10},{6,14},... | collective-permute-start | bytes 737288 | tf_op jit(solution)/shard_map/ppermute | solution.py:19
  20.6 0.8 %copy-done.1 = bf16[64,384]{1,0:T(8,128)(2,1)S(1)} copy-done((bf16[64,384]{1,0:T(8,128)(2,1)S(1)}, bf16[64,384]{1,0:T(8,128)(2,1)}, u32[]{:S(2)}) %copy-start.1) | copy-done | bytes 49176
  21.4 0.8 %shard_map.64.refs_0_ = f32[128,512]{1,0:T(8,128)S(1)} custom-call(f32[4,2]{1,0:T(4,128)S(1)} %add_convert_fusion.seen_ref, bf16[64,384]{1,0:T(8,128)(2,1)S(1)} %copy-done.1, bf16[64,384]{1,0:T(8,128)(2,1)S(1)} %collective-permute-done.1.refs_1_, bf16[288,384]{1,0:T(8,128)(2,1)S(1)} %pad_maximum_fusion.refs_2_, ...), custom_call_target="tpu_custom_call" | custom-call | tf_op jit(solution)/shard_map/pallas_call | solution.py:95
  22.2 1.6 %collective-permute-start.10 = (f16[64,512]{1,0:T(8,128)(2,1)S(1)}, f16[64,512]{1,0:T(8,128)(2,1)S(1)}, u32[]{:S(2)}, u32[]{:S(2)}) collective-permute-start(f16[64,512]{1,0:T(8,128)(2,1)S(1)} %slice_convert_fusion), channel_id=1, source_target_pairs={{0,1},{1,0},{2,3},{3,2},{4,5},{5,4},{6,7},{7,6},{8,9},{9,8},{10,11... | collective-permute-start | bytes 196616 | tf_op jit(solution)/shard_map/ppermute | solution.py:19
  23.9 1.0 %collective-permute-start.15 = (bf16[160,384]{1,0:T(8,128)(2,1)S(1)}, bf16[160,384]{1,0:T(8,128)(2,1)S(1)}, u32[]{:S(2)}, u32[]{:S(2)}) collective-permute-start(bf16[160,384]{1,0:T(8,128)(2,1)S(1)} %collective-permute-done.14.refs_8_), channel_id=1, source_target_pairs={{0,8},{4,12},{8,0},{12,4},{1,9},{5,13},{9,1},{13,5},{2,10},{6,14},... | collective-permute-start | bytes 368648 | tf_op jit(solution)/shard_map/ppermute | solution.py:19
  24.9 1.7 %collective-permute-done.10 = f16[64,512]{1,0:T(8,128)(2,1)S(1)} collective-permute-done((f16[64,512]{1,0:T(8,128)(2,1)S(1)}, f16[64,512]{1,0:T(8,128)(2,1)S(1)}, u32[]{:S(2)}, u32[]{:S(2)}) %collective-permute-start.10) | collective-permute-done | bytes 65568 | tf_op jit(solution)/shard_map/ppermute | solution.py:19
  26.7 1.1 %collective-permute-done.13.refs_7_ = bf16[320,384]{1,0:T(8,128)(2,1)S(1)} collective-permute-done((bf16[320,384]{1,0:T(8,128)(2,1)S(1)}, bf16[320,384]{1,0:T(8,128)(2,1)S(1)}, u32[]{:S(2)}, u32[]{:S(2)}) %collective-permute-start.13) | collective-permute-done | bytes 245792 | tf_op jit(solution)/shard_map/ppermute | solution.py:19
  27.8 0.5 %collective-permute-start.18 = (bf16[160,384]{1,0:T(8,128)(2,1)S(1)}, bf16[160,384]{1,0:T(8,128)(2,1)S(1)}, u32[]{:S(2)}, u32[]{:S(2)}) collective-permute-start(bf16[160,384]{1,0:T(8,128)(2,1)S(1)} %collective-permute-done.14.refs_8_), channel_id=1, source_target_pairs={{0,4},{4,0},{8,12},{12,8},{1,5},{5,1},{9,13},{13,9},{2,6},{6,2},{1... | collective-permute-start | bytes 368648 | tf_op jit(solution)/shard_map/ppermute | solution.py:19
  28.3 1.3 %collective-permute-done.15.refs_9_ = bf16[160,384]{1,0:T(8,128)(2,1)S(1)} collective-permute-done((bf16[160,384]{1,0:T(8,128)(2,1)S(1)}, bf16[160,384]{1,0:T(8,128)(2,1)S(1)}, u32[]{:S(2)}, u32[]{:S(2)}) %collective-permute-start.15) | collective-permute-done | bytes 122912 | tf_op jit(solution)/shard_map/ppermute | solution.py:19
  30.0 1.0 %collective-permute-done.19.refs_3_ = bf16[160,384]{1,0:T(8,128)(2,1)S(1)} collective-permute-done((bf16[160,384]{1,0:T(8,128)(2,1)S(1)}, bf16[160,384]{1,0:T(8,128)(2,1)S(1)}, u32[]{:S(2)}, u32[]{:S(2)}) %collective-permute-start.19) | collective-permute-done | bytes 122912 | tf_op jit(solution)/shard_map/ppermute | solution.py:19
  30.9 1.6 %shard_map.66 = (bf16[64,2560]{1,0:T(8,128)(2,1)}, bf16[2560,384]{1,0:T(8,128)(2,1)S(1)}) custom-call(bf16[2560,384]{1,0:T(8,128)(2,1)S(1)} %get-tuple-element.20.begun_ref, bf16[64,384]{1,0:T(8,128)(2,1)S(1)} %get-tuple-element.21.attended_ref, bf16[320,384]{1,0:T(8,128)(2,1)S(1)} %collective-permute-done.16.refs_0_, ...), custom_call_target="tpu_custom_call", output_to_operand_aliasing={{1}: (0, {})} | custom-call | tf_op jit(solution)/shard_map/pallas_call | solution.py:155
  (31 shorter events, 1.3 us)
Async XLA Ops:
  0.0 10.0 %collective-permute-start = (s32[2,2]{1,0:T(2,128)}, s32[2,2]{1,0:T(2,128)S(1)}, u32[]{:S(2)}, u32[]{:S(2)}) collective-permute-start(s32[2,2]{1,0:T(2,128)} %param.9), channel_id=1, source_target_pairs={{0,2},{1,3},{2,0},{3,1},{4,6},{5,7},{6,4},{7,5},{8,10},{9,11},{10,... | collective-permute-start | bytes 56 | tf_op jit(solution)/shard_map/ppermute | solution.py:19
  4.0 6.0 %collective-permute-start.1 = (bf16[64,384]{1,0:T(8,128)(2,1)}, bf16[64,384]{1,0:T(8,128)(2,1)S(1)}, u32[]{:S(2)}, u32[]{:S(2)}) collective-permute-start(bf16[64,384]{1,0:T(8,128)(2,1)} %refs_0_.1), channel_id=1, source_target_pairs={{0,1},{1,0},{2,3},{3,2},{4,5},{5,4},{6,7},{7,6},{8,9},{9,8},{10,11... | collective-permute-start | bytes 147464 | tf_op jit(solution)/shard_map/ppermute | solution.py:19
  5.6 6.4 %collective-permute-start.5 = (bf16[64,384]{1,0:T(8,128)(2,1)}, bf16[64,384]{1,0:T(8,128)(2,1)S(1)}, u32[]{:S(2)}, u32[]{:S(2)}) collective-permute-start(bf16[64,384]{1,0:T(8,128)(2,1)} %param.7), channel_id=1, source_target_pairs={{0,2},{1,3},{2,0},{3,1},{4,6},{5,7},{6,4},{7,5},{8,10},{9,11},{10,... | collective-permute-start | bytes 147464 | tf_op jit(solution)/shard_map/ppermute | solution.py:19
  6.0 7.2 %collective-permute-start.6 = (bf16[64,384]{1,0:T(8,128)(2,1)}, bf16[64,384]{1,0:T(8,128)(2,1)S(1)}, u32[]{:S(2)}, u32[]{:S(2)}) collective-permute-start(bf16[64,384]{1,0:T(8,128)(2,1)} %param.8), channel_id=1, source_target_pairs={{0,2},{1,3},{2,0},{3,1},{4,6},{5,7},{6,4},{7,5},{8,10},{9,11},{10,... | collective-permute-start | bytes 147464 | tf_op jit(solution)/shard_map/ppermute | solution.py:19
  8.5 7.5 %collective-permute-start.12 = (bf16[160,384]{1,0:T(8,128)(2,1)}, bf16[160,384]{1,0:T(8,128)(2,1)S(1)}, u32[]{:S(2)}, u32[]{:S(2)}) collective-permute-start(bf16[160,384]{1,0:T(8,128)(2,1)} %bitcast.1), channel_id=1, source_target_pairs={{0,1},{1,0},{2,3},{3,2},{4,5},{5,4},{6,7},{7,6},{8,9},{9,8},{10,11... | collective-permute-start | bytes 368648 | tf_op jit(solution)/shard_map/ppermute | solution.py:19
  10.0 8.0 %collective-permute-start.11 = (bf16[160,384]{1,0:T(8,128)(2,1)}, bf16[160,384]{1,0:T(8,128)(2,1)S(1)}, u32[]{:S(2)}, u32[]{:S(2)}) collective-permute-start(bf16[160,384]{1,0:T(8,128)(2,1)} %bitcast.3), channel_id=1, source_target_pairs={{0,2},{1,3},{2,0},{3,1},{4,6},{5,7},{6,4},{7,5},{8,10},{9,11},{10,... | collective-permute-start | bytes 368648 | tf_op jit(solution)/shard_map/ppermute | solution.py:19
  10.1 8.4 %collective-permute-start.2 = (bf16[288,384]{1,0:T(8,128)(2,1)S(1)}, bf16[288,384]{1,0:T(8,128)(2,1)S(1)}, u32[]{:S(2)}, u32[]{:S(2)}) collective-permute-start(bf16[288,384]{1,0:T(8,128)(2,1)S(1)} %pad_maximum_fusion.refs_2_), channel_id=1, source_target_pairs={{0,8},{4,12},{8,0},{12,4},{1,9},{5,13},{9,1},{13,5},{2,10},{6,14},... | collective-permute-start | bytes 663560 | tf_op jit(solution)/shard_map/ppermute | solution.py:19
  13.1 2.9 %collective-permute-start.8 = (bf16[128,384]{1,0:T(8,128)(2,1)S(1)}, bf16[128,384]{1,0:T(8,128)(2,1)S(1)}, u32[]{:S(2)}, u32[]{:S(2)}) collective-permute-start(bf16[128,384]{1,0:T(8,128)(2,1)S(1)} %constant_dynamic-update-slice_fusion.refs_6_), channel_id=1, source_target_pairs={{0,4},{4,0},{8,12},{12,8},{1,5},{5,1},{9,13},{13,9},{2,6},{6,2},{1... | collective-permute-start | bytes 294920 | tf_op jit(solution)/shard_map/ppermute | solution.py:19
  13.2 5.2 %collective-permute-start.7 = (bf16[128,384]{1,0:T(8,128)(2,1)S(1)}, bf16[128,384]{1,0:T(8,128)(2,1)S(1)}, u32[]{:S(2)}, u32[]{:S(2)}) collective-permute-start(bf16[128,384]{1,0:T(8,128)(2,1)S(1)} %constant_dynamic-update-slice_fusion.refs_6_), channel_id=1, source_target_pairs={{0,8},{4,12},{8,0},{12,4},{1,9},{5,13},{9,1},{13,5},{2,10},{6,14},... | collective-permute-start | bytes 294920 | tf_op jit(solution)/shard_map/ppermute | solution.py:19
  16.1 4.5 %collective-permute-start.3 = (bf16[288,384]{1,0:T(8,128)(2,1)S(1)}, bf16[288,384]{1,0:T(8,128)(2,1)S(1)}, u32[]{:S(2)}, u32[]{:S(2)}) collective-permute-start(bf16[288,384]{1,0:T(8,128)(2,1)S(1)} %pad_maximum_fusion.refs_2_), channel_id=1, source_target_pairs={{0,4},{4,0},{8,12},{12,8},{1,5},{5,1},{9,13},{13,9},{2,6},{6,2},{1... | collective-permute-start | bytes 663560 | tf_op jit(solution)/shard_map/ppermute | solution.py:19
  18.0 5.9 %collective-permute-start.14 = (bf16[160,384]{1,0:T(8,128)(2,1)S(1)}, bf16[160,384]{1,0:T(8,128)(2,1)S(1)}, u32[]{:S(2)}, u32[]{:S(2)}) collective-permute-start(bf16[160,384]{1,0:T(8,128)(2,1)S(1)} %collective-permute-done.11), channel_id=1, source_target_pairs={{0,1},{1,0},{2,3},{3,2},{4,5},{5,4},{6,7},{7,6},{8,9},{9,8},{10,11... | collective-permute-start | bytes 368648 | tf_op jit(solution)/shard_map/ppermute | solution.py:19
  18.4 2.1 %collective-permute-start.9 = (bf16[128,384]{1,0:T(8,128)(2,1)S(1)}, bf16[128,384]{1,0:T(8,128)(2,1)S(1)}, u32[]{:S(2)}, u32[]{:S(2)}) collective-permute-start(bf16[128,384]{1,0:T(8,128)(2,1)S(1)} %collective-permute-done.7.refs_7_), channel_id=1, source_target_pairs={{0,4},{4,0},{8,12},{12,8},{1,5},{5,1},{9,13},{13,9},{2,6},{6,2},{1... | collective-permute-start | bytes 294920 | tf_op jit(solution)/shard_map/ppermute | solution.py:19
  18.4 2.1 %collective-permute-start.4 = (bf16[288,384]{1,0:T(8,128)(2,1)S(1)}, bf16[288,384]{1,0:T(8,128)(2,1)S(1)}, u32[]{:S(2)}, u32[]{:S(2)}) collective-permute-start(bf16[288,384]{1,0:T(8,128)(2,1)S(1)} %collective-permute-done.2.refs_3_.refs_4_), channel_id=1, source_target_pairs={{0,4},{4,0},{8,12},{12,8},{1,5},{5,1},{9,13},{13,9},{2,6},{6,2},{1... | collective-permute-start | bytes 663560 | tf_op jit(solution)/shard_map/ppermute | solution.py:19
  19.0 11.9 %copy-start = (bf16[64,2560]{1,0:T(8,128)(2,1)S(1)}, bf16[64,2560]{1,0:T(8,128)(2,1)}, u32[]{:S(2)}) copy-start(bf16[64,2560]{1,0:T(8,128)(2,1)} %refs_4_.1) | copy-start | bytes 983044
  19.0 8.8 %collective-permute-start.13 = (bf16[320,384]{1,0:T(8,128)(2,1)S(1)}, bf16[320,384]{1,0:T(8,128)(2,1)S(1)}, u32[]{:S(2)}, u32[]{:S(2)}) collective-permute-start(bf16[320,384]{1,0:T(8,128)(2,1)S(1)} %constant_dynamic-update-slice_fusion.2.refs_6_), channel_id=1, source_target_pairs={{0,8},{4,12},{8,0},{12,4},{1,9},{5,13},{9,1},{13,5},{2,10},{6,14},... | collective-permute-start | bytes 737288 | tf_op jit(solution)/shard_map/ppermute | solution.py:19
  20.6 0.8 %copy-start.1 = (bf16[64,384]{1,0:T(8,128)(2,1)S(1)}, bf16[64,384]{1,0:T(8,128)(2,1)}, u32[]{:S(2)}) copy-start(bf16[64,384]{1,0:T(8,128)(2,1)} %refs_0_.1) | copy-start | bytes 147460
  22.2 4.3 %collective-permute-start.10 = (f16[64,512]{1,0:T(8,128)(2,1)S(1)}, f16[64,512]{1,0:T(8,128)(2,1)S(1)}, u32[]{:S(2)}, u32[]{:S(2)}) collective-permute-start(f16[64,512]{1,0:T(8,128)(2,1)S(1)} %slice_convert_fusion), channel_id=1, source_target_pairs={{0,1},{1,0},{2,3},{3,2},{4,5},{5,4},{6,7},{7,6},{8,9},{9,8},{10,11... | collective-permute-start | bytes 196616 | tf_op jit(solution)/shard_map/ppermute | solution.py:19
  23.9 5.7 %collective-permute-start.15 = (bf16[160,384]{1,0:T(8,128)(2,1)S(1)}, bf16[160,384]{1,0:T(8,128)(2,1)S(1)}, u32[]{:S(2)}, u32[]{:S(2)}) collective-permute-start(bf16[160,384]{1,0:T(8,128)(2,1)S(1)} %collective-permute-done.14.refs_8_), channel_id=1, source_target_pairs={{0,8},{4,12},{8,0},{12,4},{1,9},{5,13},{9,1},{13,5},{2,10},{6,14},... | collective-permute-start | bytes 368648 | tf_op jit(solution)/shard_map/ppermute | solution.py:19
  26.6 4.3 %collective-permute-start.16 = (bf16[320,384]{1,0:T(8,128)(2,1)S(1)}, bf16[320,384]{1,0:T(8,128)(2,1)S(1)}, u32[]{:S(2)}, u32[]{:S(2)}) collective-permute-start(bf16[320,384]{1,0:T(8,128)(2,1)S(1)} %constant_dynamic-update-slice_fusion.2.refs_6_), channel_id=1, source_target_pairs={{0,4},{4,0},{8,12},{12,8},{1,5},{5,1},{9,13},{13,9},{2,6},{6,2},{1... | collective-permute-start | bytes 737288 | tf_op jit(solution)/shard_map/ppermute | solution.py:19
  27.8 3.1 %collective-permute-start.17 = (bf16[320,384]{1,0:T(8,128)(2,1)S(1)}, bf16[320,384]{1,0:T(8,128)(2,1)S(1)}, u32[]{:S(2)}, u32[]{:S(2)}) collective-permute-start(bf16[320,384]{1,0:T(8,128)(2,1)S(1)} %collective-permute-done.13.refs_7_), channel_id=1, source_target_pairs={{0,4},{4,0},{8,12},{12,8},{1,5},{5,1},{9,13},{13,9},{2,6},{6,2},{1... | collective-permute-start | bytes 737288 | tf_op jit(solution)/shard_map/ppermute | solution.py:19
  27.8 2.2 %collective-permute-start.18 = (bf16[160,384]{1,0:T(8,128)(2,1)S(1)}, bf16[160,384]{1,0:T(8,128)(2,1)S(1)}, u32[]{:S(2)}, u32[]{:S(2)}) collective-permute-start(bf16[160,384]{1,0:T(8,128)(2,1)S(1)} %collective-permute-done.14.refs_8_), channel_id=1, source_target_pairs={{0,4},{4,0},{8,12},{12,8},{1,5},{5,1},{9,13},{13,9},{2,6},{6,2},{1... | collective-permute-start | bytes 368648 | tf_op jit(solution)/shard_map/ppermute | solution.py:19
  29.6 1.3 %collective-permute-start.19 = (bf16[160,384]{1,0:T(8,128)(2,1)S(1)}, bf16[160,384]{1,0:T(8,128)(2,1)S(1)}, u32[]{:S(2)}, u32[]{:S(2)}) collective-permute-start(bf16[160,384]{1,0:T(8,128)(2,1)S(1)} %collective-permute-done.15.refs_9_), channel_id=1, source_target_pairs={{0,4},{4,0},{8,12},{12,8},{1,5},{5,1},{9,13},{13,9},{2,6},{6,2},{1... | collective-permute-start | bytes 368648 | tf_op jit(solution)/shard_map/ppermute | solution.py:19
